TPU v7x, 256 devices: a whole 4x4x8 slice. The times are simulated.
256 devices in a mesh: ctx: 64 (over z, x, core), tp: 4 (over y).
Axes of the slice: x: 4, y: 4, z: 8, core: 2. Of those that a mesh axis runs over, the one named last changes fastest.
Arguments:
- queries: bfloat16 [8192, 4096], P('ctx', 'tp'), may hold values from -80 to 80
- keys: bfloat16 [8192, 512], P('ctx', 'tp'), may hold values from -4 to 4
- values: bfloat16 [8192, 512], P('ctx', 'tp'), may hold values from -16 to 16
- segment_ids: int32 [8192], P('ctx'), may hold values from 0 to 15, never falling along the last dimension, each value on 1 to 4224 neighbouring positions
- out_weight: bfloat16 [4096, 4096], P('tp'), may hold values from -0.09375 to 0.09375
Outputs:
- mixed: bfloat16 [8192, 4096], P('ctx', 'tp')
All inputs are finite; a program needn't handle non-finite values.
Results may differ from a plain program's by a relative error of at most 0.015.
Values may be sent and summed in bfloat16 or wider, within the bound.
No kernel may reach another device: no remote copies, remote signals or barrier semaphores. Data moves between devices by JAX's collectives and lax.ppermute only.
A program may use at most 128 MiB of HBM per device.

v0:
```python
import jax
import jax.numpy as jnp
from jax import lax
from jax.sharding import PartitionSpec as P

HEAD_DIM = 128


def fresh_state(kv_count, group, rows):
    return (
        jnp.full((kv_count, group, rows), -1e30, jnp.float32),
        jnp.zeros((kv_count, group, rows), jnp.float32),
        jnp.zeros((kv_count, group, rows, HEAD_DIM), jnp.float32),
    )


def update_state(state, query_group, key_piece, value_piece, key_seg, key_pos):
    query_heads, query_pos, query_seg = query_group
    largest, total, summed = state
    scores = jnp.einsum(
        "rcgd,pcd->cgrp", query_heads, key_piece, preferred_element_type=jnp.float32
    ) * HEAD_DIM ** (-0.5)
    allowed = (key_pos[None, :] <= query_pos[:, None]) & (key_seg[None, :] == query_seg[:, None])
    scores = jnp.where(allowed[None, None], scores, -1e30)
    new_largest = jnp.maximum(largest, jnp.max(scores, axis=-1))
    weight = jnp.exp(scores - new_largest[..., None]) * allowed[None, None]
    total = jnp.sum(weight, axis=-1)
    summed = jnp.einsum(
        "cgrp,pcd->cgrd",
        weight.astype(jnp.bfloat16),
        value_piece,
        preferred_element_type=jnp.float32,
    )
    return (new_largest, total, summed)


def finish_state(state, rows):
    largest, total, summed = state
    result = summed / total[..., None]
    return result.transpose(2, 0, 1, 3).reshape(rows, -1).astype(jnp.bfloat16)


def on_device(queries, keys, values, segment_ids, out_weight):
    tokens = queries.shape[0]
    kv_count = keys.shape[1] // HEAD_DIM
    group = queries.shape[1] // HEAD_DIM // kv_count
    index = lax.axis_index("ctx")
    segments_all = lax.all_gather(segment_ids, "ctx", axis=0, tiled=True)
    first = index * tokens
    query_group = (
        queries.reshape(tokens, kv_count, group, HEAD_DIM),
        first + jnp.arange(tokens, dtype=jnp.int32),
        lax.dynamic_slice_in_dim(segments_all, first, tokens),
    )
    last_pos = query_group[1][-1]
    first_seg = query_group[2][0]

    def absorb(state, key_rows, value_rows, start, usable):
        width = key_rows.shape[0]
        key_piece = key_rows.reshape(width, kv_count, HEAD_DIM)
        value_piece = value_rows.reshape(width, kv_count, HEAD_DIM)
        key_pos = jnp.arange(width, dtype=jnp.int32)
        live = usable & (start <= last_pos) & (segments_all[-1] >= first_seg)
        step_fn = lambda current: update_state(
            current, query_group, key_piece, value_piece, segments_all, key_pos
        )
        return lax.cond(live, step_fn, lambda current: current, state)

    initial = fresh_state(kv_count, group, tokens)
    state = absorb(
        initial,
        lax.all_gather(keys, "ctx", axis=0, tiled=True),
        lax.all_gather(values, "ctx", axis=0, tiled=True),
        jnp.int32(0),
        jnp.bool_(True),
    )
    attention = finish_state(state, tokens)
    partial_out = jnp.dot(attention, out_weight, preferred_element_type=jnp.float32)
    return lax.psum_scatter(partial_out.astype(jnp.bfloat16), "tp", scatter_dimension=1, tiled=True)


def solution(mesh):
    placed = (P("ctx", "tp"), P("ctx", "tp"), P("ctx", "tp"), P("ctx"), P("tp", None))
    return jax.shard_map(
        on_device, mesh=mesh, in_specs=placed, out_specs=P("ctx", "tp"), check_vma=False
    )
```

profile of v0, /device:TPU:1, one launch (start us, length us, event | category | flops | bytes accessed | tf_op | source)
XLA Modules:
  0.0 254.3 jit_solution(5608832425941933367)
XLA Ops:
  6.5 0.0 all-gather.4.cloned.1.call-start
  6.5 0.7 all-gather.4.cloned.1.call-update
  7.3 0.0 all-gather.6.cloned.1.call-start
  7.3 0.7 all-gather.6.cloned.1.call-update
  8.0 0.0 reduce-scatter.2.cloned.1.call-start
  8.1 0.6 slice.9
  8.7 43.9 %all-gather = s32[64,1,128]{2,1,0:T(1,128)S(1)} all-gather(s32[1,1,128]{2,1,0:T(1,128)} %bitcast.61), channel_id=1, replica_groups=mesh['ctx'=64,'tp'=4] {'ctx'}, dimensions={0}, use_global_device_ids=true | all-gather | bytes 33280 | tf_op jit(solution)/shard_map/all_gather | solution.py:48
  52.6 0.6 slice.12
  53.2 0.1 dynamic_slice.3
  54.5 37.1 %all-gather.4.cloned.1.call-done = bf16[8192,128]{1,0:T(8,128)(2,1)} async-done(((bf16[128,128]{1,0:T(8,128)(2,1)}), bf16[8192,128]{1,0:T(8,128)(2,1)}) %all-gather.4.cloned.1.call-update) | async-done | bytes 2097168 | tf_op jit(solution)/shard_map/all_gather | solution.py:72
  91.6 77.7 %all-gather.6.cloned.1.call-done = bf16[8192,128]{1,0:T(8,128)(2,1)} async-done(((bf16[128,128]{1,0:T(8,128)(2,1)}), bf16[8192,128]{1,0:T(8,128)(2,1)}) %all-gather.6.cloned.1.call-update) | async-done | bytes 2097168 | tf_op jit(solution)/shard_map/all_gather | solution.py:73
  169.3 51.2 %conditional.1 = (f32[1,8,128]{2,1,0:T(8,128)S(1)}, f32[1,8,128,128]{2,3,1,0:T(8,128)S(1)}) conditional(s32[]{:T(128)} %bitcast.9, () %tuple.13, (s32[8192]{0:T(1024)S(1)}, s32[128]{0:T(128)S(1)}, s32[8192]{0:T(1024)S(1)}, s32[128]{0:T(128)S(1)}, bf16[128,1024]{1,0:T(8,128)(2,1)}, /*index=5*/bf16[8192,128]{1,0:T(8,128)(2,1)}, ...), branch_computations={%region_0.0_spmd, %region_1.4_spmd} | conditional | flops 4408212480 | bytes 122512400 | solution.py:67
  169.3 4.9 %compare_and_fusion = (pred[128,8192]{0,1:T(8,128)(4,1)S(1)}, f32[128,8192]{0,1:T(8,128)}) fusion(s32[128]{0:T(128)S(1)} %get-tuple-element.25, s32[128]{0:T(128)S(1)} %get-tuple-element.23, s32[8192]{0:T(1024)S(1)} %get-tuple-element.24, s32[8192]{0:T(1024)S(1)} %get-tuple-element.22), kind=kLoop, calls=%fused_computation.8 | loop fusion | flops 4194304 | bytes 5309440 | tf_op jit(solution)/shard_map/cond/branch_1_fun/and | solution.py:23
  174.3 14.5 %fusion = (f32[8,128]{1,0:T(8,128)S(1)}, f32[8192,128,8]{1,0,2:T(8,128)}) fusion(pred[128,8192]{0,1:T(8,128)(4,1)S(1)} %get-tuple-element.36, bf16[8192,128]{1,0:T(8,128)(2,1)} %get-tuple-element.26, bf16[128,1024]{1,0:T(8,128)(2,1)} %get-tuple-element.34), kind=kOutput, calls=%fused_computation.2 | convolution fusion | flops 2172648448 | bytes 36966400 | tf_op jit(solution)/shard_map/cond/branch_1_fun/rcgd,pcd->cgrp/dot_general | solution.py:20
  188.7 16.7 %fusion.10 = f32[1,8,128,128]{2,3,1,0:T(8,128)S(1)} fusion(bf16[8192,128]{1,0:T(8,128)(2,1)} %get-tuple-element.28, f32[8192,128,8]{1,0,2:T(8,128)} %get-tuple-element.39, f32[128,8192]{0,1:T(8,128)} %get-tuple-element.37, f32[8,128]{1,0:T(8,128)S(1)} %broadcast_maximum_fusion, pred[128,8192]{0,1:T(8,128)(4,1)S(1)} %get-tuple-element.36), kind=kOutput, calls=%fused_computation.12 | convolution fusion | flops 2189426688 | bytes 41422848 | tf_op jit(solution)/shard_map/cond/branch_1_fun/cgrp,pcd->cgrd/dot_general | solution.py:28
  205.4 15.1 %fusion.2 = f32[8,128]{1,0:T(8,128)S(1)} fusion(f32[8192,128,8]{1,0,2:T(8,128)} %get-tuple-element.39, f32[128,8192]{0,1:T(8,128)} %get-tuple-element.37, f32[8,128]{1,0:T(8,128)S(1)} %broadcast_maximum_fusion, pred[128,8192]{0,1:T(8,128)(4,1)S(1)} %get-tuple-element.36), kind=kLoop, calls=%fused_computation.4 | loop fusion | flops 41942016 | bytes 38805504 | tf_op jit(solution)/shard_map/cond/branch_1_fun/reduce_sum | solution.py:27
  220.5 0.1 divide_convert_fusion
  220.6 5.6 %convolution_convert_fusion = bf16[128,4096]{1,0:T(8,128)(2,1)} fusion(bf16[128,1024]{0,1:T(8,128)(2,1)S(1)} %bitcast.55, bf16[1024,4096]{1,0:T(8,128)(2,1)} %param.11), kind=kOutput, calls=%fused_computation.19 | convolution fusion | flops 1074266112 | bytes 9699328 | tf_op jit(solution)/shard_map/dot_general | solution.py:78
  226.3 0.0 reduce-scatter.2.cloned.1.call-update
  226.3 21.5 %reduce-scatter.2.cloned.1.call-done = bf16[128,1024]{1,0:T(8,128)(2,1)} async-done(((bf16[128,4096]{1,0:T(8,128)(2,1)}), bf16[128,1024]{1,0:T(8,128)(2,1)}) %reduce-scatter.2.cloned.1.call-update) | async-done | bytes 262160 | tf_op jit(solution)/shard_map/reduce_scatter | solution.py:79
  (3 shorter events, 0.0 us)
Async XLA Ops:
  6.5 85.1 %all-gather.4.cloned.1.call-start = ((), (), s32[]{:S(2)}) async-start(), calls=%async_computation.1 | async-start | bytes 2129920 | tf_op jit(solution)/shard_map/all_gather | solution.py:72
  7.3 162.1 %all-gather.6.cloned.1.call-start = ((), (), s32[]{:S(2)}) async-start(), calls=%async_computation.2 | async-start | bytes 2129920 | tf_op jit(solution)/shard_map/all_gather | solution.py:73
  8.0 239.8 %reduce-scatter.2.cloned.1.call-start = ((), (), s32[]{:S(2)}) async-start(), calls=%async_computation.3 | async-start | bytes 1310720 | tf_op jit(solution)/shard_map/reduce_scatter | solution.py:79
Sparse Core Ops, SparseCore 0:
  10.1 81.4 all-gather.3
  94.4 74.9 all-gather.5
  226.4 21.3 reduce-scatter.1
where the time goes:
time: 256 us; the launch traced here: 254 us
  waiting for transfers between devices  138 us (54%)
  blocking collectives  43.9 us (17%)
  matrix products  36.8 us (14%)
  other arithmetic  20.1 us (8%)
  between operations  14.4 us (6%)
    all_gather x1, waiting for transfers between devices, on_device(): lax.all_gather(values, 'ctx', axis=0, tiled=True)  77.7 us
    all_gather x1, blocking collectives, on_device(): segments_all = lax.all_gather(segment_ids, 'ctx', axis=0, tiled=True)  43.9 us
    all_gather x1, waiting for transfers between devices, on_device(): lax.all_gather(keys, 'ctx', axis=0, tiled=True)  37.1 us
    reduce_scatter x1, waiting for transfers between devices, on_device(): lax.psum_scatter(partial_out.astype(jnp.bfloat16), 'tp', scatter_dimensio...  21.5 us
    dot_general x1, matrix products, update_state(): jnp.einsum('cgrp,pcd->cgrd', weight.astype(jnp.bfloat16), value_piece, pr...  16.7 us
    reduce_sum x1, other arithmetic, update_state(): total = jnp.sum(weight, axis=-1)  15.1 us
    dot_general x1, matrix products, update_state(): jnp.einsum('rcgd,pcd->cgrp', query_heads, key_piece, preferred_element_ty...  14.5 us
    dot_general x1, matrix products, on_device(): jnp.dot(attention, out_weight, preferred_element_type=jnp.float32)  5.64 us
  transfers between devices with their start and end apart: 3, of which 3 were waited for; matrix products, arithmetic and copies ran while one was open for 0% of the time, Pallas kernels for 0%

commit v1 on v0

v1 whole, which is shorter than its diff:
```python
import functools

import jax
import jax.numpy as jnp
from jax import lax
from jax.experimental import pallas as pl
from jax.experimental.pallas import tpu as pltpu
from jax.sharding import PartitionSpec as P

HEAD_DIM = 128
ROWS = 272
LOG2E = 1.4426950408889634
NEG = -1e30


def ctx_pairs(size, target):
    pairs = [(i, target(i)) for i in range(size)]
    return [(i, k) for i, k in pairs if k is not None and 0 <= k < size]


def shift_z(size, planes):
    return ctx_pairs(size, lambda i: i + 8 * planes)


def shift_x(size, steps):
    return ctx_pairs(size, lambda i: i // 8 * 8 + (i + 2 * steps) % 8)


def swap_core(size):
    return ctx_pairs(size, lambda i: i ^ 1)


def heads_of(q_ref):
    tokens, width = q_ref.shape
    return jnp.concatenate(
        [q_ref[:, h * HEAD_DIM : (h + 1) * HEAD_DIM] for h in range(width // HEAD_DIM)], 0
    )


def column(row):
    return jnp.transpose(jnp.broadcast_to(row, (128, 128)))


def absorb(q, state, keys, values, allowed, scale):
    m, acc = state
    n = keys.shape[0]
    s = lax.dot_general(q, keys, (((1,), (1,)), ((), ())), preferred_element_type=jnp.float32)
    s = jnp.where(allowed[None], s.reshape(-1, 128, n), NEG).reshape(-1, n)
    top = jnp.max(s, axis=1, keepdims=True)
    new_m = top if m is None else jnp.maximum(m, top)
    weight = jnp.exp2((s - new_m) * scale).astype(jnp.bfloat16)
    extended = jnp.concatenate([values, jnp.ones_like(values)], 1)
    part = jnp.dot(weight, extended, preferred_element_type=jnp.float32)
    if m is not None:
        part = acc * jnp.exp2((m - new_m) * scale) + part
    return new_m, part


def own_kernel(scale, q_ref, own_ref, m_ref, acc_ref):
    q = heads_of(q_ref)
    seg = own_ref[256:272, :].astype(jnp.float32)[0:1]
    later = lax.broadcasted_iota(jnp.int32, (128, 128), 1) > lax.broadcasted_iota(
        jnp.int32, (128, 128), 0
    )
    allowed = (column(seg) == seg) & ~later
    m, acc = absorb(
        q, (None, None), own_ref[0:128, :], own_ref[128:256, :], allowed, scale
    )
    m_ref[...] = jnp.broadcast_to(m, m_ref.shape)
    acc_ref[...] = acc


def group_kernel(scale, last, usable_ref, q_ref, own_ref, near_ref, far_ref, m_in, acc_in, *rest):
    if last:
        out_ref, m_ref, acc_ref = rest
    else:
        m_ref, acc_ref = rest
    _, n, _, _ = near_ref.shape
    m_ref[...] = m_in[...]
    acc_ref[...] = acc_in[...]
    q = heads_of(q_ref)
    own_seg = column(own_ref[256:272, :].astype(jnp.float32)[0:1])

    def step(x, carry):
        flags = [usable_ref[(side * 4 + x) * n + k] for k in range(n) for side in range(2)]
        some = functools.reduce(jnp.maximum, flags)

        @pl.when(some > 0)
        def _():
            blocks = [ref[x, k] for k in range(n) for ref in (near_ref, far_ref)]
            keys = jnp.concatenate([b[0:128] for b in blocks], 0)
            values = jnp.concatenate([b[128:256] for b in blocks], 0)
            allowed = jnp.concatenate(
                [
                    own_seg == jnp.where(flag > 0, b[256:272].astype(jnp.float32)[0:1], -1.0)
                    for b, flag in zip(blocks, flags)
                ],
                1,
            )
            m, acc = absorb(
                q, (m_ref[:, 0:1], acc_ref[...]), keys, values, allowed, scale
            )
            m_ref[...] = jnp.broadcast_to(m, m_ref.shape)
            acc_ref[...] = acc

        return carry

    lax.fori_loop(0, 4, step, 0)
    if last:
        for h in range(q_ref.shape[1] // HEAD_DIM):
            rows = slice(h * 128, (h + 1) * 128)
            out_ref[:, h * HEAD_DIM : (h + 1) * HEAD_DIM] = (
                acc_ref[rows, 0:128] / acc_ref[rows, 128:256]
            ).astype(out_ref.dtype)


VMEM = pl.BlockSpec(memory_space=pltpu.VMEM)
SMEM = pl.BlockSpec(memory_space=pltpu.SMEM)
PARAMS = pltpu.CompilerParams(vmem_limit_bytes=40 * 1024 * 1024)


def on_device(size, queries, keys, values, segment_ids, out_weight):
    tokens = queries.shape[0]
    rows = tokens * (queries.shape[1] // HEAD_DIM)
    scale = HEAD_DIM ** (-0.5) * LOG2E
    index = lax.axis_index("ctx")
    lane = lax.axis_index("tp")
    z, x, c = index // 8, index % 8 // 2, index % 2
    seg = (segment_ids + 1).astype(jnp.bfloat16)
    own = jnp.concatenate([keys, values, jnp.broadcast_to(seg[None], (16, tokens))], 0)

    def send(value, pairs):
        return lax.ppermute(value, "ctx", pairs)

    own1 = own[None]
    planes = [own1] + [send(own1, shift_z(size, k)) for k in (1, 2, 3, 4)]
    beyond = send(own, [(8 * k - 33, 8 * k) for k in range(5, size // 8)])

    def spread(part):
        sides = [send(part, shift_x(size, k)) for k in (2, 1, 3)]
        near = jnp.stack([part, *sides])
        return near, send(near, swap_core(size))

    def usable(plane_numbers):
        cells = []
        for side in range(2):
            for back in (0, 2, 1, 3):
                for k in plane_numbers:
                    g = 8 * (z - k) + 2 * ((x - back) % 4) + (c + side) % 2
                    cells.append((g >= 0) & (g < index))
        return jnp.stack(cells).astype(jnp.int32)

    state_shape = (
        jax.ShapeDtypeStruct((rows, 128), jnp.float32),
        jax.ShapeDtypeStruct((rows, 256), jnp.float32),
    )
    m, acc = pl.pallas_call(
        functools.partial(own_kernel, scale),
        out_shape=state_shape,
        in_specs=[VMEM] * 2,
        out_specs=(VMEM, VMEM),
        compiler_params=PARAMS,
        name="own",
    )(queries, own)

    group_a = spread(jnp.concatenate(planes[0:3], 0))
    group_b = spread(jnp.concatenate(planes[3:5], 0))

    m, acc = pl.pallas_call(
        functools.partial(group_kernel, scale, False),
        out_shape=state_shape,
        in_specs=[SMEM] + [VMEM] * 6,
        out_specs=(VMEM, VMEM),
        compiler_params=PARAMS,
        name="near",
    )(usable((0, 1, 2)), queries, own, *group_a, m, acc)

    beyond4 = jnp.concatenate([beyond[None, None], jnp.zeros((3, 1) + beyond.shape, beyond.dtype)])
    flag = jnp.zeros((8,), jnp.int32).at[0].set(((index % 8 == 0) & (z >= 5)).astype(jnp.int32))
    m, acc = pl.pallas_call(
        functools.partial(group_kernel, scale, False),
        out_shape=state_shape,
        in_specs=[SMEM] + [VMEM] * 6,
        out_specs=(VMEM, VMEM),
        compiler_params=PARAMS,
        name="beyond",
    )(flag, queries, own, beyond4, beyond4, m, acc)

    attention = pl.pallas_call(
        functools.partial(group_kernel, scale, True),
        out_shape=jax.ShapeDtypeStruct((tokens, queries.shape[1]), jnp.bfloat16),
        in_specs=[SMEM] + [VMEM] * 6,
        out_specs=VMEM,
        scratch_shapes=[pltpu.VMEM(s.shape, s.dtype) for s in state_shape],
        compiler_params=PARAMS,
        name="last",
    )(usable((3, 4)), queries, own, *group_b, m, acc)

    width = out_weight.shape[1] // 4
    partial_out = jnp.dot(attention, out_weight, preferred_element_type=jnp.float32)

    def share(k):
        return lax.dynamic_slice_in_dim(partial_out, (lane ^ k) * width, width, 1)

    total = share(0)
    for k in (2, 1, 3):
        got = lax.ppermute(share(k).astype(jnp.bfloat16), "tp", [(i, i ^ k) for i in range(4)])
        total = total + got.astype(jnp.float32)
    return total.astype(jnp.bfloat16)


def solution(mesh):
    placed = (P("ctx", "tp"), P("ctx", "tp"), P("ctx", "tp"), P("ctx"), P("tp", None))
    return jax.shard_map(
        functools.partial(on_device, mesh.shape["ctx"]),
        mesh=mesh,
        in_specs=placed,
        out_specs=P("ctx", "tp"),
        check_vma=False,
    )
```

time: 256 us -> 94.6 us (0.37)
  the two profiles are of different devices: /device:TPU:1 before, /device:TPU:160 now
where the time goes in v1:
time: 94.6 us; the launch traced here: 94.2 us
  waiting for transfers between devices  35.5 us (38%)
  Pallas kernels  25.9 us (27%)
  starting transfers between devices  23.2 us (25%)
  local copies, waits for them, and re-layouts  4.17 us (4%)
  other arithmetic  3.48 us (4%)
  matrix products  1.27 us (1%)
    ppermute x13, waiting for transfers between devices, send(): return lax.ppermute(value, 'ctx', pairs)  28.2 us
    ppermute x13, starting transfers between devices, send(): return lax.ppermute(value, 'ctx', pairs)  18.8 us
    pallas_call x2, Pallas kernels, on_device(): pl.pallas_call(functools.partial(group_kernel, scale, False), out_shape=s...  15.5 us
    pallas_call x1, Pallas kernels, on_device(): pl.pallas_call(functools.partial(group_kernel, scale, True), out_shape=ja...  9.84 us
    ppermute x3, waiting for transfers between devices, on_device(): lax.ppermute(share(k).astype(jnp.bfloat16), 'tp', [(i, i ^ k) for i in ra...  7.31 us
    ppermute x3, starting transfers between devices, on_device(): lax.ppermute(share(k).astype(jnp.bfloat16), 'tp', [(i, i ^ k) for i in ra...  4.34 us
    unnamed x11, local copies, waits for them, and re-layouts  3.76 us
  transfers between devices with their start and end apart: 16, of which 10 were waited for; matrix products, arithmetic and copies ran while one was open for 1% of the time, Pallas kernels for 17%

profile of v1, /device:TPU:160, one launch (start us, length us, event | category | flops | bytes accessed | tf_op | source)
XLA Modules:
  0.0 94.2 jit_solution(8785456018560490869)
XLA Ops:
  0.0 0.7 add_convert_fusion.1
  0.7 0.8 fusion
  1.5 2.9 %collective-permute-start.7 = (bf16[1,272,128]{2,1,0:T(8,128)(2,1)S(1)}, bf16[1,272,128]{2,1,0:T(8,128)(2,1)S(1)}, u32[]{:S(2)}, u32[]{:S(2)}) collective-permute-start(bf16[1,272,128]{2,1,0:T(8,128)(2,1)S(1)} %get-tuple-element.34), channel_id=1, source_target_pairs={{0,32},{4,36},{8,40},{12,44},{16,48},{20,52},{24,56},{28,60},{32,6... | collective-permute-start | bytes 208904 | tf_op jit(solution)/shard_map/ppermute | solution.py:133
  4.4 1.9 %collective-permute-start.8 = (bf16[1,272,128]{2,1,0:T(8,128)(2,1)S(1)}, bf16[1,272,128]{2,1,0:T(8,128)(2,1)S(1)}, u32[]{:S(2)}, u32[]{:S(2)}) collective-permute-start(bf16[1,272,128]{2,1,0:T(8,128)(2,1)S(1)} %get-tuple-element.34), channel_id=1, source_target_pairs={{0,64},{4,68},{8,72},{12,76},{16,80},{20,84},{24,88},{28,92},{32,9... | collective-permute-start | bytes 208904 | tf_op jit(solution)/shard_map/ppermute | solution.py:133
  6.3 1.3 %collective-permute-done.7 = bf16[1,272,128]{2,1,0:T(8,128)(2,1)S(1)} collective-permute-done((bf16[1,272,128]{2,1,0:T(8,128)(2,1)S(1)}, bf16[1,272,128]{2,1,0:T(8,128)(2,1)S(1)}, u32[]{:S(2)}, u32[]{:S(2)}) %collective-permute-start.7) | collective-permute-done | bytes 69664 | tf_op jit(solution)/shard_map/ppermute | solution.py:133
  7.7 5.3 %collective-permute-done.8 = bf16[1,272,128]{2,1,0:T(8,128)(2,1)S(1)} collective-permute-done((bf16[1,272,128]{2,1,0:T(8,128)(2,1)S(1)}, bf16[1,272,128]{2,1,0:T(8,128)(2,1)S(1)}, u32[]{:S(2)}, u32[]{:S(2)}) %collective-permute-start.8) | collective-permute-done | bytes 69664 | tf_op jit(solution)/shard_map/ppermute | solution.py:133
  13.0 3.1 %collective-permute-start.9 = (bf16[3,272,128]{2,1,0:T(8,128)(2,1)S(1)}, bf16[3,272,128]{2,1,0:T(8,128)(2,1)S(1)}, u32[]{:S(2)}, u32[]{:S(2)}) collective-permute-start(bf16[3,272,128]{2,1,0:T(8,128)(2,1)S(1)} %get-tuple-element.33), channel_id=1, source_target_pairs={{0,16},{4,20},{8,24},{12,28},{16,0},{20,4},{24,8},{28,12},{32,48},... | collective-permute-start | bytes 626696 | tf_op jit(solution)/shard_map/ppermute | solution.py:133
  16.1 0.6 collective-permute-start.10
  16.7 2.6 %collective-permute-start.11 = (bf16[3,272,128]{2,1,0:T(8,128)(2,1)S(1)}, bf16[3,272,128]{2,1,0:T(8,128)(2,1)S(1)}, u32[]{:S(2)}, u32[]{:S(2)}) collective-permute-start(bf16[3,272,128]{2,1,0:T(8,128)(2,1)S(1)} %get-tuple-element.33), channel_id=1, source_target_pairs={{0,24},{4,28},{8,0},{12,4},{16,8},{20,12},{24,16},{28,20},{32,56},... | collective-permute-start | bytes 626696 | tf_op jit(solution)/shard_map/ppermute | solution.py:133
  19.3 1.3 %collective-permute-start = (bf16[1,272,128]{2,1,0:T(8,128)(2,1)S(1)}, bf16[1,272,128]{2,1,0:T(8,128)(2,1)S(1)}, u32[]{:S(2)}, u32[]{:S(2)}) collective-permute-start(bf16[1,272,128]{2,1,0:T(8,128)(2,1)S(1)} %get-tuple-element.34), channel_id=1, source_target_pairs={{0,96},{4,100},{8,104},{12,108},{16,112},{20,116},{24,120},{28,124... | collective-permute-start | bytes 208904 | tf_op jit(solution)/shard_map/ppermute | solution.py:133
  20.6 1.3 %collective-permute-start.1 = (bf16[1,272,128]{2,1,0:T(8,128)(2,1)S(1)}, bf16[1,272,128]{2,1,0:T(8,128)(2,1)S(1)}, u32[]{:S(2)}, u32[]{:S(2)}) collective-permute-start(bf16[1,272,128]{2,1,0:T(8,128)(2,1)S(1)} %get-tuple-element.34), channel_id=1, source_target_pairs={{0,128},{4,132},{8,136},{12,140},{16,144},{20,148},{24,152},{28,15... | collective-permute-start | bytes 208904 | tf_op jit(solution)/shard_map/ppermute | solution.py:133
  21.9 8.4 %collective-permute-done = bf16[1,272,128]{2,1,0:T(8,128)(2,1)S(1)} collective-permute-done((bf16[1,272,128]{2,1,0:T(8,128)(2,1)S(1)}, bf16[1,272,128]{2,1,0:T(8,128)(2,1)S(1)}, u32[]{:S(2)}, u32[]{:S(2)}) %collective-permute-start) | collective-permute-done | bytes 69664 | tf_op jit(solution)/shard_map/ppermute | solution.py:133
  31.2 0.8 collective-permute-start.3
  32.0 2.5 %collective-permute-start.4 = (bf16[2,272,128]{2,1,0:T(8,128)(2,1)S(1)}, bf16[2,272,128]{2,1,0:T(8,128)(2,1)S(1)}, u32[]{:S(2)}, u32[]{:S(2)}) collective-permute-start(bf16[2,272,128]{2,1,0:T(8,128)(2,1)S(1)} %constant_dynamic-update-slice_fusion), channel_id=1, source_target_pairs={{0,24},{4,28},{8,0},{12,4},{16,8},{20,12},{24,16},{28,20},{32,56},... | collective-permute-start | bytes 417800 | tf_op jit(solution)/shard_map/ppermute | solution.py:133
  34.5 4.8 %collective-permute-done.2 = bf16[2,272,128]{2,1,0:T(8,128)(2,1)S(1)} collective-permute-done((bf16[2,272,128]{2,1,0:T(8,128)(2,1)S(1)}, bf16[2,272,128]{2,1,0:T(8,128)(2,1)S(1)}, u32[]{:S(2)}, u32[]{:S(2)}) %collective-permute-start.2) | collective-permute-done | bytes 139296 | tf_op jit(solution)/shard_map/ppermute | solution.py:133
  39.2 1.8 %collective-permute-done.3 = bf16[2,272,128]{2,1,0:T(8,128)(2,1)S(1)} collective-permute-done((bf16[2,272,128]{2,1,0:T(8,128)(2,1)S(1)}, bf16[2,272,128]{2,1,0:T(8,128)(2,1)S(1)}, u32[]{:S(2)}, u32[]{:S(2)}) %collective-permute-start.3) | collective-permute-done | bytes 139296 | tf_op jit(solution)/shard_map/ppermute | solution.py:133
  41.2 1.5 %collective-permute-start.6 = (bf16[272,128]{1,0:T(8,128)(2,1)S(1)}, bf16[272,128]{1,0:T(8,128)(2,1)S(1)}, u32[]{:S(2)}, u32[]{:S(2)}) collective-permute-start(bf16[272,128]{1,0:T(8,128)(2,1)S(1)} %get-tuple-element.35.own_ref), channel_id=1, source_target_pairs={{28,160},{60,192},{92,224},{29,161},{61,193},{93,225},{30,162},{62... | collective-permute-start | bytes 208904 | tf_op jit(solution)/shard_map/ppermute | solution.py:133
  43.3 0.9 %copy-done = bf16[128,1024]{1,0:T(8,128)(2,1)S(1)} copy-done((bf16[128,1024]{1,0:T(8,128)(2,1)S(1)}, bf16[128,1024]{1,0:T(8,128)(2,1)}, u32[]{:S(2)}) %copy-start) | copy-done | bytes 262168
  44.2 0.6 own.1
  44.8 0.8 copy-done.2
  45.8 6.2 %collective-permute-done.6 = bf16[272,128]{1,0:T(8,128)(2,1)S(1)} collective-permute-done((bf16[272,128]{1,0:T(8,128)(2,1)S(1)}, bf16[272,128]{1,0:T(8,128)(2,1)S(1)}, u32[]{:S(2)}, u32[]{:S(2)}) %collective-permute-start.6) | collective-permute-done | bytes 69664 | tf_op jit(solution)/shard_map/ppermute | solution.py:133
  52.0 0.9 copy-done.1
  53.0 1.0 %copy-done.3 = f32[1024,128]{1,0:T(8,128)S(1)} copy-done((f32[1024,128]{1,0:T(8,128)S(1)}, f32[1024,128]{1,0:T(8,128)}, u32[]{:S(2)}) %copy-start.3) | copy-done | bytes 524312
  54.0 12.8 %near.1 = (f32[1024,128]{1,0:T(8,128)S(1)}, f32[1024,256]{1,0:T(8,128)S(1)}) custom-call(s32[24]{0:T(128)S(1)} %convert_element_type.33.usable_ref, bf16[128,1024]{1,0:T(8,128)(2,1)S(1)} %copy-done.1, bf16[272,128]{1,0:T(8,128)(2,1)S(1)} %get-tuple-element.35.own_ref, bf16[4,3,272,128]{3,2,1,0:T(8,128)(2,1)S(1)} %pad_maximum_fusion.near_ref, ...), custom_call_target="tpu_custom_call" | custom-call | tf_op jit(solution)/shard_map/near/pallas_call | solution.py:169
  66.8 2.7 %beyond.1 = (f32[1024,128]{1,0:T(8,128)S(1)}, f32[1024,256]{1,0:T(8,128)S(1)}) custom-call(s32[8]{0:T(128)S(1)} %pad_convert_fusion.usable_ref, bf16[128,1024]{1,0:T(8,128)(2,1)S(1)} %copy-done.1, bf16[272,128]{1,0:T(8,128)(2,1)S(1)} %get-tuple-element.35.own_ref, bf16[4,1,272,128]{3,2,1,0:T(8,128)(2,1)S(1)} %concatenate.16.near_ref.far_ref, ...), custom_call_target="tpu_custom_call" | custom-call | tf_op jit(solution)/shard_map/beyond/pallas_call | solution.py:180
  69.5 9.8 %last.1 = bf16[128,1024]{1,0:T(8,128)(2,1)S(1)} custom-call(s32[16]{0:T(128)S(1)} %convert_element_type.31.usable_ref, bf16[128,1024]{1,0:T(8,128)(2,1)S(1)} %copy-done.1, bf16[272,128]{1,0:T(8,128)(2,1)S(1)} %get-tuple-element.35.own_ref, bf16[4,2,272,128]{3,2,1,0:T(8,128)(2,1)S(1)} %pad_maximum_fusion.1.near_ref, ...), custom_call_target="tpu_custom_call" | custom-call | tf_op jit(solution)/shard_map/last/pallas_call | solution.py:189
  79.3 1.3 %fusion.2 = f32[128,4096]{1,0:T(8,128)S(1)} fusion(bf16[128,1024]{1,0:T(8,128)(2,1)S(1)} %last.1, bf16[1024,4096]{1,0:T(8,128)(2,1)S(1)} %copy-done.4), kind=kOutput, calls=%fused_computation.14 | convolution fusion | flops 1073741824 | bytes 10747904 | tf_op jit(solution)/shard_map/dot_general | solution.py:200
  80.7 3.3 %collective-permute-start.13 = (bf16[128,1024]{1,0:T(8,128)(2,1)S(1)}, bf16[128,1024]{1,0:T(8,128)(2,1)S(1)}, u32[]{:S(2)}, u32[]{:S(2)}) collective-permute-start(bf16[128,1024]{1,0:T(8,128)(2,1)S(1)} %get-tuple-element.29), channel_id=1, source_target_pairs={{0,2},{1,3},{2,0},{3,1},{4,6},{5,7},{6,4},{7,5},{8,10},{9,11},{10,... | collective-permute-start | bytes 786440 | tf_op jit(solution)/shard_map/ppermute | solution.py:207
  84.0 0.7 collective-permute-start.14
  85.1 3.6 %collective-permute-done.13 = bf16[128,1024]{1,0:T(8,128)(2,1)S(1)} collective-permute-done((bf16[128,1024]{1,0:T(8,128)(2,1)S(1)}, bf16[128,1024]{1,0:T(8,128)(2,1)S(1)}, u32[]{:S(2)}, u32[]{:S(2)}) %collective-permute-start.13) | collective-permute-done | bytes 262176 | tf_op jit(solution)/shard_map/ppermute | solution.py:207
  88.7 3.2 %collective-permute-done.14 = bf16[128,1024]{1,0:T(8,128)(2,1)S(1)} collective-permute-done((bf16[128,1024]{1,0:T(8,128)(2,1)S(1)}, bf16[128,1024]{1,0:T(8,128)(2,1)S(1)}, u32[]{:S(2)}, u32[]{:S(2)}) %collective-permute-start.14) | collective-permute-done | bytes 262176 | tf_op jit(solution)/shard_map/ppermute | solution.py:207
  92.4 1.8 %add_convert_fusion = bf16[128,1024]{1,0:T(8,128)(2,1)} fusion(bf16[128,1024]{1,0:T(8,128)(2,1)} %collective-permute-done.15, bf16[128,1024]{1,0:T(8,128)(2,1)S(1)} %collective-permute-done.14, bf16[128,1024]{1,0:T(8,128)(2,1)S(1)} %collective-permute-done.13, f32[128,4096]{1,0:T(8,128)S(1)} %fusion.2, s32[]{:T(128)S(6)} %select_n.214), kind=kLoop, calls=%fused_computation.2 | loop fusion | flops 917504 | bytes 1572868 | tf_op jit(solution)/shard_map/convert_element_type | solution.py:209
  (31 shorter events, 2.3 us)
Async XLA Ops:
  1.5 6.2 %collective-permute-start.7 = (bf16[1,272,128]{2,1,0:T(8,128)(2,1)S(1)}, bf16[1,272,128]{2,1,0:T(8,128)(2,1)S(1)}, u32[]{:S(2)}, u32[]{:S(2)}) collective-permute-start(bf16[1,272,128]{2,1,0:T(8,128)(2,1)S(1)} %get-tuple-element.34), channel_id=1, source_target_pairs={{0,32},{4,36},{8,40},{12,44},{16,48},{20,52},{24,56},{28,60},{32,6... | collective-permute-start | bytes 208904 | tf_op jit(solution)/shard_map/ppermute | solution.py:133
  4.4 8.6 %collective-permute-start.8 = (bf16[1,272,128]{2,1,0:T(8,128)(2,1)S(1)}, bf16[1,272,128]{2,1,0:T(8,128)(2,1)S(1)}, u32[]{:S(2)}, u32[]{:S(2)}) collective-permute-start(bf16[1,272,128]{2,1,0:T(8,128)(2,1)S(1)} %get-tuple-element.34), channel_id=1, source_target_pairs={{0,64},{4,68},{8,72},{12,76},{16,80},{20,84},{24,88},{28,92},{32,9... | collective-permute-start | bytes 208904 | tf_op jit(solution)/shard_map/ppermute | solution.py:133
  13.0 17.3 %collective-permute-start.9 = (bf16[3,272,128]{2,1,0:T(8,128)(2,1)S(1)}, bf16[3,272,128]{2,1,0:T(8,128)(2,1)S(1)}, u32[]{:S(2)}, u32[]{:S(2)}) collective-permute-start(bf16[3,272,128]{2,1,0:T(8,128)(2,1)S(1)} %get-tuple-element.33), channel_id=1, source_target_pairs={{0,16},{4,20},{8,24},{12,28},{16,0},{20,4},{24,8},{28,12},{32,48},... | collective-permute-start | bytes 626696 | tf_op jit(solution)/shard_map/ppermute | solution.py:133
  16.1 14.2 %collective-permute-start.10 = (bf16[3,272,128]{2,1,0:T(8,128)(2,1)S(1)}, bf16[3,272,128]{2,1,0:T(8,128)(2,1)S(1)}, u32[]{:S(2)}, u32[]{:S(2)}) collective-permute-start(bf16[3,272,128]{2,1,0:T(8,128)(2,1)S(1)} %get-tuple-element.33), channel_id=1, source_target_pairs={{0,8},{4,12},{8,16},{12,20},{16,24},{20,28},{24,0},{28,4},{32,40},... | collective-permute-start | bytes 626696 | tf_op jit(solution)/shard_map/ppermute | solution.py:133
  16.7 13.6 %collective-permute-start.11 = (bf16[3,272,128]{2,1,0:T(8,128)(2,1)S(1)}, bf16[3,272,128]{2,1,0:T(8,128)(2,1)S(1)}, u32[]{:S(2)}, u32[]{:S(2)}) collective-permute-start(bf16[3,272,128]{2,1,0:T(8,128)(2,1)S(1)} %get-tuple-element.33), channel_id=1, source_target_pairs={{0,24},{4,28},{8,0},{12,4},{16,8},{20,12},{24,16},{28,20},{32,56},... | collective-permute-start | bytes 626696 | tf_op jit(solution)/shard_map/ppermute | solution.py:133
  19.3 11.0 %collective-permute-start = (bf16[1,272,128]{2,1,0:T(8,128)(2,1)S(1)}, bf16[1,272,128]{2,1,0:T(8,128)(2,1)S(1)}, u32[]{:S(2)}, u32[]{:S(2)}) collective-permute-start(bf16[1,272,128]{2,1,0:T(8,128)(2,1)S(1)} %get-tuple-element.34), channel_id=1, source_target_pairs={{0,96},{4,100},{8,104},{12,108},{16,112},{20,116},{24,120},{28,124... | collective-permute-start | bytes 208904 | tf_op jit(solution)/shard_map/ppermute | solution.py:133
  20.6 10.4 %collective-permute-start.1 = (bf16[1,272,128]{2,1,0:T(8,128)(2,1)S(1)}, bf16[1,272,128]{2,1,0:T(8,128)(2,1)S(1)}, u32[]{:S(2)}, u32[]{:S(2)}) collective-permute-start(bf16[1,272,128]{2,1,0:T(8,128)(2,1)S(1)} %get-tuple-element.34), channel_id=1, source_target_pairs={{0,128},{4,132},{8,136},{12,140},{16,144},{20,148},{24,152},{28,15... | collective-permute-start | bytes 208904 | tf_op jit(solution)/shard_map/ppermute | solution.py:133
  30.5 21.5 %collective-permute-start.12 = (bf16[4,3,272,128]{3,2,1,0:T(8,128)(2,1)S(1)}, bf16[4,3,272,128]{3,2,1,0:T(8,128)(2,1)S(1)}, u32[]{:S(2)}, u32[]{:S(2)}) collective-permute-start(bf16[4,3,272,128]{3,2,1,0:T(8,128)(2,1)S(1)} %pad_maximum_fusion.near_ref), channel_id=1, source_target_pairs={{0,4},{4,0},{8,12},{12,8},{16,20},{20,16},{24,28},{28,24},{32,36},... | collective-permute-start | bytes 2506760 | tf_op jit(solution)/shard_map/ppermute | solution.py:133
  31.1 8.2 %collective-permute-start.2 = (bf16[2,272,128]{2,1,0:T(8,128)(2,1)S(1)}, bf16[2,272,128]{2,1,0:T(8,128)(2,1)S(1)}, u32[]{:S(2)}, u32[]{:S(2)}) collective-permute-start(bf16[2,272,128]{2,1,0:T(8,128)(2,1)S(1)} %constant_dynamic-update-slice_fusion), channel_id=1, source_target_pairs={{0,16},{4,20},{8,24},{12,28},{16,0},{20,4},{24,8},{28,12},{32,48},... | collective-permute-start | bytes 417800 | tf_op jit(solution)/shard_map/ppermute | solution.py:133
  31.2 9.9 %collective-permute-start.3 = (bf16[2,272,128]{2,1,0:T(8,128)(2,1)S(1)}, bf16[2,272,128]{2,1,0:T(8,128)(2,1)S(1)}, u32[]{:S(2)}, u32[]{:S(2)}) collective-permute-start(bf16[2,272,128]{2,1,0:T(8,128)(2,1)S(1)} %constant_dynamic-update-slice_fusion), channel_id=1, source_target_pairs={{0,8},{4,12},{8,16},{12,20},{16,24},{20,28},{24,0},{28,4},{32,40},... | collective-permute-start | bytes 417800 | tf_op jit(solution)/shard_map/ppermute | solution.py:133
  32.0 9.0 %collective-permute-start.4 = (bf16[2,272,128]{2,1,0:T(8,128)(2,1)S(1)}, bf16[2,272,128]{2,1,0:T(8,128)(2,1)S(1)}, u32[]{:S(2)}, u32[]{:S(2)}) collective-permute-start(bf16[2,272,128]{2,1,0:T(8,128)(2,1)S(1)} %constant_dynamic-update-slice_fusion), channel_id=1, source_target_pairs={{0,24},{4,28},{8,0},{12,4},{16,8},{20,12},{24,16},{28,20},{32,56},... | collective-permute-start | bytes 417800 | tf_op jit(solution)/shard_map/ppermute | solution.py:133
  41.1 28.4 %collective-permute-start.5 = (bf16[4,2,272,128]{3,2,1,0:T(8,128)(2,1)S(1)}, bf16[4,2,272,128]{3,2,1,0:T(8,128)(2,1)}, u32[]{:S(2)}, u32[]{:S(2)}) collective-permute-start(bf16[4,2,272,128]{3,2,1,0:T(8,128)(2,1)S(1)} %pad_maximum_fusion.1.near_ref), channel_id=1, source_target_pairs={{0,4},{4,0},{8,12},{12,8},{16,20},{20,16},{24,28},{28,24},{32,36},... | collective-permute-start | bytes 1671176 | tf_op jit(solution)/shard_map/ppermute | solution.py:133
  41.2 10.7 %collective-permute-start.6 = (bf16[272,128]{1,0:T(8,128)(2,1)S(1)}, bf16[272,128]{1,0:T(8,128)(2,1)S(1)}, u32[]{:S(2)}, u32[]{:S(2)}) collective-permute-start(bf16[272,128]{1,0:T(8,128)(2,1)S(1)} %get-tuple-element.35.own_ref), channel_id=1, source_target_pairs={{28,160},{60,192},{92,224},{29,161},{61,193},{93,225},{30,162},{62... | collective-permute-start | bytes 208904 | tf_op jit(solution)/shard_map/ppermute | solution.py:133
  43.3 1.0 %copy-start = (bf16[128,1024]{1,0:T(8,128)(2,1)S(1)}, bf16[128,1024]{1,0:T(8,128)(2,1)}, u32[]{:S(2)}) copy-start(bf16[128,1024]{1,0:T(8,128)(2,1)} %q_ref.7) | copy-start | bytes 786436
  44.8 0.8 copy-start.2
  52.0 1.0 %copy-start.1 = (bf16[128,1024]{1,0:T(8,128)(2,1)S(1)}, bf16[128,1024]{1,0:T(8,128)(2,1)}, u32[]{:S(2)}) copy-start(bf16[128,1024]{1,0:T(8,128)(2,1)} %q_ref.7) | copy-start | bytes 786436
  53.0 1.0 %copy-start.3 = (f32[1024,128]{1,0:T(8,128)S(1)}, f32[1024,128]{1,0:T(8,128)}, u32[]{:S(2)}) copy-start(f32[1024,128]{1,0:T(8,128)} %copy-done.2) | copy-start | bytes 1572868
  54.0 25.3 %copy-start.4 = (bf16[1024,4096]{1,0:T(8,128)(2,1)S(1)}, bf16[1024,4096]{1,0:T(8,128)(2,1)}, u32[]{:S(2)}) copy-start(bf16[1024,4096]{1,0:T(8,128)(2,1)} %param.11) | copy-start | bytes 25165828
  80.7 8.0 %collective-permute-start.13 = (bf16[128,1024]{1,0:T(8,128)(2,1)S(1)}, bf16[128,1024]{1,0:T(8,128)(2,1)S(1)}, u32[]{:S(2)}, u32[]{:S(2)}) collective-permute-start(bf16[128,1024]{1,0:T(8,128)(2,1)S(1)} %get-tuple-element.29), channel_id=1, source_target_pairs={{0,2},{1,3},{2,0},{3,1},{4,6},{5,7},{6,4},{7,5},{8,10},{9,11},{10,... | collective-permute-start | bytes 786440 | tf_op jit(solution)/shard_map/ppermute | solution.py:207
  84.0 7.9 %collective-permute-start.14 = (bf16[128,1024]{1,0:T(8,128)(2,1)S(1)}, bf16[128,1024]{1,0:T(8,128)(2,1)S(1)}, u32[]{:S(2)}, u32[]{:S(2)}) collective-permute-start(bf16[128,1024]{1,0:T(8,128)(2,1)S(1)} %get-tuple-element.31), channel_id=1, source_target_pairs={{0,1},{1,0},{2,3},{3,2},{4,5},{5,4},{6,7},{7,6},{8,9},{9,8},{10,11... | collective-permute-start | bytes 786440 | tf_op jit(solution)/shard_map/ppermute | solution.py:207
  84.7 7.7 %collective-permute-start.15 = (bf16[128,1024]{1,0:T(8,128)(2,1)S(1)}, bf16[128,1024]{1,0:T(8,128)(2,1)}, u32[]{:S(2)}, u32[]{:S(2)}) collective-permute-start(bf16[128,1024]{1,0:T(8,128)(2,1)S(1)} %get-tuple-element.30), channel_id=1, source_target_pairs={{0,3},{1,2},{2,1},{3,0},{4,7},{5,6},{6,5},{7,4},{8,11},{9,10},{10,... | collective-permute-start | bytes 786440 | tf_op jit(solution)/shard_map/ppermute | solution.py:207

commit v2 on v0

v2 whole, which is shorter than its diff:
```python
import functools

import jax
import jax.numpy as jnp
from jax import lax
from jax.experimental import pallas as pl
from jax.experimental.pallas import tpu as pltpu
from jax.sharding import PartitionSpec as P

HEAD_DIM = 128
LOG2E = 1.4426950408889634
SCALE = HEAD_DIM ** (-0.5) * LOG2E
NEG = -1e30
ACC_ROWS = 144

VMEM = pl.BlockSpec(memory_space=pltpu.VMEM)
SMEM = pl.BlockSpec(memory_space=pltpu.SMEM)
HBM = pl.BlockSpec(memory_space=pltpu.HBM)


def ctx_pairs(size, target):
    pairs = [(i, target(i)) for i in range(size)]
    return [(i, k) for i, k in pairs if 0 <= k < size]


def shift_z(size, planes):
    return ctx_pairs(size, lambda i: i + 8 * planes)


def shift_x(size, steps):
    return ctx_pairs(size, lambda i: i // 8 * 8 + (i + 2 * steps) % 8)


def swap_core(size):
    return ctx_pairs(size, lambda i: i ^ 1)


def params(mebibytes):
    return pltpu.CompilerParams(vmem_limit_bytes=mebibytes * 1024 * 1024)


def cost(blocks, rows, more=0):
    return pl.CostEstimate(
        flops=blocks * 128 * rows * 128 * 128 + more,
        bytes_accessed=blocks * 65536,
        transcendentals=blocks * 128 * rows,
    )


def seg_row(block):
    return block[256:272].astype(jnp.float32)[0:1]


def column(row):
    return jnp.transpose(jnp.broadcast_to(row, (128, 128)))


def absorb(q, m, acc, blocks, allowed):
    keys = jnp.concatenate([b[0:128] for b in blocks], 0)
    values = jnp.concatenate([b[128:256] for b in blocks], 1)
    s = lax.dot_general(keys, q, (((1,), (1,)), ((), ())), preferred_element_type=jnp.float32)
    allowed = jnp.concatenate(allowed, 0)
    s = jnp.concatenate(
        [jnp.where(allowed, s[:, h : h + 128], NEG) for h in range(0, s.shape[1], 128)], 1
    )
    top = jnp.max(s, axis=0, keepdims=True)
    new_m = top if m is None else jnp.maximum(m, top)
    weight = jnp.exp2((s - new_m) * SCALE).astype(jnp.bfloat16)
    ones = jnp.ones((ACC_ROWS - 128, values.shape[1]), values.dtype)
    part = jnp.dot(
        jnp.concatenate([values, ones], 0), weight, preferred_element_type=jnp.float32
    )
    if m is not None:
        part = acc * jnp.exp2((m - new_m) * SCALE) + part
    return new_m, part


def pack_kernel(k_ref, v_ref, seg_ref, out_ref, v_buf, seg_buf, sems):
    copies = [
        pltpu.make_async_copy(k_ref, out_ref.at[0, 0:128, :], sems.at[0]),
        pltpu.make_async_copy(v_ref, v_buf, sems.at[1]),
        pltpu.make_async_copy(seg_ref, seg_buf, sems.at[2]),
    ]
    for copy in copies:
        copy.start()
    for copy in copies:
        copy.wait()
    out_ref[0, 128:256, :] = jnp.transpose(v_buf[...].astype(jnp.float32)).astype(out_ref.dtype)
    seg = (seg_buf[...] + 1).astype(jnp.float32)
    out_ref[0, 256:272, :] = jnp.broadcast_to(seg, (16, 128)).astype(out_ref.dtype)


def own_kernel(q_ref, own_ref, m_ref, acc_ref, heads_ref):
    width = q_ref.shape[1]
    q = jnp.concatenate(
        [q_ref[:, h * HEAD_DIM : (h + 1) * HEAD_DIM] for h in range(width // HEAD_DIM)], 0
    )
    heads_ref[...] = q
    own = own_ref[0]
    seg = seg_row(own)
    later = lax.broadcasted_iota(jnp.int32, (128, 128), 0) > lax.broadcasted_iota(
        jnp.int32, (128, 128), 1
    )
    allowed = (column(seg) == seg) & ~later
    m, acc = absorb(q, None, None, [own], [allowed])
    m_ref[...] = jnp.broadcast_to(m, m_ref.shape)
    acc_ref[...] = acc


def gather_blocks(refs):
    return [ref[(*lead,)] for ref in refs for lead in _leads(ref.shape[:-2])]


def _leads(shape):
    if not shape:
        return [()]
    return [(i, *rest) for i in range(shape[0]) for rest in _leads(shape[1:])]


def run(q_ref, own_ref, m_in, acc_in, refs):
    blocks = gather_blocks(refs)
    seg = seg_row(own_ref[0])
    allowed = [column(seg_row(block)) == seg for block in blocks]
    return absorb(q_ref[...], m_in[0:1], acc_in[...], blocks, allowed)


def group_kernel(q_ref, own_ref, m_in, acc_in, *rest):
    *refs, m_ref, acc_ref = rest
    m, acc = run(q_ref, own_ref, m_in, acc_in, refs)
    m_ref[...] = jnp.broadcast_to(m, m_ref.shape)
    acc_ref[...] = acc


def last_kernel(lane_ref, q_ref, own_ref, m_in, acc_in, far_ref, beyond_ref, w_ref, *outs):
    own_out, *shares, att = outs
    _, acc = run(q_ref, own_ref, m_in, acc_in, [far_ref, beyond_ref])
    result = acc[0:128] / acc[128:129]
    for h in range(q_ref.shape[0] // att.shape[0]):
        part = slice(h * HEAD_DIM, (h + 1) * HEAD_DIM)
        att[:, part] = jnp.transpose(result[:, part]).astype(att.dtype)
    lane = lane_ref[0]
    width = own_out.shape[1]
    for k, ref in ((2, shares[0]), (1, shares[1]), (3, shares[2]), (0, own_out)):
        columns = pl.ds(pl.multiple_of((lane ^ k) * width, width), width)
        ref[...] = jnp.dot(
            att[...], w_ref[:, columns], preferred_element_type=jnp.float32
        ).astype(ref.dtype)


def on_device(size, queries, keys, values, segment_ids, out_weight):
    tokens = queries.shape[0]
    rows = tokens * (queries.shape[1] // HEAD_DIM)
    index = lax.axis_index("ctx")
    lane = lax.axis_index("tp")
    x, c = index % 8 // 2, index % 2

    def send(value, pairs):
        return lax.ppermute(value, "ctx", pairs)

    own = pl.pallas_call(
        pack_kernel,
        out_shape=jax.ShapeDtypeStruct((1, 272, 128), jnp.bfloat16),
        in_specs=[HBM] * 3,
        out_specs=VMEM,
        scratch_shapes=[
            pltpu.VMEM((128, 128), jnp.bfloat16),
            pltpu.VMEM((1, 128), jnp.int32),
            pltpu.SemaphoreType.DMA((3,)),
        ],
        compiler_params=params(2),
        name="pack",
    )(keys, values, segment_ids[None])

    state_shape = (
        jax.ShapeDtypeStruct((8, rows), jnp.float32),
        jax.ShapeDtypeStruct((ACC_ROWS, rows), jnp.float32),
    )

    def attend(name, state, blocks, operands):
        return pl.pallas_call(
            group_kernel,
            out_shape=state_shape,
            in_specs=[VMEM] * (4 + len(operands)),
            out_specs=(VMEM, VMEM),
            compiler_params=params(16),
            cost_estimate=cost(blocks, rows),
            name=name,
        )(heads, own, *state, *operands)

    p1 = send(own, shift_z(size, 1))
    p2 = send(own, shift_z(size, 2))
    *state, heads = pl.pallas_call(
        own_kernel,
        out_shape=(*state_shape, jax.ShapeDtypeStruct((rows, HEAD_DIM), queries.dtype)),
        in_specs=[VMEM] * 2,
        out_specs=(VMEM,) * 3,
        compiler_params=params(12),
        cost_estimate=cost(1, rows),
        name="own",
    )(queries, own)
    p12 = jnp.concatenate([p1, p2], 0)
    p12, state, heads = lax.optimization_barrier((p12, state, heads))

    near_a = [p12] + [send(p12, shift_x(size, k)) for k in (2, 1, 3)]
    p34 = send(p12, shift_z(size, 2))
    p34, near_a = lax.optimization_barrier((p34, near_a))

    def with_either(first):
        return jnp.concatenate([p34[0:1], jnp.where(first, own, p34[1:2])], 0)

    far_a = send(jnp.stack(near_a), swap_core(size))
    side_b = [send(with_either(x + k < 4), shift_x(size, k)) for k in (2, 1, 3)]
    beyond = send(p34[1:2], ctx_pairs(size, lambda i: i + 1))
    state = attend("near_a", state, 8, near_a)
    state = attend("far_a", state, 8, [far_a])
    side_b, beyond, state = lax.optimization_barrier((side_b, beyond, state))

    far_b = send(jnp.stack([with_either(c == 0), *side_b]), swap_core(size))
    state = attend("near_b", state, 8, [p34, *side_b])
    width = out_weight.shape[1] // 4
    share = jax.ShapeDtypeStruct((tokens, width), jnp.bfloat16)
    total, *shares = pl.pallas_call(
        last_kernel,
        out_shape=(jax.ShapeDtypeStruct(share.shape, jnp.float32), share, share, share),
        in_specs=[SMEM] + [VMEM] * 7,
        out_specs=(VMEM,) * 4,
        scratch_shapes=[pltpu.VMEM(queries.shape, queries.dtype)],
        compiler_params=params(16),
        cost_estimate=cost(9, rows, 2 * tokens * out_weight.shape[0] * out_weight.shape[1]),
        name="last",
    )(lane[None], heads, own, *state, far_b, beyond, out_weight)

    for k, part in zip((2, 1, 3), shares):
        got = lax.ppermute(part, "tp", [(i, i ^ k) for i in range(4)])
        total = total + got.astype(jnp.float32)
    return total.astype(jnp.bfloat16)


def solution(mesh):
    placed = (P("ctx", "tp"), P("ctx", "tp"), P("ctx", "tp"), P("ctx"), P("tp", None))
    return jax.shard_map(
        functools.partial(on_device, mesh.shape["ctx"]),
        mesh=mesh,
        in_specs=placed,
        out_specs=P("ctx", "tp"),
        check_vma=False,
    )
```

time: 256 us -> 66.2 us (0.26)
  waiting for transfers between devices: 138 us -> 15.9 us
  blocking collectives: 43.9 us -> 0 us
  matrix products: 36.8 us -> 0 us
  starting transfers between devices: 0.08 us -> 34.7 us
  other arithmetic: 20.1 us -> 1.1 us
  between operations: 14.4 us -> 0.2 us
  Pallas kernels: 0 us -> 9.05 us
  local copies, waits for them, and re-layouts: 1.25 us -> 4.29 us
    all_gather x2 -> x0, waiting for transfers between devices: 115 us -> none  [the longest x1 77.7 us: on_device(): lax.all_gather(values, 'ctx', axis=0, tiled=True)]
    all_gather x1 -> x0, blocking collectives: 43.9 us -> none  [on_device(): segments_all = lax.all_gather(segment_ids, 'ctx', axis=0, tiled=True)]
    dot_general x3 -> x0, matrix products: 36.8 us -> none  [the longest x1 16.7 us: update_state(): jnp.einsum('cgrp,pcd->cgrd', weight.astype(jnp.bfloat16), value_piece, pr...]
    ppermute x0 -> x15, starting transfers between devices: none -> 34.7 us  [the longest x12 30.9 us: send(): return lax.ppermute(value, 'ctx', pairs)]
    reduce_scatter x1 -> x0, waiting for transfers between devices: 21.5 us -> none  [on_device(): lax.psum_scatter(partial_out.astype(jnp.bfloat16), 'tp', scatter_dimensio...]
    ppermute x0 -> x15, waiting for transfers between devices: none -> 15.9 us  [the longest x3 11.7 us: on_device(): got = lax.ppermute(part, 'tp', [(i, i ^ k) for i in range(4)])]
    reduce_sum x1 -> x0, other arithmetic: 15.1 us -> none  [update_state(): total = jnp.sum(weight, axis=-1)]
    pallas_call x0 -> x6, Pallas kernels: none -> 9.05 us  [the longest x3 5.13 us: attend(): pl.pallas_call(group_kernel, out_shape=state_shape, in_specs=[VMEM] * (4...]
  transfers between devices with their start and end apart: 3 -> 15, of which waited for: 3 -> 4; matrix products, arithmetic and copies ran while one was open for 0% -> 0% of each run, Pallas kernels for 0% -> 9%
where the time goes in v2:
time: 66.2 us; the launch traced here: 65.2 us
  starting transfers between devices  34.7 us (52%)
  waiting for transfers between devices  15.9 us (24%)
  Pallas kernels  9.05 us (14%)
  local copies, waits for them, and re-layouts  4.29 us (6%)
  other arithmetic  1.1 us (2%)
    ppermute x12, starting transfers between devices, send(): return lax.ppermute(value, 'ctx', pairs)  30.9 us
    ppermute x3, waiting for transfers between devices, on_device(): got = lax.ppermute(part, 'tp', [(i, i ^ k) for i in range(4)])  11.7 us
    pallas_call x3, Pallas kernels, attend(): pl.pallas_call(group_kernel, out_shape=state_shape, in_specs=[VMEM] * (4...  5.13 us
    unnamed x12, local copies, waits for them, and re-layouts  4.29 us
    ppermute x12, waiting for transfers between devices, send(): return lax.ppermute(value, 'ctx', pairs)  4.17 us
    ppermute x3, starting transfers between devices, on_device(): got = lax.ppermute(part, 'tp', [(i, i ^ k) for i in range(4)])  3.78 us
    pallas_call x1, Pallas kernels, on_device(): pl.pallas_call(last_kernel, out_shape=(jax.ShapeDtypeStruct(share.shape,...  3.24 us
  transfers between devices with their start and end apart: 15, of which 4 were waited for; matrix products, arithmetic and copies ran while one was open for 0% of the time, Pallas kernels for 9%

profile of v2, /device:TPU:1, one launch (start us, length us, event | category | flops | bytes accessed | tf_op | source)
XLA Modules:
  0.0 65.2 jit_solution(12355640423283764802)
XLA Ops:
  0.0 0.8 %copy-done = bf16[128,128]{1,0:T(8,128)(2,1)S(1)} copy-done((bf16[128,128]{1,0:T(8,128)(2,1)S(1)}, bf16[128,128]{1,0:T(8,128)(2,1)}, u32[]{:S(2)}) %copy-start) | copy-done | bytes 32792
  0.8 0.8 %copy-done.1 = bf16[128,128]{1,0:T(8,128)(2,1)S(1)} copy-done((bf16[128,128]{1,0:T(8,128)(2,1)S(1)}, bf16[128,128]{1,0:T(8,128)(2,1)}, u32[]{:S(2)}) %copy-start.1) | copy-done | bytes 32792
  1.5 0.7 %copy-done.2 = s32[128]{0:T(128)S(1)} copy-done((s32[128]{0:T(128)S(1)}, s32[128]{0:T(128)}, u32[]{:S(2)}) %copy-start.2) | copy-done | bytes 536
  2.2 0.2 pack.1.own_ref
  2.4 4.4 %collective-permute-start = (bf16[1,272,128]{2,1,0:T(8,128)(2,1)S(1)}, bf16[1,272,128]{2,1,0:T(8,128)(2,1)S(1)}, u32[]{:S(2)}, u32[]{:S(2)}) collective-permute-start(bf16[1,272,128]{2,1,0:T(8,128)(2,1)S(1)} %pack.1.own_ref), channel_id=1, source_target_pairs={{0,32},{4,36},{8,40},{12,44},{16,48},{20,52},{24,56},{28,60},{32,6... | collective-permute-start | bytes 208904 | tf_op jit(solution)/shard_map/ppermute | solution.py:158
  6.7 4.9 %collective-permute-start.1 = (bf16[1,272,128]{2,1,0:T(8,128)(2,1)S(1)}, bf16[1,272,128]{2,1,0:T(8,128)(2,1)S(1)}, u32[]{:S(2)}, u32[]{:S(2)}) collective-permute-start(bf16[1,272,128]{2,1,0:T(8,128)(2,1)S(1)} %pack.1.own_ref), channel_id=1, source_target_pairs={{0,64},{4,68},{8,72},{12,76},{16,80},{20,84},{24,88},{28,92},{32,9... | collective-permute-start | bytes 208904 | tf_op jit(solution)/shard_map/ppermute | solution.py:158
  11.7 0.9 %copy-done.3 = bf16[128,1024]{1,0:T(8,128)(2,1)S(1)} copy-done((bf16[128,1024]{1,0:T(8,128)(2,1)S(1)}, bf16[128,1024]{1,0:T(8,128)(2,1)}, u32[]{:S(2)}) %copy-start.3) | copy-done | bytes 262168
  12.6 0.5 own.1
  13.1 5.2 %collective-permute-start.2 = (bf16[2,272,128]{2,1,0:T(8,128)(2,1)S(1)}, bf16[2,272,128]{2,1,0:T(8,128)(2,1)S(1)}, u32[]{:S(2)}, u32[]{:S(2)}) collective-permute-start(bf16[2,272,128]{2,1,0:T(8,128)(2,1)S(1)} %pad_maximum_fusion.6.rest_0_), channel_id=1, source_target_pairs={{0,64},{4,68},{8,72},{12,76},{16,80},{20,84},{24,88},{28,92},{32,9... | collective-permute-start | bytes 417800 | tf_op jit(solution)/shard_map/ppermute | solution.py:158
  18.4 2.8 %collective-permute-start.3 = (bf16[2,272,128]{2,1,0:T(8,128)(2,1)S(1)}, bf16[2,272,128]{2,1,0:T(8,128)(2,1)S(1)}, u32[]{:S(2)}, u32[]{:S(2)}) collective-permute-start(bf16[2,272,128]{2,1,0:T(8,128)(2,1)S(1)} %pad_maximum_fusion.6.rest_0_), channel_id=1, source_target_pairs={{0,16},{4,20},{8,24},{12,28},{16,0},{20,4},{24,8},{28,12},{32,48},... | collective-permute-start | bytes 417800 | tf_op jit(solution)/shard_map/ppermute | solution.py:158
  21.2 0.3 collective-permute-start.4
  21.5 2.4 %collective-permute-start.5 = (bf16[2,272,128]{2,1,0:T(8,128)(2,1)S(1)}, bf16[2,272,128]{2,1,0:T(8,128)(2,1)S(1)}, u32[]{:S(2)}, u32[]{:S(2)}) collective-permute-start(bf16[2,272,128]{2,1,0:T(8,128)(2,1)S(1)} %pad_maximum_fusion.6.rest_0_), channel_id=1, source_target_pairs={{0,24},{4,28},{8,0},{12,4},{16,8},{20,12},{24,16},{28,20},{32,56},... | collective-permute-start | bytes 417800 | tf_op jit(solution)/shard_map/ppermute | solution.py:158
  23.9 3.9 %collective-permute-done.4.rest_2_ = bf16[2,272,128]{2,1,0:T(8,128)(2,1)S(1)} collective-permute-done((bf16[2,272,128]{2,1,0:T(8,128)(2,1)S(1)}, bf16[2,272,128]{2,1,0:T(8,128)(2,1)S(1)}, u32[]{:S(2)}, u32[]{:S(2)}) %collective-permute-start.4) | collective-permute-done | bytes 139296 | tf_op jit(solution)/shard_map/ppermute | solution.py:158
  27.9 2.9 %collective-permute-start.10 = (bf16[4,2,272,128]{3,2,1,0:T(8,128)(2,1)S(1)}, bf16[4,2,272,128]{3,2,1,0:T(8,128)(2,1)S(1)}, u32[]{:S(2)}, u32[]{:S(2)}) collective-permute-start(bf16[4,2,272,128]{3,2,1,0:T(8,128)(2,1)S(1)} %pad_maximum_fusion), channel_id=1, source_target_pairs={{0,4},{4,0},{8,12},{12,8},{16,20},{20,16},{24,28},{28,24},{32,36},... | collective-permute-start | bytes 1671176 | tf_op jit(solution)/shard_map/ppermute | solution.py:158
  30.9 1.3 %collective-permute-start.6 = (bf16[2,272,128]{2,1,0:T(8,128)(2,1)S(1)}, bf16[2,272,128]{2,1,0:T(8,128)(2,1)S(1)}, u32[]{:S(2)}, u32[]{:S(2)}) collective-permute-start(bf16[2,272,128]{2,1,0:T(8,128)(2,1)S(1)} %get-tuple-element.70), channel_id=1, source_target_pairs={{0,16},{4,20},{8,24},{12,28},{16,0},{20,4},{24,8},{28,12},{32,48},... | collective-permute-start | bytes 417800 | tf_op jit(solution)/shard_map/ppermute | solution.py:158
  32.2 2.3 %collective-permute-start.7 = (bf16[2,272,128]{2,1,0:T(8,128)(2,1)S(1)}, bf16[2,272,128]{2,1,0:T(8,128)(2,1)S(1)}, u32[]{:S(2)}, u32[]{:S(2)}) collective-permute-start(bf16[2,272,128]{2,1,0:T(8,128)(2,1)S(1)} %get-tuple-element.68), channel_id=1, source_target_pairs={{0,8},{4,12},{8,16},{12,20},{16,24},{20,28},{24,0},{28,4},{32,40},... | collective-permute-start | bytes 417800 | tf_op jit(solution)/shard_map/ppermute | solution.py:158
  34.5 0.3 collective-permute-start.8
  34.8 3.8 %collective-permute-start.9 = (bf16[1,272,128]{2,1,0:T(8,128)(2,1)S(1)}, bf16[1,272,128]{2,1,0:T(8,128)(2,1)S(1)}, u32[]{:S(2)}, u32[]{:S(2)}) collective-permute-start(bf16[1,272,128]{2,1,0:T(8,128)(2,1)S(1)} %get-tuple-element.65), channel_id=1, source_target_pairs={{0,4},{4,8},{8,12},{12,16},{16,20},{20,24},{24,28},{28,32},{32,36}... | collective-permute-start | bytes 208904 | tf_op jit(solution)/shard_map/ppermute | solution.py:158
  38.6 1.7 %near_a.1 = (f32[8,1024]{1,0:T(8,128)S(1)}, f32[144,1024]{1,0:T(8,128)S(1)}) custom-call(bf16[1024,128]{1,0:T(8,128)(2,1)S(1)} %get-tuple-element.36.q_ref, bf16[1,272,128]{2,1,0:T(8,128)(2,1)S(1)} %pack.1.own_ref, f32[8,1024]{1,0:T(8,128)S(1)} %get-tuple-element.39.m_in, f32[144,1024]{1,0:T(8,128)S(1)} %get-tuple-element.40.acc_in, ...), custom_call_target="tpu_custom_call" | custom-call | flops 17179869184 | bytes 524288 | tf_op jit(solution)/shard_map/near_a/pallas_call | solution.py:180
  40.4 1.7 %far_a.1 = (f32[8,1024]{1,0:T(8,128)S(1)}, f32[144,1024]{1,0:T(8,128)S(1)}) custom-call(bf16[1024,128]{1,0:T(8,128)(2,1)S(1)} %get-tuple-element.36.q_ref, bf16[1,272,128]{2,1,0:T(8,128)(2,1)S(1)} %pack.1.own_ref, f32[8,1024]{1,0:T(8,128)S(1)} %get-tuple-element.45.m_in, f32[144,1024]{1,0:T(8,128)S(1)} %get-tuple-element.46.acc_in, ...), custom_call_target="tpu_custom_call" | custom-call | flops 17179869184 | bytes 524288 | tf_op jit(solution)/shard_map/far_a/pallas_call | solution.py:180
  42.1 0.1 pad_maximum_fusion.1
  42.2 0.3 collective-permute-start.11
  42.5 1.7 %near_b.1 = (f32[8,1024]{1,0:T(8,128)S(1)}, f32[144,1024]{1,0:T(8,128)S(1)}) custom-call(bf16[1024,128]{1,0:T(8,128)(2,1)S(1)} %get-tuple-element.36.q_ref, bf16[1,272,128]{2,1,0:T(8,128)(2,1)S(1)} %pack.1.own_ref, f32[8,1024]{1,0:T(8,128)S(1)} %get-tuple-element.49.m_in, f32[144,1024]{1,0:T(8,128)S(1)} %get-tuple-element.50.acc_in, ...), custom_call_target="tpu_custom_call" | custom-call | flops 17179869184 | bytes 524288 | tf_op jit(solution)/shard_map/near_b/pallas_call | solution.py:180
  44.2 0.2 collective-permute-done.11.far_ref
  44.5 1.2 %slice-done.1 = s8[4194304]{0:T(1024)(128)(4,1)S(1)} async-done(((s8[8388608]{0:T(1024)(128)(4,1)}), s8[4194304]{0:T(1024)(128)(4,1)S(1)}, s32[]{:S(2)}) %slice-start.1) | async-done | bytes 4194328
  45.6 3.2 %last.1 = (f32[128,1024]{1,0:T(8,128)S(1)}, bf16[128,1024]{1,0:T(8,128)(2,1)S(1)}, bf16[128,1024]{1,0:T(8,128)(2,1)S(1)}, bf16[128,1024]{1,0:T(8,128)(2,1)S(1)}) custom-call(s32[1]{0:T(128)} %bitcast.lane_ref, bf16[1024,128]{1,0:T(8,128)(2,1)S(1)} %get-tuple-element.36.q_ref, bf16[1,272,128]{2,1,0:T(8,128)(2,1)S(1)} %pack.1.own_ref, ...), custom_call_target="tpu_custom_call" | custom-call | flops 20401094656 | bytes 589824 | tf_op jit(solution)/shard_map/last/pallas_call | solution.py:222
  48.9 3.0 %collective-permute-start.12 = (bf16[128,1024]{1,0:T(8,128)(2,1)S(1)}, bf16[128,1024]{1,0:T(8,128)(2,1)S(1)}, u32[]{:S(2)}, u32[]{:S(2)}) collective-permute-start(bf16[128,1024]{1,0:T(8,128)(2,1)S(1)} %get-tuple-element.58), channel_id=1, source_target_pairs={{0,2},{1,3},{2,0},{3,1},{4,6},{5,7},{6,4},{7,5},{8,10},{9,11},{10,... | collective-permute-start | bytes 786440 | tf_op jit(solution)/shard_map/ppermute | solution.py:234
  51.9 0.4 collective-permute-start.13
  52.3 0.4 collective-permute-start.14
  52.7 5.8 %collective-permute-done.12 = bf16[128,1024]{1,0:T(8,128)(2,1)S(1)} collective-permute-done((bf16[128,1024]{1,0:T(8,128)(2,1)S(1)}, bf16[128,1024]{1,0:T(8,128)(2,1)S(1)}, u32[]{:S(2)}, u32[]{:S(2)}) %collective-permute-start.12) | collective-permute-done | bytes 262176 | tf_op jit(solution)/shard_map/ppermute | solution.py:234
  58.4 6.0 %collective-permute-done.13 = bf16[128,1024]{1,0:T(8,128)(2,1)S(1)} collective-permute-done((bf16[128,1024]{1,0:T(8,128)(2,1)S(1)}, bf16[128,1024]{1,0:T(8,128)(2,1)S(1)}, u32[]{:S(2)}, u32[]{:S(2)}) %collective-permute-start.13) | collective-permute-done | bytes 262176 | tf_op jit(solution)/shard_map/ppermute | solution.py:234
  64.4 0.9 %add_convert_fusion = bf16[128,1024]{1,0:T(8,128)(2,1)} fusion(bf16[128,1024]{1,0:T(8,128)(2,1)S(1)} %collective-permute-done.14, bf16[128,1024]{1,0:T(8,128)(2,1)S(1)} %collective-permute-done.13, f32[128,1024]{1,0:T(8,128)S(1)} %get-tuple-element.57, bf16[128,1024]{1,0:T(8,128)(2,1)S(1)} %collective-permute-done.12), kind=kLoop, calls=%fused_computation.2 | loop fusion | flops 917504 | bytes 1572864 | tf_op jit(solution)/shard_map/convert_element_type | solution.py:236
  (23 shorter events, 0.2 us)
Async XLA Ops:
  0.0 0.8 %copy-start = (bf16[128,128]{1,0:T(8,128)(2,1)S(1)}, bf16[128,128]{1,0:T(8,128)(2,1)}, u32[]{:S(2)}) copy-start(bf16[128,128]{1,0:T(8,128)(2,1)} %k_ref.1) | copy-start | bytes 98308
  0.8 0.8 %copy-start.1 = (bf16[128,128]{1,0:T(8,128)(2,1)S(1)}, bf16[128,128]{1,0:T(8,128)(2,1)}, u32[]{:S(2)}) copy-start(bf16[128,128]{1,0:T(8,128)(2,1)} %v_ref.1) | copy-start | bytes 98308
  1.5 0.7 %copy-start.2 = (s32[128]{0:T(128)S(1)}, s32[128]{0:T(128)}, u32[]{:S(2)}) copy-start(s32[128]{0:T(128)} %param.8) | copy-start | bytes 1540
  2.4 10.7 %collective-permute-start = (bf16[1,272,128]{2,1,0:T(8,128)(2,1)S(1)}, bf16[1,272,128]{2,1,0:T(8,128)(2,1)S(1)}, u32[]{:S(2)}, u32[]{:S(2)}) collective-permute-start(bf16[1,272,128]{2,1,0:T(8,128)(2,1)S(1)} %pack.1.own_ref), channel_id=1, source_target_pairs={{0,32},{4,36},{8,40},{12,44},{16,48},{20,52},{24,56},{28,60},{32,6... | collective-permute-start | bytes 208904 | tf_op jit(solution)/shard_map/ppermute | solution.py:158
  6.7 6.4 %collective-permute-start.1 = (bf16[1,272,128]{2,1,0:T(8,128)(2,1)S(1)}, bf16[1,272,128]{2,1,0:T(8,128)(2,1)S(1)}, u32[]{:S(2)}, u32[]{:S(2)}) collective-permute-start(bf16[1,272,128]{2,1,0:T(8,128)(2,1)S(1)} %pack.1.own_ref), channel_id=1, source_target_pairs={{0,64},{4,68},{8,72},{12,76},{16,80},{20,84},{24,88},{28,92},{32,9... | collective-permute-start | bytes 208904 | tf_op jit(solution)/shard_map/ppermute | solution.py:158
  11.7 1.0 %copy-start.3 = (bf16[128,1024]{1,0:T(8,128)(2,1)S(1)}, bf16[128,1024]{1,0:T(8,128)(2,1)}, u32[]{:S(2)}) copy-start(bf16[128,1024]{1,0:T(8,128)(2,1)} %q_ref.1) | copy-start | bytes 786436
  13.1 10.7 %collective-permute-start.2 = (bf16[2,272,128]{2,1,0:T(8,128)(2,1)S(1)}, bf16[2,272,128]{2,1,0:T(8,128)(2,1)S(1)}, u32[]{:S(2)}, u32[]{:S(2)}) collective-permute-start(bf16[2,272,128]{2,1,0:T(8,128)(2,1)S(1)} %pad_maximum_fusion.6.rest_0_), channel_id=1, source_target_pairs={{0,64},{4,68},{8,72},{12,76},{16,80},{20,84},{24,88},{28,92},{32,9... | collective-permute-start | bytes 417800 | tf_op jit(solution)/shard_map/ppermute | solution.py:158
  18.4 5.5 %collective-permute-start.3 = (bf16[2,272,128]{2,1,0:T(8,128)(2,1)S(1)}, bf16[2,272,128]{2,1,0:T(8,128)(2,1)S(1)}, u32[]{:S(2)}, u32[]{:S(2)}) collective-permute-start(bf16[2,272,128]{2,1,0:T(8,128)(2,1)S(1)} %pad_maximum_fusion.6.rest_0_), channel_id=1, source_target_pairs={{0,16},{4,20},{8,24},{12,28},{16,0},{20,4},{24,8},{28,12},{32,48},... | collective-permute-start | bytes 417800 | tf_op jit(solution)/shard_map/ppermute | solution.py:158
  21.2 6.6 %collective-permute-start.4 = (bf16[2,272,128]{2,1,0:T(8,128)(2,1)S(1)}, bf16[2,272,128]{2,1,0:T(8,128)(2,1)S(1)}, u32[]{:S(2)}, u32[]{:S(2)}) collective-permute-start(bf16[2,272,128]{2,1,0:T(8,128)(2,1)S(1)} %pad_maximum_fusion.6.rest_0_), channel_id=1, source_target_pairs={{0,8},{4,12},{8,16},{12,20},{16,24},{20,28},{24,0},{28,4},{32,40},... | collective-permute-start | bytes 417800 | tf_op jit(solution)/shard_map/ppermute | solution.py:158
  21.5 6.3 %collective-permute-start.5 = (bf16[2,272,128]{2,1,0:T(8,128)(2,1)S(1)}, bf16[2,272,128]{2,1,0:T(8,128)(2,1)S(1)}, u32[]{:S(2)}, u32[]{:S(2)}) collective-permute-start(bf16[2,272,128]{2,1,0:T(8,128)(2,1)S(1)} %pad_maximum_fusion.6.rest_0_), channel_id=1, source_target_pairs={{0,24},{4,28},{8,0},{12,4},{16,8},{20,12},{24,16},{28,20},{32,56},... | collective-permute-start | bytes 417800 | tf_op jit(solution)/shard_map/ppermute | solution.py:158
  27.9 12.5 %collective-permute-start.10 = (bf16[4,2,272,128]{3,2,1,0:T(8,128)(2,1)S(1)}, bf16[4,2,272,128]{3,2,1,0:T(8,128)(2,1)S(1)}, u32[]{:S(2)}, u32[]{:S(2)}) collective-permute-start(bf16[4,2,272,128]{3,2,1,0:T(8,128)(2,1)S(1)} %pad_maximum_fusion), channel_id=1, source_target_pairs={{0,4},{4,0},{8,12},{12,8},{16,20},{20,16},{24,28},{28,24},{32,36},... | collective-permute-start | bytes 1671176 | tf_op jit(solution)/shard_map/ppermute | solution.py:158
  30.9 11.2 %collective-permute-start.6 = (bf16[2,272,128]{2,1,0:T(8,128)(2,1)S(1)}, bf16[2,272,128]{2,1,0:T(8,128)(2,1)S(1)}, u32[]{:S(2)}, u32[]{:S(2)}) collective-permute-start(bf16[2,272,128]{2,1,0:T(8,128)(2,1)S(1)} %get-tuple-element.70), channel_id=1, source_target_pairs={{0,16},{4,20},{8,24},{12,28},{16,0},{20,4},{24,8},{28,12},{32,48},... | collective-permute-start | bytes 417800 | tf_op jit(solution)/shard_map/ppermute | solution.py:158
  32.2 9.9 %collective-permute-start.7 = (bf16[2,272,128]{2,1,0:T(8,128)(2,1)S(1)}, bf16[2,272,128]{2,1,0:T(8,128)(2,1)S(1)}, u32[]{:S(2)}, u32[]{:S(2)}) collective-permute-start(bf16[2,272,128]{2,1,0:T(8,128)(2,1)S(1)} %get-tuple-element.68), channel_id=1, source_target_pairs={{0,8},{4,12},{8,16},{12,20},{16,24},{20,28},{24,0},{28,4},{32,40},... | collective-permute-start | bytes 417800 | tf_op jit(solution)/shard_map/ppermute | solution.py:158
  34.5 7.6 %collective-permute-start.8 = (bf16[2,272,128]{2,1,0:T(8,128)(2,1)S(1)}, bf16[2,272,128]{2,1,0:T(8,128)(2,1)S(1)}, u32[]{:S(2)}, u32[]{:S(2)}) collective-permute-start(bf16[2,272,128]{2,1,0:T(8,128)(2,1)S(1)} %get-tuple-element.69), channel_id=1, source_target_pairs={{0,24},{4,28},{8,0},{12,4},{16,8},{20,12},{24,16},{28,20},{32,56},... | collective-permute-start | bytes 417800 | tf_op jit(solution)/shard_map/ppermute | solution.py:158
  34.8 7.2 %collective-permute-start.9 = (bf16[1,272,128]{2,1,0:T(8,128)(2,1)S(1)}, bf16[1,272,128]{2,1,0:T(8,128)(2,1)S(1)}, u32[]{:S(2)}, u32[]{:S(2)}) collective-permute-start(bf16[1,272,128]{2,1,0:T(8,128)(2,1)S(1)} %get-tuple-element.65), channel_id=1, source_target_pairs={{0,4},{4,8},{8,12},{12,16},{16,20},{20,24},{24,28},{28,32},{32,36}... | collective-permute-start | bytes 208904 | tf_op jit(solution)/shard_map/ppermute | solution.py:158
  42.1 2.3 %slice-start = ((s8[8388608]{0:T(1024)(128)(4,1)}), s8[4194304]{0:T(1024)(128)(4,1)S(1)}, s32[]{:S(2)}) async-start(s8[8388608]{0:T(1024)(128)(4,1)} %bitcast.19), calls=%async_computation | async-start | bytes 8388608
  42.2 3.4 %slice-start.1 = ((s8[8388608]{0:T(1024)(128)(4,1)}), s8[4194304]{0:T(1024)(128)(4,1)S(1)}, s32[]{:S(2)}) async-start(s8[8388608]{0:T(1024)(128)(4,1)} %bitcast.19), calls=%async_computation.1 | async-start | bytes 8388608
  42.2 2.2 %collective-permute-start.11 = (bf16[4,2,272,128]{3,2,1,0:T(8,128)(2,1)S(1)}, bf16[4,2,272,128]{3,2,1,0:T(8,128)(2,1)S(1)}, u32[]{:S(2)}, u32[]{:S(2)}) collective-permute-start(bf16[4,2,272,128]{3,2,1,0:T(8,128)(2,1)S(1)} %pad_maximum_fusion.1), channel_id=1, source_target_pairs={{0,4},{4,0},{8,12},{12,8},{16,20},{20,16},{24,28},{28,24},{32,36},... | collective-permute-start | bytes 1671176 | tf_op jit(solution)/shard_map/ppermute | solution.py:158
  48.9 9.5 %collective-permute-start.12 = (bf16[128,1024]{1,0:T(8,128)(2,1)S(1)}, bf16[128,1024]{1,0:T(8,128)(2,1)S(1)}, u32[]{:S(2)}, u32[]{:S(2)}) collective-permute-start(bf16[128,1024]{1,0:T(8,128)(2,1)S(1)} %get-tuple-element.58), channel_id=1, source_target_pairs={{0,2},{1,3},{2,0},{3,1},{4,6},{5,7},{6,4},{7,5},{8,10},{9,11},{10,... | collective-permute-start | bytes 786440 | tf_op jit(solution)/shard_map/ppermute | solution.py:234
  51.9 12.5 %collective-permute-start.13 = (bf16[128,1024]{1,0:T(8,128)(2,1)S(1)}, bf16[128,1024]{1,0:T(8,128)(2,1)S(1)}, u32[]{:S(2)}, u32[]{:S(2)}) collective-permute-start(bf16[128,1024]{1,0:T(8,128)(2,1)S(1)} %get-tuple-element.59), channel_id=1, source_target_pairs={{0,1},{1,0},{2,3},{3,2},{4,5},{5,4},{6,7},{7,6},{8,9},{9,8},{10,11... | collective-permute-start | bytes 786440 | tf_op jit(solution)/shard_map/ppermute | solution.py:234
  52.3 12.1 %collective-permute-start.14 = (bf16[128,1024]{1,0:T(8,128)(2,1)S(1)}, bf16[128,1024]{1,0:T(8,128)(2,1)S(1)}, u32[]{:S(2)}, u32[]{:S(2)}) collective-permute-start(bf16[128,1024]{1,0:T(8,128)(2,1)S(1)} %get-tuple-element.60), channel_id=1, source_target_pairs={{0,3},{1,2},{2,1},{3,0},{4,7},{5,6},{6,5},{7,4},{8,11},{9,10},{10,... | collective-permute-start | bytes 786440 | tf_op jit(solution)/shard_map/ppermute | solution.py:234

commit v3 on v2

--- a/solution.py
+++ b/solution.py
@@ -131,19 +131,20 @@
     acc_ref[...] = acc
 
 
-def last_kernel(lane_ref, q_ref, own_ref, m_in, acc_in, far_ref, beyond_ref, w_ref, *outs):
-    own_out, *shares, att = outs
+def last_kernel(q_ref, own_ref, m_in, acc_in, far_ref, beyond_ref, att_ref):
     _, acc = run(q_ref, own_ref, m_in, acc_in, [far_ref, beyond_ref])
     result = acc[0:128] / acc[128:129]
-    for h in range(q_ref.shape[0] // att.shape[0]):
+    for h in range(q_ref.shape[0] // att_ref.shape[0]):
         part = slice(h * HEAD_DIM, (h + 1) * HEAD_DIM)
-        att[:, part] = jnp.transpose(result[:, part]).astype(att.dtype)
-    lane = lane_ref[0]
-    width = own_out.shape[1]
-    for k, ref in ((2, shares[0]), (1, shares[1]), (3, shares[2]), (0, own_out)):
-        columns = pl.ds(pl.multiple_of((lane ^ k) * width, width), width)
+        att_ref[:, part] = jnp.transpose(result[:, part]).astype(att_ref.dtype)
+
+
+def project_kernel(steps, lane_ref, att_ref, w_ref, *outs):
+    for k, ref in zip(steps, outs):
+        width = ref.shape[1]
+        columns = pl.ds(pl.multiple_of((lane_ref[0] ^ k) * width, width), width)
         ref[...] = jnp.dot(
-            att[...], w_ref[:, columns], preferred_element_type=jnp.float32
+            att_ref[...], w_ref[:, columns], preferred_element_type=jnp.float32
         ).astype(ref.dtype)
 
 
@@ -167,7 +168,7 @@
             pltpu.VMEM((1, 128), jnp.int32),
             pltpu.SemaphoreType.DMA((3,)),
         ],
-        compiler_params=params(2),
+        compiler_params=params(60),
         name="pack",
     )(keys, values, segment_ids[None])
 
@@ -187,8 +188,8 @@
             name=name,
         )(heads, own, *state, *operands)
 
+    p2 = send(own, shift_z(size, 2))
     p1 = send(own, shift_z(size, 1))
-    p2 = send(own, shift_z(size, 2))
     *state, heads = pl.pallas_call(
         own_kernel,
         out_shape=(*state_shape, jax.ShapeDtypeStruct((rows, HEAD_DIM), queries.dtype)),
@@ -198,12 +199,14 @@
         cost_estimate=cost(1, rows),
         name="own",
     )(queries, own)
+    p2, p1, state, heads = lax.optimization_barrier((p2, p1, state, heads))
     p12 = jnp.concatenate([p1, p2], 0)
-    p12, state, heads = lax.optimization_barrier((p12, state, heads))
 
     near_a = [p12] + [send(p12, shift_x(size, k)) for k in (2, 1, 3)]
     p34 = send(p12, shift_z(size, 2))
-    p34, near_a = lax.optimization_barrier((p34, near_a))
+    p34, near_a[2], near_a[3], near_a[1], near_a[0] = lax.optimization_barrier(
+        (p34, near_a[2], near_a[3], near_a[1], near_a[0])
+    )
 
     def with_either(first):
         return jnp.concatenate([p34[0:1], jnp.where(first, own, p34[1:2])], 0)
@@ -213,26 +216,47 @@
     beyond = send(p34[1:2], ctx_pairs(size, lambda i: i + 1))
     state = attend("near_a", state, 8, near_a)
     state = attend("far_a", state, 8, [far_a])
-    side_b, beyond, state = lax.optimization_barrier((side_b, beyond, state))
+    side_b[1], side_b[2], side_b[0], beyond, state = lax.optimization_barrier(
+        (side_b[1], side_b[2], side_b[0], beyond, state)
+    )
 
     far_b = send(jnp.stack([with_either(c == 0), *side_b]), swap_core(size))
     state = attend("near_b", state, 8, [p34, *side_b])
+    attention = pl.pallas_call(
+        last_kernel,
+        out_shape=jax.ShapeDtypeStruct(queries.shape, queries.dtype),
+        in_specs=[VMEM] * 6,
+        out_specs=VMEM,
+        compiler_params=params(16),
+        cost_estimate=cost(9, rows),
+        name="last",
+    )(heads, own, *state, far_b, beyond)
+
     width = out_weight.shape[1] // 4
-    share = jax.ShapeDtypeStruct((tokens, width), jnp.bfloat16)
-    total, *shares = pl.pallas_call(
-        last_kernel,
-        out_shape=(jax.ShapeDtypeStruct(share.shape, jnp.float32), share, share, share),
-        in_specs=[SMEM] + [VMEM] * 7,
-        out_specs=(VMEM,) * 4,
-        scratch_shapes=[pltpu.VMEM(queries.shape, queries.dtype)],
-        compiler_params=params(16),
-        cost_estimate=cost(9, rows, 2 * tokens * out_weight.shape[0] * out_weight.shape[1]),
-        name="last",
-    )(lane[None], heads, own, *state, far_b, beyond, out_weight)
-
-    for k, part in zip((2, 1, 3), shares):
-        got = lax.ppermute(part, "tp", [(i, i ^ k) for i in range(4)])
-        total = total + got.astype(jnp.float32)
+
+    def project(name, steps, dtypes):
+        return pl.pallas_call(
+            functools.partial(project_kernel, steps),
+            out_shape=tuple(jax.ShapeDtypeStruct((tokens, width), dtype) for dtype in dtypes),
+            in_specs=[SMEM] + [VMEM] * 2,
+            out_specs=(VMEM,) * len(steps),
+            compiler_params=params(8),
+            cost_estimate=pl.CostEstimate(
+                flops=2 * len(steps) * tokens * width * out_weight.shape[0],
+                bytes_accessed=2 * len(steps) * width * out_weight.shape[0],
+                transcendentals=0,
+            ),
+            name=name,
+        )(lane[None], attention, out_weight)
+
+    def pass_on(part, k):
+        return lax.ppermute(part, "tp", [(i, i ^ k) for i in range(4)])
+
+    share_2, share_1, share_3, total = project(
+        "project", (2, 1, 3, 0), (*[jnp.bfloat16] * 3, jnp.float32)
+    )
+    for k, part in ((2, share_2), (1, share_1), (3, share_3)):
+        total = total + pass_on(part, k).astype(jnp.float32)
     return total.astype(jnp.bfloat16)
 
 

time: 66.2 us -> 64.6 us (0.976)
  local copies, waits for them, and re-layouts: 4.29 us -> 2.16 us
  Pallas kernels: 9.05 us -> 10.4 us
    unnamed x12 -> x11, local copies, waits for them, and re-layouts: 4.29 us -> 2.15 us
    pallas_call x1, Pallas kernels: 0.18 us -> 1.53 us  [on_device(): pl.pallas_call(pack_kernel, out_shape=jax.ShapeDtypeStruct((1, 272, 128),...]
    pallas_call x1 -> x2, Pallas kernels: 3.24 us -> 3.25 us  [the longest x1 1.98 us: on_device(): pl.pallas_call(last_kernel, out_shape=jax.ShapeDtypeStruct(queries.shape,...]
  transfers between devices with their start and end apart: 15 -> 15, of which waited for: 4 -> 5; matrix products, arithmetic and copies ran while one was open for 0% -> 0% of each run, Pallas kernels for 9% -> 9%
where the time goes in v3:
time: 64.6 us; the launch traced here: 64.2 us
  starting transfers between devices  34.2 us (53%)
  waiting for transfers between devices  16.2 us (25%)
  Pallas kernels  10.4 us (16%)
  local copies, waits for them, and re-layouts  2.16 us (3%)
  other arithmetic  1.08 us (2%)
    ppermute x12, starting transfers between devices, send(): return lax.ppermute(value, 'ctx', pairs)  30.4 us
    ppermute x3, waiting for transfers between devices, pass_on(): return lax.ppermute(part, 'tp', [(i, i ^ k) for i in range(4)])  11.7 us
    pallas_call x3, Pallas kernels, attend(): pl.pallas_call(group_kernel, out_shape=state_shape, in_specs=[VMEM] * (4...  5.13 us
    ppermute x12, waiting for transfers between devices, send(): return lax.ppermute(value, 'ctx', pairs)  4.55 us
    ppermute x3, starting transfers between devices, pass_on(): return lax.ppermute(part, 'tp', [(i, i ^ k) for i in range(4)])  3.78 us
    unnamed x11, local copies, waits for them, and re-layouts  2.15 us
    pallas_call x1, Pallas kernels, on_device(): pl.pallas_call(last_kernel, out_shape=jax.ShapeDtypeStruct(queries.shape,...  1.98 us
    pallas_call x1, Pallas kernels, on_device(): pl.pallas_call(pack_kernel, out_shape=jax.ShapeDtypeStruct((1, 272, 128),...  1.53 us
  transfers between devices with their start and end apart: 15, of which 5 were waited for; matrix products, arithmetic and copies ran while one was open for 0% of the time, Pallas kernels for 9%

profile of v3, /device:TPU:1, one launch (start us, length us, event | category | flops | bytes accessed | tf_op | source)
XLA Modules:
  0.0 64.2 jit_solution(3339760654115064119)
XLA Ops:
  0.0 1.5 %pack.1.own_ref = bf16[1,272,128]{2,1,0:T(8,128)(2,1)} custom-call(bf16[128,128]{1,0:T(8,128)(2,1)} %k_ref.1, bf16[128,128]{1,0:T(8,128)(2,1)} %v_ref.1, s32[1,128]{1,0:T(1,128)} %bitcast.20), custom_call_target="tpu_custom_call" | custom-call | tf_op jit(solution)/shard_map/pack/pallas_call | solution.py:161
  1.5 5.7 %collective-permute-start = (bf16[1,272,128]{2,1,0:T(8,128)(2,1)}, bf16[1,272,128]{2,1,0:T(8,128)(2,1)S(1)}, u32[]{:S(2)}, u32[]{:S(2)}) collective-permute-start(bf16[1,272,128]{2,1,0:T(8,128)(2,1)} %pack.1.own_ref), channel_id=1, source_target_pairs={{0,64},{4,68},{8,72},{12,76},{16,80},{20,84},{24,88},{28,92},{32,9... | collective-permute-start | bytes 208904 | tf_op jit(solution)/shard_map/ppermute | solution.py:159
  7.3 3.5 %collective-permute-start.1 = (bf16[1,272,128]{2,1,0:T(8,128)(2,1)}, bf16[1,272,128]{2,1,0:T(8,128)(2,1)S(1)}, u32[]{:S(2)}, u32[]{:S(2)}) collective-permute-start(bf16[1,272,128]{2,1,0:T(8,128)(2,1)} %pack.1.own_ref), channel_id=1, source_target_pairs={{0,32},{4,36},{8,40},{12,44},{16,48},{20,52},{24,56},{28,60},{32,6... | collective-permute-start | bytes 208904 | tf_op jit(solution)/shard_map/ppermute | solution.py:159
  10.8 0.9 %copy-done = bf16[1,272,128]{2,1,0:T(8,128)(2,1)S(1)} copy-done((bf16[1,272,128]{2,1,0:T(8,128)(2,1)S(1)}, bf16[1,272,128]{2,1,0:T(8,128)(2,1)}, u32[]{:S(2)}) %copy-start) | copy-done | bytes 69656
  11.7 0.9 %copy-done.2 = bf16[128,1024]{1,0:T(8,128)(2,1)S(1)} copy-done((bf16[128,1024]{1,0:T(8,128)(2,1)S(1)}, bf16[128,1024]{1,0:T(8,128)(2,1)}, u32[]{:S(2)}) %copy-start.2) | copy-done | bytes 262168
  12.7 0.5 own.1
  13.2 5.5 %collective-permute-start.2 = (bf16[2,272,128]{2,1,0:T(8,128)(2,1)S(1)}, bf16[2,272,128]{2,1,0:T(8,128)(2,1)S(1)}, u32[]{:S(2)}, u32[]{:S(2)}) collective-permute-start(bf16[2,272,128]{2,1,0:T(8,128)(2,1)S(1)} %constant_dynamic-update-slice_fusion.rest_0_), channel_id=1, source_target_pairs={{0,64},{4,68},{8,72},{12,76},{16,80},{20,84},{24,88},{28,92},{32,9... | collective-permute-start | bytes 417800 | tf_op jit(solution)/shard_map/ppermute | solution.py:159
  18.7 1.3 %collective-permute-start.3 = (bf16[2,272,128]{2,1,0:T(8,128)(2,1)S(1)}, bf16[2,272,128]{2,1,0:T(8,128)(2,1)S(1)}, u32[]{:S(2)}, u32[]{:S(2)}) collective-permute-start(bf16[2,272,128]{2,1,0:T(8,128)(2,1)S(1)} %constant_dynamic-update-slice_fusion.rest_0_), channel_id=1, source_target_pairs={{0,8},{4,12},{8,16},{12,20},{16,24},{20,28},{24,0},{28,4},{32,40},... | collective-permute-start | bytes 417800 | tf_op jit(solution)/shard_map/ppermute | solution.py:159
  20.0 1.5 %collective-permute-start.4 = (bf16[2,272,128]{2,1,0:T(8,128)(2,1)S(1)}, bf16[2,272,128]{2,1,0:T(8,128)(2,1)S(1)}, u32[]{:S(2)}, u32[]{:S(2)}) collective-permute-start(bf16[2,272,128]{2,1,0:T(8,128)(2,1)S(1)} %constant_dynamic-update-slice_fusion.rest_0_), channel_id=1, source_target_pairs={{0,24},{4,28},{8,0},{12,4},{16,8},{20,12},{24,16},{28,20},{32,56},... | collective-permute-start | bytes 417800 | tf_op jit(solution)/shard_map/ppermute | solution.py:159
  21.4 1.5 %collective-permute-start.5 = (bf16[2,272,128]{2,1,0:T(8,128)(2,1)S(1)}, bf16[2,272,128]{2,1,0:T(8,128)(2,1)S(1)}, u32[]{:S(2)}, u32[]{:S(2)}) collective-permute-start(bf16[2,272,128]{2,1,0:T(8,128)(2,1)S(1)} %constant_dynamic-update-slice_fusion.rest_0_), channel_id=1, source_target_pairs={{0,16},{4,20},{8,24},{12,28},{16,0},{20,4},{24,8},{28,12},{32,48},... | collective-permute-start | bytes 417800 | tf_op jit(solution)/shard_map/ppermute | solution.py:159
  23.0 0.9 %collective-permute-done.3.rest_2_ = bf16[2,272,128]{2,1,0:T(8,128)(2,1)S(1)} collective-permute-done((bf16[2,272,128]{2,1,0:T(8,128)(2,1)S(1)}, bf16[2,272,128]{2,1,0:T(8,128)(2,1)S(1)}, u32[]{:S(2)}, u32[]{:S(2)}) %collective-permute-start.3) | collective-permute-done | bytes 139296 | tf_op jit(solution)/shard_map/ppermute | solution.py:159
  23.9 3.6 %collective-permute-done.5.rest_1_ = bf16[2,272,128]{2,1,0:T(8,128)(2,1)S(1)} collective-permute-done((bf16[2,272,128]{2,1,0:T(8,128)(2,1)S(1)}, bf16[2,272,128]{2,1,0:T(8,128)(2,1)S(1)}, u32[]{:S(2)}, u32[]{:S(2)}) %collective-permute-start.5) | collective-permute-done | bytes 139296 | tf_op jit(solution)/shard_map/ppermute | solution.py:159
  27.6 3.5 %collective-permute-start.10 = (bf16[4,2,272,128]{3,2,1,0:T(8,128)(2,1)S(1)}, bf16[4,2,272,128]{3,2,1,0:T(8,128)(2,1)S(1)}, u32[]{:S(2)}, u32[]{:S(2)}) collective-permute-start(bf16[4,2,272,128]{3,2,1,0:T(8,128)(2,1)S(1)} %pad_maximum_fusion), channel_id=1, source_target_pairs={{0,4},{4,0},{8,12},{12,8},{16,20},{20,16},{24,28},{28,24},{32,36},... | collective-permute-start | bytes 1671176 | tf_op jit(solution)/shard_map/ppermute | solution.py:159
  31.2 0.2 collective-permute-start.6
  31.4 2.6 %collective-permute-start.7 = (bf16[2,272,128]{2,1,0:T(8,128)(2,1)S(1)}, bf16[2,272,128]{2,1,0:T(8,128)(2,1)S(1)}, u32[]{:S(2)}, u32[]{:S(2)}) collective-permute-start(bf16[2,272,128]{2,1,0:T(8,128)(2,1)S(1)} %get-tuple-element.70), channel_id=1, source_target_pairs={{0,24},{4,28},{8,0},{12,4},{16,8},{20,12},{24,16},{28,20},{32,56},... | collective-permute-start | bytes 417800 | tf_op jit(solution)/shard_map/ppermute | solution.py:159
  33.9 0.3 collective-permute-start.8
  34.3 3.0 %collective-permute-start.9 = (bf16[1,272,128]{2,1,0:T(8,128)(2,1)S(1)}, bf16[1,272,128]{2,1,0:T(8,128)(2,1)S(1)}, u32[]{:S(2)}, u32[]{:S(2)}) collective-permute-start(bf16[1,272,128]{2,1,0:T(8,128)(2,1)S(1)} %get-tuple-element.67), channel_id=1, source_target_pairs={{0,4},{4,8},{8,12},{12,16},{16,20},{20,24},{24,28},{28,32},{32,36}... | collective-permute-start | bytes 208904 | tf_op jit(solution)/shard_map/ppermute | solution.py:159
  37.2 1.7 %near_a.1 = (f32[8,1024]{1,0:T(8,128)S(1)}, f32[144,1024]{1,0:T(8,128)S(1)}) custom-call(bf16[1024,128]{1,0:T(8,128)(2,1)S(1)} %get-tuple-element.37.q_ref, bf16[1,272,128]{2,1,0:T(8,128)(2,1)S(1)} %copy-done.1, f32[8,1024]{1,0:T(8,128)S(1)} %get-tuple-element.41.m_in, f32[144,1024]{1,0:T(8,128)S(1)} %get-tuple-element.42.acc_in, ...), custom_call_target="tpu_custom_call" | custom-call | flops 17179869184 | bytes 524288 | tf_op jit(solution)/shard_map/near_a/pallas_call | solution.py:181
  39.0 1.7 %far_a.1 = (f32[8,1024]{1,0:T(8,128)S(1)}, f32[144,1024]{1,0:T(8,128)S(1)}) custom-call(bf16[1024,128]{1,0:T(8,128)(2,1)S(1)} %get-tuple-element.37.q_ref, bf16[1,272,128]{2,1,0:T(8,128)(2,1)S(1)} %copy-done.1, f32[8,1024]{1,0:T(8,128)S(1)} %get-tuple-element.47.m_in, f32[144,1024]{1,0:T(8,128)S(1)} %get-tuple-element.48.acc_in, ...), custom_call_target="tpu_custom_call" | custom-call | flops 17179869184 | bytes 524288 | tf_op jit(solution)/shard_map/far_a/pallas_call | solution.py:181
  40.7 0.1 pad_maximum_fusion.1
  40.8 1.8 %collective-permute-start.11 = (bf16[4,2,272,128]{3,2,1,0:T(8,128)(2,1)S(1)}, bf16[4,2,272,128]{3,2,1,0:T(8,128)(2,1)S(1)}, u32[]{:S(2)}, u32[]{:S(2)}) collective-permute-start(bf16[4,2,272,128]{3,2,1,0:T(8,128)(2,1)S(1)} %pad_maximum_fusion.1), channel_id=1, source_target_pairs={{0,4},{4,0},{8,12},{12,8},{16,20},{20,16},{24,28},{28,24},{32,36},... | collective-permute-start | bytes 1671176 | tf_op jit(solution)/shard_map/ppermute | solution.py:159
  42.6 1.7 %near_b.1 = (f32[8,1024]{1,0:T(8,128)S(1)}, f32[144,1024]{1,0:T(8,128)S(1)}) custom-call(bf16[1024,128]{1,0:T(8,128)(2,1)S(1)} %get-tuple-element.37.q_ref, bf16[1,272,128]{2,1,0:T(8,128)(2,1)S(1)} %copy-done.1, f32[8,1024]{1,0:T(8,128)S(1)} %get-tuple-element.51.m_in, f32[144,1024]{1,0:T(8,128)S(1)} %get-tuple-element.52.acc_in, ...), custom_call_target="tpu_custom_call" | custom-call | flops 17179869184 | bytes 524288 | tf_op jit(solution)/shard_map/near_b/pallas_call | solution.py:181
  44.4 2.0 %last.1.att_ref = bf16[128,1024]{1,0:T(8,128)(2,1)S(1)} custom-call(bf16[1024,128]{1,0:T(8,128)(2,1)S(1)} %get-tuple-element.37.q_ref, bf16[1,272,128]{2,1,0:T(8,128)(2,1)S(1)} %copy-done.1, f32[8,1024]{1,0:T(8,128)S(1)} %get-tuple-element.56.m_in, f32[144,1024]{1,0:T(8,128)S(1)} %get-tuple-element.57.acc_in, ...), custom_call_target="tpu_custom_call" | custom-call | flops 19327352832 | bytes 589824 | tf_op jit(solution)/shard_map/last/pallas_call | solution.py:225
  46.4 0.3 slice-done.1
  46.7 1.3 %project.1 = (bf16[128,1024]{1,0:T(8,128)(2,1)S(1)}, bf16[128,1024]{1,0:T(8,128)(2,1)S(1)}, bf16[128,1024]{1,0:T(8,128)(2,1)S(1)}, f32[128,1024]{1,0:T(8,128)S(1)}) custom-call(s32[1]{0:T(128)} %bitcast.lane_ref, bf16[128,1024]{1,0:T(8,128)(2,1)S(1)} %last.1.att_ref, bf16[1024,4096]{1,0:T(8,128)(2,1)S(1)} %bitcast.12), custom_call_target="tpu_custom_call" | custom-call | flops 1073741824 | bytes 8388608 | tf_op jit(solution)/shard_map/project/pallas_call | solution.py:238
  47.9 3.0 %collective-permute-start.12 = (bf16[128,1024]{1,0:T(8,128)(2,1)S(1)}, bf16[128,1024]{1,0:T(8,128)(2,1)S(1)}, u32[]{:S(2)}, u32[]{:S(2)}) collective-permute-start(bf16[128,1024]{1,0:T(8,128)(2,1)S(1)} %get-tuple-element.60), channel_id=1, source_target_pairs={{0,2},{1,3},{2,0},{3,1},{4,6},{5,7},{6,4},{7,5},{8,10},{9,11},{10,... | collective-permute-start | bytes 786440 | tf_op jit(solution)/shard_map/ppermute | solution.py:253
  50.9 0.4 collective-permute-start.13
  51.3 0.4 collective-permute-start.14
  51.7 5.6 %collective-permute-done.12 = bf16[128,1024]{1,0:T(8,128)(2,1)S(1)} collective-permute-done((bf16[128,1024]{1,0:T(8,128)(2,1)S(1)}, bf16[128,1024]{1,0:T(8,128)(2,1)S(1)}, u32[]{:S(2)}, u32[]{:S(2)}) %collective-permute-start.12) | collective-permute-done | bytes 262176 | tf_op jit(solution)/shard_map/ppermute | solution.py:253
  57.3 6.0 %collective-permute-done.13 = bf16[128,1024]{1,0:T(8,128)(2,1)S(1)} collective-permute-done((bf16[128,1024]{1,0:T(8,128)(2,1)S(1)}, bf16[128,1024]{1,0:T(8,128)(2,1)S(1)}, u32[]{:S(2)}, u32[]{:S(2)}) %collective-permute-start.13) | collective-permute-done | bytes 262176 | tf_op jit(solution)/shard_map/ppermute | solution.py:253
  63.3 0.1 collective-permute-done.14
  63.4 0.9 %add_convert_fusion = bf16[128,1024]{1,0:T(8,128)(2,1)} fusion(bf16[128,1024]{1,0:T(8,128)(2,1)S(1)} %collective-permute-done.14, bf16[128,1024]{1,0:T(8,128)(2,1)S(1)} %collective-permute-done.13, f32[128,1024]{1,0:T(8,128)S(1)} %get-tuple-element.59, bf16[128,1024]{1,0:T(8,128)(2,1)S(1)} %collective-permute-done.12), kind=kLoop, calls=%fused_computation.2 | loop fusion | flops 917504 | bytes 1572864 | tf_op jit(solution)/shard_map/convert_element_type | solution.py:260
  (23 shorter events, 0.2 us)
Async XLA Ops:
  1.5 11.6 %collective-permute-start = (bf16[1,272,128]{2,1,0:T(8,128)(2,1)}, bf16[1,272,128]{2,1,0:T(8,128)(2,1)S(1)}, u32[]{:S(2)}, u32[]{:S(2)}) collective-permute-start(bf16[1,272,128]{2,1,0:T(8,128)(2,1)} %pack.1.own_ref), channel_id=1, source_target_pairs={{0,64},{4,68},{8,72},{12,76},{16,80},{20,84},{24,88},{28,92},{32,9... | collective-permute-start | bytes 208904 | tf_op jit(solution)/shard_map/ppermute | solution.py:159
  7.3 5.9 %collective-permute-start.1 = (bf16[1,272,128]{2,1,0:T(8,128)(2,1)}, bf16[1,272,128]{2,1,0:T(8,128)(2,1)S(1)}, u32[]{:S(2)}, u32[]{:S(2)}) collective-permute-start(bf16[1,272,128]{2,1,0:T(8,128)(2,1)} %pack.1.own_ref), channel_id=1, source_target_pairs={{0,32},{4,36},{8,40},{12,44},{16,48},{20,52},{24,56},{28,60},{32,6... | collective-permute-start | bytes 208904 | tf_op jit(solution)/shard_map/ppermute | solution.py:159
  10.8 0.9 %copy-start = (bf16[1,272,128]{2,1,0:T(8,128)(2,1)S(1)}, bf16[1,272,128]{2,1,0:T(8,128)(2,1)}, u32[]{:S(2)}) copy-start(bf16[1,272,128]{2,1,0:T(8,128)(2,1)} %pack.1.own_ref) | copy-start | bytes 208900
  11.7 0.9 %copy-start.2 = (bf16[128,1024]{1,0:T(8,128)(2,1)S(1)}, bf16[128,1024]{1,0:T(8,128)(2,1)}, u32[]{:S(2)}) copy-start(bf16[128,1024]{1,0:T(8,128)(2,1)} %q_ref.1) | copy-start | bytes 786436
  12.7 18.4 %copy-start.1 = (bf16[1,272,128]{2,1,0:T(8,128)(2,1)S(1)}, bf16[1,272,128]{2,1,0:T(8,128)(2,1)}, u32[]{:S(2)}) copy-start(bf16[1,272,128]{2,1,0:T(8,128)(2,1)} %pack.1.own_ref) | copy-start | bytes 208900
  13.2 9.7 %collective-permute-start.2 = (bf16[2,272,128]{2,1,0:T(8,128)(2,1)S(1)}, bf16[2,272,128]{2,1,0:T(8,128)(2,1)S(1)}, u32[]{:S(2)}, u32[]{:S(2)}) collective-permute-start(bf16[2,272,128]{2,1,0:T(8,128)(2,1)S(1)} %constant_dynamic-update-slice_fusion.rest_0_), channel_id=1, source_target_pairs={{0,64},{4,68},{8,72},{12,76},{16,80},{20,84},{24,88},{28,92},{32,9... | collective-permute-start | bytes 417800 | tf_op jit(solution)/shard_map/ppermute | solution.py:159
  18.7 5.2 %collective-permute-start.3 = (bf16[2,272,128]{2,1,0:T(8,128)(2,1)S(1)}, bf16[2,272,128]{2,1,0:T(8,128)(2,1)S(1)}, u32[]{:S(2)}, u32[]{:S(2)}) collective-permute-start(bf16[2,272,128]{2,1,0:T(8,128)(2,1)S(1)} %constant_dynamic-update-slice_fusion.rest_0_), channel_id=1, source_target_pairs={{0,8},{4,12},{8,16},{12,20},{16,24},{20,28},{24,0},{28,4},{32,40},... | collective-permute-start | bytes 417800 | tf_op jit(solution)/shard_map/ppermute | solution.py:159
  20.0 3.9 %collective-permute-start.4 = (bf16[2,272,128]{2,1,0:T(8,128)(2,1)S(1)}, bf16[2,272,128]{2,1,0:T(8,128)(2,1)S(1)}, u32[]{:S(2)}, u32[]{:S(2)}) collective-permute-start(bf16[2,272,128]{2,1,0:T(8,128)(2,1)S(1)} %constant_dynamic-update-slice_fusion.rest_0_), channel_id=1, source_target_pairs={{0,24},{4,28},{8,0},{12,4},{16,8},{20,12},{24,16},{28,20},{32,56},... | collective-permute-start | bytes 417800 | tf_op jit(solution)/shard_map/ppermute | solution.py:159
  21.4 6.1 %collective-permute-start.5 = (bf16[2,272,128]{2,1,0:T(8,128)(2,1)S(1)}, bf16[2,272,128]{2,1,0:T(8,128)(2,1)S(1)}, u32[]{:S(2)}, u32[]{:S(2)}) collective-permute-start(bf16[2,272,128]{2,1,0:T(8,128)(2,1)S(1)} %constant_dynamic-update-slice_fusion.rest_0_), channel_id=1, source_target_pairs={{0,16},{4,20},{8,24},{12,28},{16,0},{20,4},{24,8},{28,12},{32,48},... | collective-permute-start | bytes 417800 | tf_op jit(solution)/shard_map/ppermute | solution.py:159
  27.6 11.4 %collective-permute-start.10 = (bf16[4,2,272,128]{3,2,1,0:T(8,128)(2,1)S(1)}, bf16[4,2,272,128]{3,2,1,0:T(8,128)(2,1)S(1)}, u32[]{:S(2)}, u32[]{:S(2)}) collective-permute-start(bf16[4,2,272,128]{3,2,1,0:T(8,128)(2,1)S(1)} %pad_maximum_fusion), channel_id=1, source_target_pairs={{0,4},{4,0},{8,12},{12,8},{16,20},{20,16},{24,28},{28,24},{32,36},... | collective-permute-start | bytes 1671176 | tf_op jit(solution)/shard_map/ppermute | solution.py:159
  31.2 9.5 %collective-permute-start.6 = (bf16[2,272,128]{2,1,0:T(8,128)(2,1)S(1)}, bf16[2,272,128]{2,1,0:T(8,128)(2,1)S(1)}, u32[]{:S(2)}, u32[]{:S(2)}) collective-permute-start(bf16[2,272,128]{2,1,0:T(8,128)(2,1)S(1)} %get-tuple-element.72), channel_id=1, source_target_pairs={{0,8},{4,12},{8,16},{12,20},{16,24},{20,28},{24,0},{28,4},{32,40},... | collective-permute-start | bytes 417800 | tf_op jit(solution)/shard_map/ppermute | solution.py:159
  31.4 9.3 %collective-permute-start.7 = (bf16[2,272,128]{2,1,0:T(8,128)(2,1)S(1)}, bf16[2,272,128]{2,1,0:T(8,128)(2,1)S(1)}, u32[]{:S(2)}, u32[]{:S(2)}) collective-permute-start(bf16[2,272,128]{2,1,0:T(8,128)(2,1)S(1)} %get-tuple-element.70), channel_id=1, source_target_pairs={{0,24},{4,28},{8,0},{12,4},{16,8},{20,12},{24,16},{28,20},{32,56},... | collective-permute-start | bytes 417800 | tf_op jit(solution)/shard_map/ppermute | solution.py:159
  33.9 6.8 %collective-permute-start.8 = (bf16[2,272,128]{2,1,0:T(8,128)(2,1)S(1)}, bf16[2,272,128]{2,1,0:T(8,128)(2,1)S(1)}, u32[]{:S(2)}, u32[]{:S(2)}) collective-permute-start(bf16[2,272,128]{2,1,0:T(8,128)(2,1)S(1)} %get-tuple-element.71), channel_id=1, source_target_pairs={{0,16},{4,20},{8,24},{12,28},{16,0},{20,4},{24,8},{28,12},{32,48},... | collective-permute-start | bytes 417800 | tf_op jit(solution)/shard_map/ppermute | solution.py:159
  34.3 6.4 %collective-permute-start.9 = (bf16[1,272,128]{2,1,0:T(8,128)(2,1)S(1)}, bf16[1,272,128]{2,1,0:T(8,128)(2,1)S(1)}, u32[]{:S(2)}, u32[]{:S(2)}) collective-permute-start(bf16[1,272,128]{2,1,0:T(8,128)(2,1)S(1)} %get-tuple-element.67), channel_id=1, source_target_pairs={{0,4},{4,8},{8,12},{12,16},{16,20},{20,24},{24,28},{28,32},{32,36}... | collective-permute-start | bytes 208904 | tf_op jit(solution)/shard_map/ppermute | solution.py:159
  40.8 3.5 %collective-permute-start.11 = (bf16[4,2,272,128]{3,2,1,0:T(8,128)(2,1)S(1)}, bf16[4,2,272,128]{3,2,1,0:T(8,128)(2,1)S(1)}, u32[]{:S(2)}, u32[]{:S(2)}) collective-permute-start(bf16[4,2,272,128]{3,2,1,0:T(8,128)(2,1)S(1)} %pad_maximum_fusion.1), channel_id=1, source_target_pairs={{0,4},{4,0},{8,12},{12,8},{16,20},{20,16},{24,28},{28,24},{32,36},... | collective-permute-start | bytes 1671176 | tf_op jit(solution)/shard_map/ppermute | solution.py:159
  42.6 3.7 %slice-start = ((s8[8388608]{0:T(1024)(128)(4,1)}), s8[4194304]{0:T(1024)(128)(4,1)S(1)}, s32[]{:S(2)}) async-start(s8[8388608]{0:T(1024)(128)(4,1)} %bitcast.11), calls=%async_computation | async-start | bytes 8388608
  44.4 2.3 %slice-start.1 = ((s8[8388608]{0:T(1024)(128)(4,1)}), s8[4194304]{0:T(1024)(128)(4,1)S(1)}, s32[]{:S(2)}) async-start(s8[8388608]{0:T(1024)(128)(4,1)} %bitcast.11), calls=%async_computation.1 | async-start | bytes 8388608
  47.9 9.4 %collective-permute-start.12 = (bf16[128,1024]{1,0:T(8,128)(2,1)S(1)}, bf16[128,1024]{1,0:T(8,128)(2,1)S(1)}, u32[]{:S(2)}, u32[]{:S(2)}) collective-permute-start(bf16[128,1024]{1,0:T(8,128)(2,1)S(1)} %get-tuple-element.60), channel_id=1, source_target_pairs={{0,2},{1,3},{2,0},{3,1},{4,6},{5,7},{6,4},{7,5},{8,10},{9,11},{10,... | collective-permute-start | bytes 786440 | tf_op jit(solution)/shard_map/ppermute | solution.py:253
  50.9 12.3 %collective-permute-start.13 = (bf16[128,1024]{1,0:T(8,128)(2,1)S(1)}, bf16[128,1024]{1,0:T(8,128)(2,1)S(1)}, u32[]{:S(2)}, u32[]{:S(2)}) collective-permute-start(bf16[128,1024]{1,0:T(8,128)(2,1)S(1)} %get-tuple-element.61), channel_id=1, source_target_pairs={{0,1},{1,0},{2,3},{3,2},{4,5},{5,4},{6,7},{7,6},{8,9},{9,8},{10,11... | collective-permute-start | bytes 786440 | tf_op jit(solution)/shard_map/ppermute | solution.py:253
  51.3 12.0 %collective-permute-start.14 = (bf16[128,1024]{1,0:T(8,128)(2,1)S(1)}, bf16[128,1024]{1,0:T(8,128)(2,1)S(1)}, u32[]{:S(2)}, u32[]{:S(2)}) collective-permute-start(bf16[128,1024]{1,0:T(8,128)(2,1)S(1)} %get-tuple-element.62), channel_id=1, source_target_pairs={{0,3},{1,2},{2,1},{3,0},{4,7},{5,6},{6,5},{7,4},{8,11},{9,10},{10,... | collective-permute-start | bytes 786440 | tf_op jit(solution)/shard_map/ppermute | solution.py:253

commit v4 on v3

--- a/solution.py
+++ b/solution.py
@@ -24,7 +24,7 @@
 
 
 def shift_z(size, planes):
-    return ctx_pairs(size, lambda i: i + 8 * planes)
+    return ctx_pairs(size, lambda i: (i + 8 * planes) % size)
 
 
 def shift_x(size, steps):
@@ -153,7 +153,7 @@
     rows = tokens * (queries.shape[1] // HEAD_DIM)
     index = lax.axis_index("ctx")
     lane = lax.axis_index("tp")
-    x, c = index % 8 // 2, index % 2
+    z, x, c = index // 8, index % 8 // 2, index % 2
 
     def send(value, pairs):
         return lax.ppermute(value, "ctx", pairs)
@@ -203,7 +203,11 @@
     p12 = jnp.concatenate([p1, p2], 0)
 
     near_a = [p12] + [send(p12, shift_x(size, k)) for k in (2, 1, 3)]
-    p34 = send(p12, shift_z(size, 2))
+    onward = z < size // 8 - 2
+    p12_on = jnp.concatenate(
+        [jnp.where(onward & (z >= 1), p1, 0), jnp.where(onward & (z >= 2), p2, 0)], 0
+    )
+    p34 = send(p12_on, shift_z(size, 2))
     p34, near_a[2], near_a[3], near_a[1], near_a[0] = lax.optimization_barrier(
         (p34, near_a[2], near_a[3], near_a[1], near_a[0])
     )
@@ -211,9 +215,9 @@
     def with_either(first):
         return jnp.concatenate([p34[0:1], jnp.where(first, own, p34[1:2])], 0)
 
+    side_b = [send(with_either(x + k < 4), shift_x(size, k)) for k in (2, 1, 3)]
+    beyond = send(p34[1:2], [(i, i + 1) for i in range(32, size - 1)])
     far_a = send(jnp.stack(near_a), swap_core(size))
-    side_b = [send(with_either(x + k < 4), shift_x(size, k)) for k in (2, 1, 3)]
-    beyond = send(p34[1:2], ctx_pairs(size, lambda i: i + 1))
     state = attend("near_a", state, 8, near_a)
     state = attend("far_a", state, 8, [far_a])
     side_b[1], side_b[2], side_b[0], beyond, state = lax.optimization_barrier(

time: 64.6 us -> 58.7 us (0.909)
  starting transfers between devices: 34.2 us -> 21.1 us
  waiting for transfers between devices: 16.2 us -> 23.3 us
    ppermute x12, starting transfers between devices: 30.4 us -> 17.3 us  [send(): return lax.ppermute(value, 'ctx', pairs)]
    ppermute x12, waiting for transfers between devices: 4.55 us -> 11.7 us  [send(): return lax.ppermute(value, 'ctx', pairs)]
    unnamed x11 -> x10, local copies, waits for them, and re-layouts: 2.15 us -> 2.18 us
  transfers between devices with their start and end apart: 15 -> 15, of which waited for: 5 -> 8; matrix products, arithmetic and copies ran while one was open for 0% -> 0% of each run, Pallas kernels for 9% -> 10%
where the time goes in v4:
time: 58.7 us; the launch traced here: 58.3 us
  waiting for transfers between devices  23.3 us (40%)
  starting transfers between devices  21.1 us (36%)
  Pallas kernels  10.3 us (18%)
  local copies, waits for them, and re-layouts  2.18 us (4%)
  other arithmetic  1.14 us (2%)
    ppermute x12, starting transfers between devices, send(): return lax.ppermute(value, 'ctx', pairs)  17.3 us
    ppermute x12, waiting for transfers between devices, send(): return lax.ppermute(value, 'ctx', pairs)  11.7 us
    ppermute x3, waiting for transfers between devices, pass_on(): return lax.ppermute(part, 'tp', [(i, i ^ k) for i in range(4)])  11.6 us
    pallas_call x3, Pallas kernels, attend(): pl.pallas_call(group_kernel, out_shape=state_shape, in_specs=[VMEM] * (4...  5.09 us
    ppermute x3, starting transfers between devices, pass_on(): return lax.ppermute(part, 'tp', [(i, i ^ k) for i in range(4)])  3.78 us
    unnamed x10, local copies, waits for them, and re-layouts  2.18 us
    pallas_call x1, Pallas kernels, on_device(): pl.pallas_call(last_kernel, out_shape=jax.ShapeDtypeStruct(queries.shape,...  1.98 us
    pallas_call x1, Pallas kernels, on_device(): pl.pallas_call(pack_kernel, out_shape=jax.ShapeDtypeStruct((1, 272, 128),...  1.53 us
  transfers between devices with their start and end apart: 15, of which 8 were waited for; matrix products, arithmetic and copies ran while one was open for 0% of the time, Pallas kernels for 10%

profile of v4, /device:TPU:1, one launch (start us, length us, event | category | flops | bytes accessed | tf_op | source)
XLA Modules:
  0.0 58.3 jit_solution(12160143456265713529)
XLA Ops:
  0.0 1.5 %pack.1.own_ref = bf16[1,272,128]{2,1,0:T(8,128)(2,1)} custom-call(bf16[128,128]{1,0:T(8,128)(2,1)} %k_ref.1, bf16[128,128]{1,0:T(8,128)(2,1)} %v_ref.1, s32[1,128]{1,0:T(1,128)} %bitcast.20), custom_call_target="tpu_custom_call" | custom-call | tf_op jit(solution)/shard_map/pack/pallas_call | solution.py:161
  1.5 3.9 %collective-permute-start = (bf16[1,272,128]{2,1,0:T(8,128)(2,1)}, bf16[1,272,128]{2,1,0:T(8,128)(2,1)S(1)}, u32[]{:S(2)}, u32[]{:S(2)}) collective-permute-start(bf16[1,272,128]{2,1,0:T(8,128)(2,1)} %pack.1.own_ref), channel_id=1, source_target_pairs={{0,64},{4,68},{8,72},{12,76},{16,80},{20,84},{24,88},{28,92},{32,9... | collective-permute-start | bytes 208904 | tf_op jit(solution)/shard_map/ppermute | solution.py:159
  5.4 1.6 %collective-permute-start.1 = (bf16[1,272,128]{2,1,0:T(8,128)(2,1)}, bf16[1,272,128]{2,1,0:T(8,128)(2,1)S(1)}, u32[]{:S(2)}, u32[]{:S(2)}) collective-permute-start(bf16[1,272,128]{2,1,0:T(8,128)(2,1)} %pack.1.own_ref), channel_id=1, source_target_pairs={{0,32},{4,36},{8,40},{12,44},{16,48},{20,52},{24,56},{28,60},{32,6... | collective-permute-start | bytes 208904 | tf_op jit(solution)/shard_map/ppermute | solution.py:159
  7.1 0.9 %copy-done = bf16[1,272,128]{2,1,0:T(8,128)(2,1)S(1)} copy-done((bf16[1,272,128]{2,1,0:T(8,128)(2,1)S(1)}, bf16[1,272,128]{2,1,0:T(8,128)(2,1)}, u32[]{:S(2)}) %copy-start) | copy-done | bytes 69656
  8.0 0.9 %copy-done.2 = bf16[128,1024]{1,0:T(8,128)(2,1)S(1)} copy-done((bf16[128,1024]{1,0:T(8,128)(2,1)S(1)}, bf16[128,1024]{1,0:T(8,128)(2,1)}, u32[]{:S(2)}) %copy-start.2) | copy-done | bytes 262168
  8.9 0.5 own.1
  9.5 1.0 %collective-permute-done = bf16[1,272,128]{2,1,0:T(8,128)(2,1)S(1)} collective-permute-done((bf16[1,272,128]{2,1,0:T(8,128)(2,1)}, bf16[1,272,128]{2,1,0:T(8,128)(2,1)S(1)}, u32[]{:S(2)}, u32[]{:S(2)}) %collective-permute-start) | collective-permute-done | bytes 69664 | tf_op jit(solution)/shard_map/ppermute | solution.py:159
  10.5 3.0 %collective-permute-done.1 = bf16[1,272,128]{2,1,0:T(8,128)(2,1)S(1)} collective-permute-done((bf16[1,272,128]{2,1,0:T(8,128)(2,1)}, bf16[1,272,128]{2,1,0:T(8,128)(2,1)S(1)}, u32[]{:S(2)}, u32[]{:S(2)}) %collective-permute-start.1) | collective-permute-done | bytes 69664 | tf_op jit(solution)/shard_map/ppermute | solution.py:159
  13.5 0.6 %collective-permute-start.2 = (bf16[2,272,128]{2,1,0:T(8,128)(2,1)S(1)}, bf16[2,272,128]{2,1,0:T(8,128)(2,1)S(1)}, u32[]{:S(2)}, u32[]{:S(2)}) collective-permute-start(bf16[2,272,128]{2,1,0:T(8,128)(2,1)S(1)} %pad_maximum_fusion.6), channel_id=1, source_target_pairs={{0,64},{4,68},{8,72},{12,76},{16,80},{20,84},{24,88},{28,92},{32,9... | collective-permute-start | bytes 417800 | tf_op jit(solution)/shard_map/ppermute | solution.py:159
  14.1 1.2 %collective-permute-start.3 = (bf16[2,272,128]{2,1,0:T(8,128)(2,1)S(1)}, bf16[2,272,128]{2,1,0:T(8,128)(2,1)S(1)}, u32[]{:S(2)}, u32[]{:S(2)}) collective-permute-start(bf16[2,272,128]{2,1,0:T(8,128)(2,1)S(1)} %get-tuple-element.43.rest_0_), channel_id=1, source_target_pairs={{0,8},{4,12},{8,16},{12,20},{16,24},{20,28},{24,0},{28,4},{32,40},... | collective-permute-start | bytes 417800 | tf_op jit(solution)/shard_map/ppermute | solution.py:159
  15.3 1.5 %collective-permute-start.4 = (bf16[2,272,128]{2,1,0:T(8,128)(2,1)S(1)}, bf16[2,272,128]{2,1,0:T(8,128)(2,1)S(1)}, u32[]{:S(2)}, u32[]{:S(2)}) collective-permute-start(bf16[2,272,128]{2,1,0:T(8,128)(2,1)S(1)} %get-tuple-element.43.rest_0_), channel_id=1, source_target_pairs={{0,24},{4,28},{8,0},{12,4},{16,8},{20,12},{24,16},{28,20},{32,56},... | collective-permute-start | bytes 417800 | tf_op jit(solution)/shard_map/ppermute | solution.py:159
  16.8 1.5 %collective-permute-start.5 = (bf16[2,272,128]{2,1,0:T(8,128)(2,1)S(1)}, bf16[2,272,128]{2,1,0:T(8,128)(2,1)S(1)}, u32[]{:S(2)}, u32[]{:S(2)}) collective-permute-start(bf16[2,272,128]{2,1,0:T(8,128)(2,1)S(1)} %get-tuple-element.43.rest_0_), channel_id=1, source_target_pairs={{0,16},{4,20},{8,24},{12,28},{16,0},{20,4},{24,8},{28,12},{32,48},... | collective-permute-start | bytes 417800 | tf_op jit(solution)/shard_map/ppermute | solution.py:159
  18.3 3.4 %collective-permute-done.2.rest_0_ = bf16[2,272,128]{2,1,0:T(8,128)(2,1)S(1)} collective-permute-done((bf16[2,272,128]{2,1,0:T(8,128)(2,1)S(1)}, bf16[2,272,128]{2,1,0:T(8,128)(2,1)S(1)}, u32[]{:S(2)}, u32[]{:S(2)}) %collective-permute-start.2) | collective-permute-done | bytes 139296 | tf_op jit(solution)/shard_map/ppermute | solution.py:159
  21.7 2.3 %collective-permute-done.5.rest_1_ = bf16[2,272,128]{2,1,0:T(8,128)(2,1)S(1)} collective-permute-done((bf16[2,272,128]{2,1,0:T(8,128)(2,1)S(1)}, bf16[2,272,128]{2,1,0:T(8,128)(2,1)S(1)}, u32[]{:S(2)}, u32[]{:S(2)}) %collective-permute-start.5) | collective-permute-done | bytes 139296 | tf_op jit(solution)/shard_map/ppermute | solution.py:159
  24.1 1.9 %collective-permute-start.10 = (bf16[4,2,272,128]{3,2,1,0:T(8,128)(2,1)S(1)}, bf16[4,2,272,128]{3,2,1,0:T(8,128)(2,1)S(1)}, u32[]{:S(2)}, u32[]{:S(2)}) collective-permute-start(bf16[4,2,272,128]{3,2,1,0:T(8,128)(2,1)S(1)} %pad_maximum_fusion), channel_id=1, source_target_pairs={{0,4},{4,0},{8,12},{12,8},{16,20},{20,16},{24,28},{28,24},{32,36},... | collective-permute-start | bytes 1671176 | tf_op jit(solution)/shard_map/ppermute | solution.py:159
  26.1 0.5 collective-permute-start.6
  26.6 2.2 %collective-permute-start.7 = (bf16[2,272,128]{2,1,0:T(8,128)(2,1)S(1)}, bf16[2,272,128]{2,1,0:T(8,128)(2,1)S(1)}, u32[]{:S(2)}, u32[]{:S(2)}) collective-permute-start(bf16[2,272,128]{2,1,0:T(8,128)(2,1)S(1)} %get-tuple-element.70), channel_id=1, source_target_pairs={{0,24},{4,28},{8,0},{12,4},{16,8},{20,12},{24,16},{28,20},{32,56},... | collective-permute-start | bytes 417800 | tf_op jit(solution)/shard_map/ppermute | solution.py:159
  28.8 0.7 %collective-permute-start.9 = (bf16[1,272,128]{2,1,0:T(8,128)(2,1)S(1)}, bf16[1,272,128]{2,1,0:T(8,128)(2,1)S(1)}, u32[]{:S(2)}, u32[]{:S(2)}) collective-permute-start(bf16[1,272,128]{2,1,0:T(8,128)(2,1)S(1)} %get-tuple-element.67), channel_id=1, source_target_pairs={{128,132},{132,136},{136,140},{140,144},{144,148},{148,152},{152,1... | collective-permute-start | bytes 208904 | tf_op jit(solution)/shard_map/ppermute | solution.py:159
  29.5 1.7 %near_a.1 = (f32[8,1024]{1,0:T(8,128)S(1)}, f32[144,1024]{1,0:T(8,128)S(1)}) custom-call(bf16[1024,128]{1,0:T(8,128)(2,1)S(1)} %get-tuple-element.37.q_ref, bf16[1,272,128]{2,1,0:T(8,128)(2,1)S(1)} %copy-done.1, f32[8,1024]{1,0:T(8,128)S(1)} %get-tuple-element.41.m_in, f32[144,1024]{1,0:T(8,128)S(1)} %get-tuple-element.42.acc_in, ...), custom_call_target="tpu_custom_call" | custom-call | flops 17179869184 | bytes 524288 | tf_op jit(solution)/shard_map/near_a/pallas_call | solution.py:181
  31.2 1.7 %far_a.1 = (f32[8,1024]{1,0:T(8,128)S(1)}, f32[144,1024]{1,0:T(8,128)S(1)}) custom-call(bf16[1024,128]{1,0:T(8,128)(2,1)S(1)} %get-tuple-element.37.q_ref, bf16[1,272,128]{2,1,0:T(8,128)(2,1)S(1)} %copy-done.1, f32[8,1024]{1,0:T(8,128)S(1)} %get-tuple-element.47.m_in, f32[144,1024]{1,0:T(8,128)S(1)} %get-tuple-element.48.acc_in, ...), custom_call_target="tpu_custom_call" | custom-call | flops 17179869184 | bytes 524288 | tf_op jit(solution)/shard_map/far_a/pallas_call | solution.py:181
  33.0 2.0 %collective-permute-done.8.rest_1_ = bf16[2,272,128]{2,1,0:T(8,128)(2,1)S(1)} collective-permute-done((bf16[2,272,128]{2,1,0:T(8,128)(2,1)S(1)}, bf16[2,272,128]{2,1,0:T(8,128)(2,1)S(1)}, u32[]{:S(2)}, u32[]{:S(2)}) %collective-permute-start.8) | collective-permute-done | bytes 139296 | tf_op jit(solution)/shard_map/ppermute | solution.py:159
  35.1 1.7 %collective-permute-start.11 = (bf16[4,2,272,128]{3,2,1,0:T(8,128)(2,1)S(1)}, bf16[4,2,272,128]{3,2,1,0:T(8,128)(2,1)S(1)}, u32[]{:S(2)}, u32[]{:S(2)}) collective-permute-start(bf16[4,2,272,128]{3,2,1,0:T(8,128)(2,1)S(1)} %pad_maximum_fusion.1), channel_id=1, source_target_pairs={{0,4},{4,0},{8,12},{12,8},{16,20},{20,16},{24,28},{28,24},{32,36},... | collective-permute-start | bytes 1671176 | tf_op jit(solution)/shard_map/ppermute | solution.py:159
  36.8 1.7 %near_b.1 = (f32[8,1024]{1,0:T(8,128)S(1)}, f32[144,1024]{1,0:T(8,128)S(1)}) custom-call(bf16[1024,128]{1,0:T(8,128)(2,1)S(1)} %get-tuple-element.37.q_ref, bf16[1,272,128]{2,1,0:T(8,128)(2,1)S(1)} %copy-done.1, f32[8,1024]{1,0:T(8,128)S(1)} %get-tuple-element.51.m_in, f32[144,1024]{1,0:T(8,128)S(1)} %get-tuple-element.52.acc_in, ...), custom_call_target="tpu_custom_call" | custom-call | flops 17179869184 | bytes 524288 | tf_op jit(solution)/shard_map/near_b/pallas_call | solution.py:181
  38.5 2.0 %last.1.att_ref = bf16[128,1024]{1,0:T(8,128)(2,1)S(1)} custom-call(bf16[1024,128]{1,0:T(8,128)(2,1)S(1)} %get-tuple-element.37.q_ref, bf16[1,272,128]{2,1,0:T(8,128)(2,1)S(1)} %copy-done.1, f32[8,1024]{1,0:T(8,128)S(1)} %get-tuple-element.56.m_in, f32[144,1024]{1,0:T(8,128)S(1)} %get-tuple-element.57.acc_in, ...), custom_call_target="tpu_custom_call" | custom-call | flops 19327352832 | bytes 589824 | tf_op jit(solution)/shard_map/last/pallas_call | solution.py:229
  40.5 0.3 slice-done.1
  40.8 1.3 %project.1 = (bf16[128,1024]{1,0:T(8,128)(2,1)S(1)}, bf16[128,1024]{1,0:T(8,128)(2,1)S(1)}, bf16[128,1024]{1,0:T(8,128)(2,1)S(1)}, f32[128,1024]{1,0:T(8,128)S(1)}) custom-call(s32[1]{0:T(128)} %bitcast.lane_ref, bf16[128,1024]{1,0:T(8,128)(2,1)S(1)} %last.1.att_ref, bf16[1024,4096]{1,0:T(8,128)(2,1)S(1)} %bitcast.12), custom_call_target="tpu_custom_call" | custom-call | flops 1073741824 | bytes 8388608 | tf_op jit(solution)/shard_map/project/pallas_call | solution.py:242
  42.0 3.0 %collective-permute-start.12 = (bf16[128,1024]{1,0:T(8,128)(2,1)S(1)}, bf16[128,1024]{1,0:T(8,128)(2,1)S(1)}, u32[]{:S(2)}, u32[]{:S(2)}) collective-permute-start(bf16[128,1024]{1,0:T(8,128)(2,1)S(1)} %get-tuple-element.60), channel_id=1, source_target_pairs={{0,2},{1,3},{2,0},{3,1},{4,6},{5,7},{6,4},{7,5},{8,10},{9,11},{10,... | collective-permute-start | bytes 786440 | tf_op jit(solution)/shard_map/ppermute | solution.py:257
  45.1 0.4 collective-permute-start.13
  45.5 0.4 collective-permute-start.14
  45.8 5.6 %collective-permute-done.12 = bf16[128,1024]{1,0:T(8,128)(2,1)S(1)} collective-permute-done((bf16[128,1024]{1,0:T(8,128)(2,1)S(1)}, bf16[128,1024]{1,0:T(8,128)(2,1)S(1)}, u32[]{:S(2)}, u32[]{:S(2)}) %collective-permute-start.12) | collective-permute-done | bytes 262176 | tf_op jit(solution)/shard_map/ppermute | solution.py:257
  51.4 6.0 %collective-permute-done.13 = bf16[128,1024]{1,0:T(8,128)(2,1)S(1)} collective-permute-done((bf16[128,1024]{1,0:T(8,128)(2,1)S(1)}, bf16[128,1024]{1,0:T(8,128)(2,1)S(1)}, u32[]{:S(2)}, u32[]{:S(2)}) %collective-permute-start.13) | collective-permute-done | bytes 262176 | tf_op jit(solution)/shard_map/ppermute | solution.py:257
  57.5 0.8 %add_convert_fusion = bf16[128,1024]{1,0:T(8,128)(2,1)} fusion(bf16[128,1024]{1,0:T(8,128)(2,1)S(1)} %collective-permute-done.14, bf16[128,1024]{1,0:T(8,128)(2,1)S(1)} %collective-permute-done.13, f32[128,1024]{1,0:T(8,128)S(1)} %get-tuple-element.59, bf16[128,1024]{1,0:T(8,128)(2,1)S(1)} %collective-permute-done.12), kind=kLoop, calls=%fused_computation.2 | loop fusion | flops 917504 | bytes 1572864 | tf_op jit(solution)/shard_map/convert_element_type | solution.py:264
  (24 shorter events, 0.5 us)
Async XLA Ops:
  1.5 8.9 %collective-permute-start = (bf16[1,272,128]{2,1,0:T(8,128)(2,1)}, bf16[1,272,128]{2,1,0:T(8,128)(2,1)S(1)}, u32[]{:S(2)}, u32[]{:S(2)}) collective-permute-start(bf16[1,272,128]{2,1,0:T(8,128)(2,1)} %pack.1.own_ref), channel_id=1, source_target_pairs={{0,64},{4,68},{8,72},{12,76},{16,80},{20,84},{24,88},{28,92},{32,9... | collective-permute-start | bytes 208904 | tf_op jit(solution)/shard_map/ppermute | solution.py:159
  5.4 8.0 %collective-permute-start.1 = (bf16[1,272,128]{2,1,0:T(8,128)(2,1)}, bf16[1,272,128]{2,1,0:T(8,128)(2,1)S(1)}, u32[]{:S(2)}, u32[]{:S(2)}) collective-permute-start(bf16[1,272,128]{2,1,0:T(8,128)(2,1)} %pack.1.own_ref), channel_id=1, source_target_pairs={{0,32},{4,36},{8,40},{12,44},{16,48},{20,52},{24,56},{28,60},{32,6... | collective-permute-start | bytes 208904 | tf_op jit(solution)/shard_map/ppermute | solution.py:159
  7.1 0.9 %copy-start = (bf16[1,272,128]{2,1,0:T(8,128)(2,1)S(1)}, bf16[1,272,128]{2,1,0:T(8,128)(2,1)}, u32[]{:S(2)}) copy-start(bf16[1,272,128]{2,1,0:T(8,128)(2,1)} %pack.1.own_ref) | copy-start | bytes 208900
  8.0 0.9 %copy-start.2 = (bf16[128,1024]{1,0:T(8,128)(2,1)S(1)}, bf16[128,1024]{1,0:T(8,128)(2,1)}, u32[]{:S(2)}) copy-start(bf16[128,1024]{1,0:T(8,128)(2,1)} %q_ref.1) | copy-start | bytes 786436
  8.9 17.0 %copy-start.1 = (bf16[1,272,128]{2,1,0:T(8,128)(2,1)S(1)}, bf16[1,272,128]{2,1,0:T(8,128)(2,1)}, u32[]{:S(2)}) copy-start(bf16[1,272,128]{2,1,0:T(8,128)(2,1)} %pack.1.own_ref) | copy-start | bytes 208900
  13.5 8.2 %collective-permute-start.2 = (bf16[2,272,128]{2,1,0:T(8,128)(2,1)S(1)}, bf16[2,272,128]{2,1,0:T(8,128)(2,1)S(1)}, u32[]{:S(2)}, u32[]{:S(2)}) collective-permute-start(bf16[2,272,128]{2,1,0:T(8,128)(2,1)S(1)} %pad_maximum_fusion.6), channel_id=1, source_target_pairs={{0,64},{4,68},{8,72},{12,76},{16,80},{20,84},{24,88},{28,92},{32,9... | collective-permute-start | bytes 417800 | tf_op jit(solution)/shard_map/ppermute | solution.py:159
  14.1 7.6 %collective-permute-start.3 = (bf16[2,272,128]{2,1,0:T(8,128)(2,1)S(1)}, bf16[2,272,128]{2,1,0:T(8,128)(2,1)S(1)}, u32[]{:S(2)}, u32[]{:S(2)}) collective-permute-start(bf16[2,272,128]{2,1,0:T(8,128)(2,1)S(1)} %get-tuple-element.43.rest_0_), channel_id=1, source_target_pairs={{0,8},{4,12},{8,16},{12,20},{16,24},{20,28},{24,0},{28,4},{32,40},... | collective-permute-start | bytes 417800 | tf_op jit(solution)/shard_map/ppermute | solution.py:159
  15.3 6.4 %collective-permute-start.4 = (bf16[2,272,128]{2,1,0:T(8,128)(2,1)S(1)}, bf16[2,272,128]{2,1,0:T(8,128)(2,1)S(1)}, u32[]{:S(2)}, u32[]{:S(2)}) collective-permute-start(bf16[2,272,128]{2,1,0:T(8,128)(2,1)S(1)} %get-tuple-element.43.rest_0_), channel_id=1, source_target_pairs={{0,24},{4,28},{8,0},{12,4},{16,8},{20,12},{24,16},{28,20},{32,56},... | collective-permute-start | bytes 417800 | tf_op jit(solution)/shard_map/ppermute | solution.py:159
  16.8 7.2 %collective-permute-start.5 = (bf16[2,272,128]{2,1,0:T(8,128)(2,1)S(1)}, bf16[2,272,128]{2,1,0:T(8,128)(2,1)S(1)}, u32[]{:S(2)}, u32[]{:S(2)}) collective-permute-start(bf16[2,272,128]{2,1,0:T(8,128)(2,1)S(1)} %get-tuple-element.43.rest_0_), channel_id=1, source_target_pairs={{0,16},{4,20},{8,24},{12,28},{16,0},{20,4},{24,8},{28,12},{32,48},... | collective-permute-start | bytes 417800 | tf_op jit(solution)/shard_map/ppermute | solution.py:159
  24.1 7.1 %collective-permute-start.10 = (bf16[4,2,272,128]{3,2,1,0:T(8,128)(2,1)S(1)}, bf16[4,2,272,128]{3,2,1,0:T(8,128)(2,1)S(1)}, u32[]{:S(2)}, u32[]{:S(2)}) collective-permute-start(bf16[4,2,272,128]{3,2,1,0:T(8,128)(2,1)S(1)} %pad_maximum_fusion), channel_id=1, source_target_pairs={{0,4},{4,0},{8,12},{12,8},{16,20},{20,16},{24,28},{28,24},{32,36},... | collective-permute-start | bytes 1671176 | tf_op jit(solution)/shard_map/ppermute | solution.py:159
  26.1 6.9 %collective-permute-start.6 = (bf16[2,272,128]{2,1,0:T(8,128)(2,1)S(1)}, bf16[2,272,128]{2,1,0:T(8,128)(2,1)S(1)}, u32[]{:S(2)}, u32[]{:S(2)}) collective-permute-start(bf16[2,272,128]{2,1,0:T(8,128)(2,1)S(1)} %get-tuple-element.72), channel_id=1, source_target_pairs={{0,8},{4,12},{8,16},{12,20},{16,24},{20,28},{24,0},{28,4},{32,40},... | collective-permute-start | bytes 417800 | tf_op jit(solution)/shard_map/ppermute | solution.py:159
  26.6 6.4 %collective-permute-start.7 = (bf16[2,272,128]{2,1,0:T(8,128)(2,1)S(1)}, bf16[2,272,128]{2,1,0:T(8,128)(2,1)S(1)}, u32[]{:S(2)}, u32[]{:S(2)}) collective-permute-start(bf16[2,272,128]{2,1,0:T(8,128)(2,1)S(1)} %get-tuple-element.70), channel_id=1, source_target_pairs={{0,24},{4,28},{8,0},{12,4},{16,8},{20,12},{24,16},{28,20},{32,56},... | collective-permute-start | bytes 417800 | tf_op jit(solution)/shard_map/ppermute | solution.py:159
  28.8 6.2 %collective-permute-start.8 = (bf16[2,272,128]{2,1,0:T(8,128)(2,1)S(1)}, bf16[2,272,128]{2,1,0:T(8,128)(2,1)S(1)}, u32[]{:S(2)}, u32[]{:S(2)}) collective-permute-start(bf16[2,272,128]{2,1,0:T(8,128)(2,1)S(1)} %get-tuple-element.71), channel_id=1, source_target_pairs={{0,16},{4,20},{8,24},{12,28},{16,0},{20,4},{24,8},{28,12},{32,48},... | collective-permute-start | bytes 417800 | tf_op jit(solution)/shard_map/ppermute | solution.py:159
  28.8 4.1 %collective-permute-start.9 = (bf16[1,272,128]{2,1,0:T(8,128)(2,1)S(1)}, bf16[1,272,128]{2,1,0:T(8,128)(2,1)S(1)}, u32[]{:S(2)}, u32[]{:S(2)}) collective-permute-start(bf16[1,272,128]{2,1,0:T(8,128)(2,1)S(1)} %get-tuple-element.67), channel_id=1, source_target_pairs={{128,132},{132,136},{136,140},{140,144},{144,148},{148,152},{152,1... | collective-permute-start | bytes 208904 | tf_op jit(solution)/shard_map/ppermute | solution.py:159
  35.1 3.4 %collective-permute-start.11 = (bf16[4,2,272,128]{3,2,1,0:T(8,128)(2,1)S(1)}, bf16[4,2,272,128]{3,2,1,0:T(8,128)(2,1)S(1)}, u32[]{:S(2)}, u32[]{:S(2)}) collective-permute-start(bf16[4,2,272,128]{3,2,1,0:T(8,128)(2,1)S(1)} %pad_maximum_fusion.1), channel_id=1, source_target_pairs={{0,4},{4,0},{8,12},{12,8},{16,20},{20,16},{24,28},{28,24},{32,36},... | collective-permute-start | bytes 1671176 | tf_op jit(solution)/shard_map/ppermute | solution.py:159
  36.8 3.7 %slice-start = ((s8[8388608]{0:T(1024)(128)(4,1)}), s8[4194304]{0:T(1024)(128)(4,1)S(1)}, s32[]{:S(2)}) async-start(s8[8388608]{0:T(1024)(128)(4,1)} %bitcast.11), calls=%async_computation | async-start | bytes 8388608
  38.5 2.3 %slice-start.1 = ((s8[8388608]{0:T(1024)(128)(4,1)}), s8[4194304]{0:T(1024)(128)(4,1)S(1)}, s32[]{:S(2)}) async-start(s8[8388608]{0:T(1024)(128)(4,1)} %bitcast.11), calls=%async_computation.1 | async-start | bytes 8388608
  42.0 9.4 %collective-permute-start.12 = (bf16[128,1024]{1,0:T(8,128)(2,1)S(1)}, bf16[128,1024]{1,0:T(8,128)(2,1)S(1)}, u32[]{:S(2)}, u32[]{:S(2)}) collective-permute-start(bf16[128,1024]{1,0:T(8,128)(2,1)S(1)} %get-tuple-element.60), channel_id=1, source_target_pairs={{0,2},{1,3},{2,0},{3,1},{4,6},{5,7},{6,4},{7,5},{8,10},{9,11},{10,... | collective-permute-start | bytes 786440 | tf_op jit(solution)/shard_map/ppermute | solution.py:257
  45.1 12.3 %collective-permute-start.13 = (bf16[128,1024]{1,0:T(8,128)(2,1)S(1)}, bf16[128,1024]{1,0:T(8,128)(2,1)S(1)}, u32[]{:S(2)}, u32[]{:S(2)}) collective-permute-start(bf16[128,1024]{1,0:T(8,128)(2,1)S(1)} %get-tuple-element.61), channel_id=1, source_target_pairs={{0,1},{1,0},{2,3},{3,2},{4,5},{5,4},{6,7},{7,6},{8,9},{9,8},{10,11... | collective-permute-start | bytes 786440 | tf_op jit(solution)/shard_map/ppermute | solution.py:257
  45.5 12.0 %collective-permute-start.14 = (bf16[128,1024]{1,0:T(8,128)(2,1)S(1)}, bf16[128,1024]{1,0:T(8,128)(2,1)S(1)}, u32[]{:S(2)}, u32[]{:S(2)}) collective-permute-start(bf16[128,1024]{1,0:T(8,128)(2,1)S(1)} %get-tuple-element.62), channel_id=1, source_target_pairs={{0,3},{1,2},{2,1},{3,0},{4,7},{5,6},{6,5},{7,4},{8,11},{9,10},{10,... | collective-permute-start | bytes 786440 | tf_op jit(solution)/shard_map/ppermute | solution.py:257

commit v5 on v4

--- a/solution.py
+++ b/solution.py
@@ -188,8 +188,8 @@
             name=name,
         )(heads, own, *state, *operands)
 
+    p1 = send(own, shift_z(size, 1))
     p2 = send(own, shift_z(size, 2))
-    p1 = send(own, shift_z(size, 1))
     *state, heads = pl.pallas_call(
         own_kernel,
         out_shape=(*state_shape, jax.ShapeDtypeStruct((rows, HEAD_DIM), queries.dtype)),
@@ -199,7 +199,7 @@
         cost_estimate=cost(1, rows),
         name="own",
     )(queries, own)
-    p2, p1, state, heads = lax.optimization_barrier((p2, p1, state, heads))
+    p1, p2, state, heads = lax.optimization_barrier((p1, p2, state, heads))
     p12 = jnp.concatenate([p1, p2], 0)
 
     near_a = [p12] + [send(p12, shift_x(size, k)) for k in (2, 1, 3)]
@@ -219,13 +219,13 @@
     beyond = send(p34[1:2], [(i, i + 1) for i in range(32, size - 1)])
     far_a = send(jnp.stack(near_a), swap_core(size))
     state = attend("near_a", state, 8, near_a)
-    state = attend("far_a", state, 8, [far_a])
+    state = attend("far_a", state, 10, [far_a, p34])
     side_b[1], side_b[2], side_b[0], beyond, state = lax.optimization_barrier(
         (side_b[1], side_b[2], side_b[0], beyond, state)
     )
 
     far_b = send(jnp.stack([with_either(c == 0), *side_b]), swap_core(size))
-    state = attend("near_b", state, 8, [p34, *side_b])
+    state = attend("near_b", state, 6, side_b)
     attention = pl.pallas_call(
         last_kernel,
         out_shape=jax.ShapeDtypeStruct(queries.shape, queries.dtype),
@@ -238,7 +238,7 @@
 
     width = out_weight.shape[1] // 4
 
-    def project(name, steps, dtypes):
+    def project(name, steps, dtypes, weigh=1):
         return pl.pallas_call(
             functools.partial(project_kernel, steps),
             out_shape=tuple(jax.ShapeDtypeStruct((tokens, width), dtype) for dtype in dtypes),
@@ -246,7 +246,7 @@
             out_specs=(VMEM,) * len(steps),
             compiler_params=params(8),
             cost_estimate=pl.CostEstimate(
-                flops=2 * len(steps) * tokens * width * out_weight.shape[0],
+                flops=weigh * 2 * len(steps) * tokens * width * out_weight.shape[0],
                 bytes_accessed=2 * len(steps) * width * out_weight.shape[0],
                 transcendentals=0,
             ),
@@ -256,11 +256,13 @@
     def pass_on(part, k):
         return lax.ppermute(part, "tp", [(i, i ^ k) for i in range(4)])
 
-    share_2, share_1, share_3, total = project(
-        "project", (2, 1, 3, 0), (*[jnp.bfloat16] * 3, jnp.float32)
-    )
-    for k, part in ((2, share_2), (1, share_1), (3, share_3)):
-        total = total + pass_on(part, k).astype(jnp.float32)
+    (share_2,) = project("project_2", (2,), [jnp.bfloat16])
+    got_2 = pass_on(share_2, 2)
+    _, attention = lax.optimization_barrier((share_2, attention))
+    share_1, share_3 = project("project_1_3", (1, 3), [jnp.bfloat16] * 2, 64)
+    (total,) = project("project_own", (0,), (jnp.float32,), 64)
+    for got in (got_2, pass_on(share_1, 1), pass_on(share_3, 3)):
+        total = total + got.astype(jnp.float32)
     return total.astype(jnp.bfloat16)
 
 

time: 58.7 us -> 57.7 us (0.983)
  waiting for transfers between devices: 23.3 us -> 20.6 us
  starting transfers between devices: 21.1 us -> 22 us
    ppermute x3, waiting for transfers between devices: 11.6 us -> 10.3 us  [pass_on(): return lax.ppermute(part, 'tp', [(i, i ^ k) for i in range(4)])]
    ppermute x12, waiting for transfers between devices: 11.7 us -> 10.3 us  [send(): return lax.ppermute(value, 'ctx', pairs)]
    ppermute x12, starting transfers between devices: 17.3 us -> 18 us  [send(): return lax.ppermute(value, 'ctx', pairs)]
    pallas_call x1 -> x3, Pallas kernels: 1.26 us -> 1.62 us  [project(): pl.pallas_call(functools.partial(project_kernel, steps), out_shape=tuple(...]
  transfers between devices with their start and end apart: 15 -> 15, of which waited for: 8 -> 8; matrix products, arithmetic and copies ran while one was open for 0% -> 0% of each run, Pallas kernels for 10% -> 12%
where the time goes in v5:
time: 57.7 us; the launch traced here: 56.9 us
  starting transfers between devices  22 us (38%)
  waiting for transfers between devices  20.6 us (36%)
  Pallas kernels  10.7 us (19%)
  local copies, waits for them, and re-layouts  2.22 us (4%)
  other arithmetic  1.14 us (2%)
    ppermute x12, starting transfers between devices, send(): return lax.ppermute(value, 'ctx', pairs)  18 us
    ppermute x12, waiting for transfers between devices, send(): return lax.ppermute(value, 'ctx', pairs)  10.3 us
    ppermute x3, waiting for transfers between devices, pass_on(): return lax.ppermute(part, 'tp', [(i, i ^ k) for i in range(4)])  10.3 us
    pallas_call x3, Pallas kernels, attend(): pl.pallas_call(group_kernel, out_shape=state_shape, in_specs=[VMEM] * (4...  5.12 us
    ppermute x3, starting transfers between devices, pass_on(): return lax.ppermute(part, 'tp', [(i, i ^ k) for i in range(4)])  3.96 us
    unnamed x10, local copies, waits for them, and re-layouts  2.22 us
    pallas_call x1, Pallas kernels, on_device(): pl.pallas_call(last_kernel, out_shape=jax.ShapeDtypeStruct(queries.shape,...  1.97 us
    pallas_call x3, Pallas kernels, project(): pl.pallas_call(functools.partial(project_kernel, steps), out_shape=tuple(...  1.62 us
  transfers between devices with their start and end apart: 15, of which 8 were waited for; matrix products, arithmetic and copies ran while one was open for 0% of the time, Pallas kernels for 12%

profile of v5, /device:TPU:1, one launch (start us, length us, event | category | flops | bytes accessed | tf_op | source)
XLA Modules:
  0.0 56.9 jit_solution(11109095742779965562)
XLA Ops:
  0.0 1.5 %pack.1.own_ref = bf16[1,272,128]{2,1,0:T(8,128)(2,1)} custom-call(bf16[128,128]{1,0:T(8,128)(2,1)} %k_ref.1, bf16[128,128]{1,0:T(8,128)(2,1)} %v_ref.1, s32[1,128]{1,0:T(1,128)} %bitcast.20), custom_call_target="tpu_custom_call" | custom-call | tf_op jit(solution)/shard_map/pack/pallas_call | solution.py:161
  1.5 2.5 %collective-permute-start = (bf16[1,272,128]{2,1,0:T(8,128)(2,1)}, bf16[1,272,128]{2,1,0:T(8,128)(2,1)S(1)}, u32[]{:S(2)}, u32[]{:S(2)}) collective-permute-start(bf16[1,272,128]{2,1,0:T(8,128)(2,1)} %pack.1.own_ref), channel_id=1, source_target_pairs={{0,32},{4,36},{8,40},{12,44},{16,48},{20,52},{24,56},{28,60},{32,6... | collective-permute-start | bytes 208904 | tf_op jit(solution)/shard_map/ppermute | solution.py:159
  4.1 3.0 %collective-permute-start.1 = (bf16[1,272,128]{2,1,0:T(8,128)(2,1)}, bf16[1,272,128]{2,1,0:T(8,128)(2,1)S(1)}, u32[]{:S(2)}, u32[]{:S(2)}) collective-permute-start(bf16[1,272,128]{2,1,0:T(8,128)(2,1)} %pack.1.own_ref), channel_id=1, source_target_pairs={{0,64},{4,68},{8,72},{12,76},{16,80},{20,84},{24,88},{28,92},{32,9... | collective-permute-start | bytes 208904 | tf_op jit(solution)/shard_map/ppermute | solution.py:159
  7.1 0.9 %copy-done = bf16[1,272,128]{2,1,0:T(8,128)(2,1)S(1)} copy-done((bf16[1,272,128]{2,1,0:T(8,128)(2,1)S(1)}, bf16[1,272,128]{2,1,0:T(8,128)(2,1)}, u32[]{:S(2)}) %copy-start) | copy-done | bytes 69656
  8.0 0.9 %copy-done.2 = bf16[128,1024]{1,0:T(8,128)(2,1)S(1)} copy-done((bf16[128,1024]{1,0:T(8,128)(2,1)S(1)}, bf16[128,1024]{1,0:T(8,128)(2,1)}, u32[]{:S(2)}) %copy-start.2) | copy-done | bytes 262168
  8.9 0.5 own.1
  9.5 0.5 collective-permute-done
  9.9 3.0 %collective-permute-done.1 = bf16[1,272,128]{2,1,0:T(8,128)(2,1)S(1)} collective-permute-done((bf16[1,272,128]{2,1,0:T(8,128)(2,1)}, bf16[1,272,128]{2,1,0:T(8,128)(2,1)S(1)}, u32[]{:S(2)}, u32[]{:S(2)}) %collective-permute-start.1) | collective-permute-done | bytes 69664 | tf_op jit(solution)/shard_map/ppermute | solution.py:159
  13.1 1.3 %collective-permute-start.3 = (bf16[2,272,128]{2,1,0:T(8,128)(2,1)S(1)}, bf16[2,272,128]{2,1,0:T(8,128)(2,1)S(1)}, u32[]{:S(2)}, u32[]{:S(2)}) collective-permute-start(bf16[2,272,128]{2,1,0:T(8,128)(2,1)S(1)} %get-tuple-element.42.rest_0_), channel_id=1, source_target_pairs={{0,8},{4,12},{8,16},{12,20},{16,24},{20,28},{24,0},{28,4},{32,40},... | collective-permute-start | bytes 417800 | tf_op jit(solution)/shard_map/ppermute | solution.py:159
  14.4 1.5 %collective-permute-start.4 = (bf16[2,272,128]{2,1,0:T(8,128)(2,1)S(1)}, bf16[2,272,128]{2,1,0:T(8,128)(2,1)S(1)}, u32[]{:S(2)}, u32[]{:S(2)}) collective-permute-start(bf16[2,272,128]{2,1,0:T(8,128)(2,1)S(1)} %get-tuple-element.42.rest_0_), channel_id=1, source_target_pairs={{0,24},{4,28},{8,0},{12,4},{16,8},{20,12},{24,16},{28,20},{32,56},... | collective-permute-start | bytes 417800 | tf_op jit(solution)/shard_map/ppermute | solution.py:159
  15.9 1.5 %collective-permute-start.5 = (bf16[2,272,128]{2,1,0:T(8,128)(2,1)S(1)}, bf16[2,272,128]{2,1,0:T(8,128)(2,1)S(1)}, u32[]{:S(2)}, u32[]{:S(2)}) collective-permute-start(bf16[2,272,128]{2,1,0:T(8,128)(2,1)S(1)} %get-tuple-element.42.rest_0_), channel_id=1, source_target_pairs={{0,16},{4,20},{8,24},{12,28},{16,0},{20,4},{24,8},{28,12},{32,48},... | collective-permute-start | bytes 417800 | tf_op jit(solution)/shard_map/ppermute | solution.py:159
  17.4 2.8 %collective-permute-done.2.rest_1_ = bf16[2,272,128]{2,1,0:T(8,128)(2,1)S(1)} collective-permute-done((bf16[2,272,128]{2,1,0:T(8,128)(2,1)S(1)}, bf16[2,272,128]{2,1,0:T(8,128)(2,1)S(1)}, u32[]{:S(2)}, u32[]{:S(2)}) %collective-permute-start.2) | collective-permute-done | bytes 139296 | tf_op jit(solution)/shard_map/ppermute | solution.py:159
  20.2 2.4 %collective-permute-done.5.rest_1_ = bf16[2,272,128]{2,1,0:T(8,128)(2,1)S(1)} collective-permute-done((bf16[2,272,128]{2,1,0:T(8,128)(2,1)S(1)}, bf16[2,272,128]{2,1,0:T(8,128)(2,1)S(1)}, u32[]{:S(2)}, u32[]{:S(2)}) %collective-permute-start.5) | collective-permute-done | bytes 139296 | tf_op jit(solution)/shard_map/ppermute | solution.py:159
  22.7 2.5 %collective-permute-start.10 = (bf16[4,2,272,128]{3,2,1,0:T(8,128)(2,1)S(1)}, bf16[4,2,272,128]{3,2,1,0:T(8,128)(2,1)S(1)}, u32[]{:S(2)}, u32[]{:S(2)}) collective-permute-start(bf16[4,2,272,128]{3,2,1,0:T(8,128)(2,1)S(1)} %pad_maximum_fusion), channel_id=1, source_target_pairs={{0,4},{4,0},{8,12},{12,8},{16,20},{20,16},{24,28},{28,24},{32,36},... | collective-permute-start | bytes 1671176 | tf_op jit(solution)/shard_map/ppermute | solution.py:159
  25.3 0.6 %collective-permute-start.6 = (bf16[2,272,128]{2,1,0:T(8,128)(2,1)S(1)}, bf16[2,272,128]{2,1,0:T(8,128)(2,1)S(1)}, u32[]{:S(2)}, u32[]{:S(2)}) collective-permute-start(bf16[2,272,128]{2,1,0:T(8,128)(2,1)S(1)} %get-tuple-element.70), channel_id=1, source_target_pairs={{0,8},{4,12},{8,16},{12,20},{16,24},{20,28},{24,0},{28,4},{32,40},... | collective-permute-start | bytes 417800 | tf_op jit(solution)/shard_map/ppermute | solution.py:159
  25.9 2.2 %collective-permute-start.7 = (bf16[2,272,128]{2,1,0:T(8,128)(2,1)S(1)}, bf16[2,272,128]{2,1,0:T(8,128)(2,1)S(1)}, u32[]{:S(2)}, u32[]{:S(2)}) collective-permute-start(bf16[2,272,128]{2,1,0:T(8,128)(2,1)S(1)} %get-tuple-element.68), channel_id=1, source_target_pairs={{0,24},{4,28},{8,0},{12,4},{16,8},{20,12},{24,16},{28,20},{32,56},... | collective-permute-start | bytes 417800 | tf_op jit(solution)/shard_map/ppermute | solution.py:159
  28.0 0.8 %collective-permute-start.8 = (bf16[2,272,128]{2,1,0:T(8,128)(2,1)S(1)}, bf16[2,272,128]{2,1,0:T(8,128)(2,1)S(1)}, u32[]{:S(2)}, u32[]{:S(2)}) collective-permute-start(bf16[2,272,128]{2,1,0:T(8,128)(2,1)S(1)} %get-tuple-element.69), channel_id=1, source_target_pairs={{0,16},{4,20},{8,24},{12,28},{16,0},{20,4},{24,8},{28,12},{32,48},... | collective-permute-start | bytes 417800 | tf_op jit(solution)/shard_map/ppermute | solution.py:159
  28.9 0.7 %collective-permute-start.9 = (bf16[1,272,128]{2,1,0:T(8,128)(2,1)S(1)}, bf16[1,272,128]{2,1,0:T(8,128)(2,1)S(1)}, u32[]{:S(2)}, u32[]{:S(2)}) collective-permute-start(bf16[1,272,128]{2,1,0:T(8,128)(2,1)S(1)} %get-tuple-element.65), channel_id=1, source_target_pairs={{128,132},{132,136},{136,140},{140,144},{144,148},{148,152},{152,1... | collective-permute-start | bytes 208904 | tf_op jit(solution)/shard_map/ppermute | solution.py:159
  29.5 1.7 %near_a.1 = (f32[8,1024]{1,0:T(8,128)S(1)}, f32[144,1024]{1,0:T(8,128)S(1)}) custom-call(bf16[1024,128]{1,0:T(8,128)(2,1)S(1)} %get-tuple-element.36.q_ref, bf16[1,272,128]{2,1,0:T(8,128)(2,1)S(1)} %copy-done.1, f32[8,1024]{1,0:T(8,128)S(1)} %get-tuple-element.40.m_in, f32[144,1024]{1,0:T(8,128)S(1)} %get-tuple-element.41.acc_in, ...), custom_call_target="tpu_custom_call" | custom-call | flops 17179869184 | bytes 524288 | tf_op jit(solution)/shard_map/near_a/pallas_call | solution.py:181
  31.2 2.1 %far_a.1 = (f32[8,1024]{1,0:T(8,128)S(1)}, f32[144,1024]{1,0:T(8,128)S(1)}) custom-call(bf16[1024,128]{1,0:T(8,128)(2,1)S(1)} %get-tuple-element.36.q_ref, bf16[1,272,128]{2,1,0:T(8,128)(2,1)S(1)} %copy-done.1, f32[8,1024]{1,0:T(8,128)S(1)} %get-tuple-element.46.m_in, f32[144,1024]{1,0:T(8,128)S(1)} %get-tuple-element.47.acc_in, ...), custom_call_target="tpu_custom_call" | custom-call | flops 21474836480 | bytes 655360 | tf_op jit(solution)/shard_map/far_a/pallas_call | solution.py:181
  33.3 1.4 %collective-permute-done.8.rest_0_ = bf16[2,272,128]{2,1,0:T(8,128)(2,1)S(1)} collective-permute-done((bf16[2,272,128]{2,1,0:T(8,128)(2,1)S(1)}, bf16[2,272,128]{2,1,0:T(8,128)(2,1)S(1)}, u32[]{:S(2)}, u32[]{:S(2)}) %collective-permute-start.8) | collective-permute-done | bytes 139296 | tf_op jit(solution)/shard_map/ppermute | solution.py:159
  34.8 1.4 %collective-permute-start.11 = (bf16[4,2,272,128]{3,2,1,0:T(8,128)(2,1)S(1)}, bf16[4,2,272,128]{3,2,1,0:T(8,128)(2,1)S(1)}, u32[]{:S(2)}, u32[]{:S(2)}) collective-permute-start(bf16[4,2,272,128]{3,2,1,0:T(8,128)(2,1)S(1)} %pad_maximum_fusion.1), channel_id=1, source_target_pairs={{0,4},{4,0},{8,12},{12,8},{16,20},{20,16},{24,28},{28,24},{32,36},... | collective-permute-start | bytes 1671176 | tf_op jit(solution)/shard_map/ppermute | solution.py:159
  36.3 1.4 %near_b.1 = (f32[8,1024]{1,0:T(8,128)S(1)}, f32[144,1024]{1,0:T(8,128)S(1)}) custom-call(bf16[1024,128]{1,0:T(8,128)(2,1)S(1)} %get-tuple-element.36.q_ref, bf16[1,272,128]{2,1,0:T(8,128)(2,1)S(1)} %copy-done.1, f32[8,1024]{1,0:T(8,128)S(1)} %get-tuple-element.50.m_in, f32[144,1024]{1,0:T(8,128)S(1)} %get-tuple-element.51.acc_in, ...), custom_call_target="tpu_custom_call" | custom-call | flops 12884901888 | bytes 393216 | tf_op jit(solution)/shard_map/near_b/pallas_call | solution.py:181
  37.8 2.0 %last.1.att_ref = bf16[128,1024]{1,0:T(8,128)(2,1)S(1)} custom-call(bf16[1024,128]{1,0:T(8,128)(2,1)S(1)} %get-tuple-element.36.q_ref, bf16[1,272,128]{2,1,0:T(8,128)(2,1)S(1)} %copy-done.1, f32[8,1024]{1,0:T(8,128)S(1)} %get-tuple-element.55.m_in, f32[144,1024]{1,0:T(8,128)S(1)} %get-tuple-element.56.acc_in, ...), custom_call_target="tpu_custom_call" | custom-call | flops 19327352832 | bytes 589824 | tf_op jit(solution)/shard_map/last/pallas_call | solution.py:229
  40.2 0.5 project_2.1
  40.6 3.0 %collective-permute-start.12 = (bf16[128,1024]{1,0:T(8,128)(2,1)S(1)}, bf16[128,1024]{1,0:T(8,128)(2,1)S(1)}, u32[]{:S(2)}, u32[]{:S(2)}) collective-permute-start(bf16[128,1024]{1,0:T(8,128)(2,1)S(1)} %project_2.1), channel_id=1, source_target_pairs={{0,2},{1,3},{2,0},{3,1},{4,6},{5,7},{6,4},{7,5},{8,10},{9,11},{10,... | collective-permute-start | bytes 786440 | tf_op jit(solution)/shard_map/ppermute | solution.py:257
  43.6 0.7 %project_1_3.1 = (bf16[128,1024]{1,0:T(8,128)(2,1)S(1)}, bf16[128,1024]{1,0:T(8,128)(2,1)S(1)}) custom-call(s32[1]{0:T(128)} %bitcast.lane_ref, bf16[128,1024]{1,0:T(8,128)(2,1)S(1)} %last.1.att_ref, bf16[1024,4096]{1,0:T(8,128)(2,1)S(1)} %bitcast.12), custom_call_target="tpu_custom_call" | custom-call | flops 34359738368 | bytes 4194304 | tf_op jit(solution)/shard_map/project_1_3/pallas_call | solution.py:242
  44.4 0.5 collective-permute-start.13
  44.9 0.5 collective-permute-start.14
  45.3 0.4 project_own.1
  45.8 10.1 %collective-permute-done.13 = bf16[128,1024]{1,0:T(8,128)(2,1)S(1)} collective-permute-done((bf16[128,1024]{1,0:T(8,128)(2,1)S(1)}, bf16[128,1024]{1,0:T(8,128)(2,1)S(1)}, u32[]{:S(2)}, u32[]{:S(2)}) %collective-permute-start.13) | collective-permute-done | bytes 262176 | tf_op jit(solution)/shard_map/ppermute | solution.py:257
  56.1 0.8 %add_convert_fusion = bf16[128,1024]{1,0:T(8,128)(2,1)} fusion(bf16[128,1024]{1,0:T(8,128)(2,1)S(1)} %collective-permute-done.14, bf16[128,1024]{1,0:T(8,128)(2,1)S(1)} %collective-permute-done.13, f32[128,1024]{1,0:T(8,128)S(1)} %project_own.1, bf16[128,1024]{1,0:T(8,128)(2,1)S(1)} %collective-permute-done.12), kind=kLoop, calls=%fused_computation.2 | loop fusion | flops 917504 | bytes 1572864 | tf_op jit(solution)/shard_map/convert_element_type | solution.py:266
  (26 shorter events, 1.2 us)
Async XLA Ops:
  1.5 8.4 %collective-permute-start = (bf16[1,272,128]{2,1,0:T(8,128)(2,1)}, bf16[1,272,128]{2,1,0:T(8,128)(2,1)S(1)}, u32[]{:S(2)}, u32[]{:S(2)}) collective-permute-start(bf16[1,272,128]{2,1,0:T(8,128)(2,1)} %pack.1.own_ref), channel_id=1, source_target_pairs={{0,32},{4,36},{8,40},{12,44},{16,48},{20,52},{24,56},{28,60},{32,6... | collective-permute-start | bytes 208904 | tf_op jit(solution)/shard_map/ppermute | solution.py:159
  4.1 8.9 %collective-permute-start.1 = (bf16[1,272,128]{2,1,0:T(8,128)(2,1)}, bf16[1,272,128]{2,1,0:T(8,128)(2,1)S(1)}, u32[]{:S(2)}, u32[]{:S(2)}) collective-permute-start(bf16[1,272,128]{2,1,0:T(8,128)(2,1)} %pack.1.own_ref), channel_id=1, source_target_pairs={{0,64},{4,68},{8,72},{12,76},{16,80},{20,84},{24,88},{28,92},{32,9... | collective-permute-start | bytes 208904 | tf_op jit(solution)/shard_map/ppermute | solution.py:159
  7.1 0.9 %copy-start = (bf16[1,272,128]{2,1,0:T(8,128)(2,1)S(1)}, bf16[1,272,128]{2,1,0:T(8,128)(2,1)}, u32[]{:S(2)}) copy-start(bf16[1,272,128]{2,1,0:T(8,128)(2,1)} %pack.1.own_ref) | copy-start | bytes 208900
  8.0 0.9 %copy-start.2 = (bf16[128,1024]{1,0:T(8,128)(2,1)S(1)}, bf16[128,1024]{1,0:T(8,128)(2,1)}, u32[]{:S(2)}) copy-start(bf16[128,1024]{1,0:T(8,128)(2,1)} %q_ref.1) | copy-start | bytes 786436
  8.9 16.3 %copy-start.1 = (bf16[1,272,128]{2,1,0:T(8,128)(2,1)S(1)}, bf16[1,272,128]{2,1,0:T(8,128)(2,1)}, u32[]{:S(2)}) copy-start(bf16[1,272,128]{2,1,0:T(8,128)(2,1)} %pack.1.own_ref) | copy-start | bytes 208900
  13.0 7.2 %collective-permute-start.2 = (bf16[2,272,128]{2,1,0:T(8,128)(2,1)S(1)}, bf16[2,272,128]{2,1,0:T(8,128)(2,1)S(1)}, u32[]{:S(2)}, u32[]{:S(2)}) collective-permute-start(bf16[2,272,128]{2,1,0:T(8,128)(2,1)S(1)} %pad_maximum_fusion.6), channel_id=1, source_target_pairs={{0,64},{4,68},{8,72},{12,76},{16,80},{20,84},{24,88},{28,92},{32,9... | collective-permute-start | bytes 417800 | tf_op jit(solution)/shard_map/ppermute | solution.py:159
  13.1 7.1 %collective-permute-start.3 = (bf16[2,272,128]{2,1,0:T(8,128)(2,1)S(1)}, bf16[2,272,128]{2,1,0:T(8,128)(2,1)S(1)}, u32[]{:S(2)}, u32[]{:S(2)}) collective-permute-start(bf16[2,272,128]{2,1,0:T(8,128)(2,1)S(1)} %get-tuple-element.42.rest_0_), channel_id=1, source_target_pairs={{0,8},{4,12},{8,16},{12,20},{16,24},{20,28},{24,0},{28,4},{32,40},... | collective-permute-start | bytes 417800 | tf_op jit(solution)/shard_map/ppermute | solution.py:159
  14.4 5.8 %collective-permute-start.4 = (bf16[2,272,128]{2,1,0:T(8,128)(2,1)S(1)}, bf16[2,272,128]{2,1,0:T(8,128)(2,1)S(1)}, u32[]{:S(2)}, u32[]{:S(2)}) collective-permute-start(bf16[2,272,128]{2,1,0:T(8,128)(2,1)S(1)} %get-tuple-element.42.rest_0_), channel_id=1, source_target_pairs={{0,24},{4,28},{8,0},{12,4},{16,8},{20,12},{24,16},{28,20},{32,56},... | collective-permute-start | bytes 417800 | tf_op jit(solution)/shard_map/ppermute | solution.py:159
  15.9 6.8 %collective-permute-start.5 = (bf16[2,272,128]{2,1,0:T(8,128)(2,1)S(1)}, bf16[2,272,128]{2,1,0:T(8,128)(2,1)S(1)}, u32[]{:S(2)}, u32[]{:S(2)}) collective-permute-start(bf16[2,272,128]{2,1,0:T(8,128)(2,1)S(1)} %get-tuple-element.42.rest_0_), channel_id=1, source_target_pairs={{0,16},{4,20},{8,24},{12,28},{16,0},{20,4},{24,8},{28,12},{32,48},... | collective-permute-start | bytes 417800 | tf_op jit(solution)/shard_map/ppermute | solution.py:159
  22.7 8.5 %collective-permute-start.10 = (bf16[4,2,272,128]{3,2,1,0:T(8,128)(2,1)S(1)}, bf16[4,2,272,128]{3,2,1,0:T(8,128)(2,1)S(1)}, u32[]{:S(2)}, u32[]{:S(2)}) collective-permute-start(bf16[4,2,272,128]{3,2,1,0:T(8,128)(2,1)S(1)} %pad_maximum_fusion), channel_id=1, source_target_pairs={{0,4},{4,0},{8,12},{12,8},{16,20},{20,16},{24,28},{28,24},{32,36},... | collective-permute-start | bytes 1671176 | tf_op jit(solution)/shard_map/ppermute | solution.py:159
  25.3 8.0 %collective-permute-start.6 = (bf16[2,272,128]{2,1,0:T(8,128)(2,1)S(1)}, bf16[2,272,128]{2,1,0:T(8,128)(2,1)S(1)}, u32[]{:S(2)}, u32[]{:S(2)}) collective-permute-start(bf16[2,272,128]{2,1,0:T(8,128)(2,1)S(1)} %get-tuple-element.70), channel_id=1, source_target_pairs={{0,8},{4,12},{8,16},{12,20},{16,24},{20,28},{24,0},{28,4},{32,40},... | collective-permute-start | bytes 417800 | tf_op jit(solution)/shard_map/ppermute | solution.py:159
  25.9 7.5 %collective-permute-start.7 = (bf16[2,272,128]{2,1,0:T(8,128)(2,1)S(1)}, bf16[2,272,128]{2,1,0:T(8,128)(2,1)S(1)}, u32[]{:S(2)}, u32[]{:S(2)}) collective-permute-start(bf16[2,272,128]{2,1,0:T(8,128)(2,1)S(1)} %get-tuple-element.68), channel_id=1, source_target_pairs={{0,24},{4,28},{8,0},{12,4},{16,8},{20,12},{24,16},{28,20},{32,56},... | collective-permute-start | bytes 417800 | tf_op jit(solution)/shard_map/ppermute | solution.py:159
  28.0 6.7 %collective-permute-start.8 = (bf16[2,272,128]{2,1,0:T(8,128)(2,1)S(1)}, bf16[2,272,128]{2,1,0:T(8,128)(2,1)S(1)}, u32[]{:S(2)}, u32[]{:S(2)}) collective-permute-start(bf16[2,272,128]{2,1,0:T(8,128)(2,1)S(1)} %get-tuple-element.69), channel_id=1, source_target_pairs={{0,16},{4,20},{8,24},{12,28},{16,0},{20,4},{24,8},{28,12},{32,48},... | collective-permute-start | bytes 417800 | tf_op jit(solution)/shard_map/ppermute | solution.py:159
  28.9 4.5 %collective-permute-start.9 = (bf16[1,272,128]{2,1,0:T(8,128)(2,1)S(1)}, bf16[1,272,128]{2,1,0:T(8,128)(2,1)S(1)}, u32[]{:S(2)}, u32[]{:S(2)}) collective-permute-start(bf16[1,272,128]{2,1,0:T(8,128)(2,1)S(1)} %get-tuple-element.65), channel_id=1, source_target_pairs={{128,132},{132,136},{136,140},{140,144},{144,148},{148,152},{152,1... | collective-permute-start | bytes 208904 | tf_op jit(solution)/shard_map/ppermute | solution.py:159
  34.8 3.0 %collective-permute-start.11 = (bf16[4,2,272,128]{3,2,1,0:T(8,128)(2,1)S(1)}, bf16[4,2,272,128]{3,2,1,0:T(8,128)(2,1)S(1)}, u32[]{:S(2)}, u32[]{:S(2)}) collective-permute-start(bf16[4,2,272,128]{3,2,1,0:T(8,128)(2,1)S(1)} %pad_maximum_fusion.1), channel_id=1, source_target_pairs={{0,4},{4,0},{8,12},{12,8},{16,20},{20,16},{24,28},{28,24},{32,36},... | collective-permute-start | bytes 1671176 | tf_op jit(solution)/shard_map/ppermute | solution.py:159
  36.3 3.6 %slice-start = ((s8[8388608]{0:T(1024)(128)(4,1)}), s8[4194304]{0:T(1024)(128)(4,1)S(1)}, s32[]{:S(2)}) async-start(s8[8388608]{0:T(1024)(128)(4,1)} %bitcast.11), calls=%async_computation | async-start | bytes 8388608
  37.8 2.3 %slice-start.1 = ((s8[8388608]{0:T(1024)(128)(4,1)}), s8[4194304]{0:T(1024)(128)(4,1)S(1)}, s32[]{:S(2)}) async-start(s8[8388608]{0:T(1024)(128)(4,1)} %bitcast.11), calls=%async_computation.1 | async-start | bytes 8388608
  40.6 15.4 %collective-permute-start.12 = (bf16[128,1024]{1,0:T(8,128)(2,1)S(1)}, bf16[128,1024]{1,0:T(8,128)(2,1)S(1)}, u32[]{:S(2)}, u32[]{:S(2)}) collective-permute-start(bf16[128,1024]{1,0:T(8,128)(2,1)S(1)} %project_2.1), channel_id=1, source_target_pairs={{0,2},{1,3},{2,0},{3,1},{4,6},{5,7},{6,4},{7,5},{8,10},{9,11},{10,... | collective-permute-start | bytes 786440 | tf_op jit(solution)/shard_map/ppermute | solution.py:257
  44.4 11.5 %collective-permute-start.13 = (bf16[128,1024]{1,0:T(8,128)(2,1)S(1)}, bf16[128,1024]{1,0:T(8,128)(2,1)S(1)}, u32[]{:S(2)}, u32[]{:S(2)}) collective-permute-start(bf16[128,1024]{1,0:T(8,128)(2,1)S(1)} %get-tuple-element.59), channel_id=1, source_target_pairs={{0,1},{1,0},{2,3},{3,2},{4,5},{5,4},{6,7},{7,6},{8,9},{9,8},{10,11... | collective-permute-start | bytes 786440 | tf_op jit(solution)/shard_map/ppermute | solution.py:257
  44.9 11.2 %collective-permute-start.14 = (bf16[128,1024]{1,0:T(8,128)(2,1)S(1)}, bf16[128,1024]{1,0:T(8,128)(2,1)S(1)}, u32[]{:S(2)}, u32[]{:S(2)}) collective-permute-start(bf16[128,1024]{1,0:T(8,128)(2,1)S(1)} %get-tuple-element.60), channel_id=1, source_target_pairs={{0,3},{1,2},{2,1},{3,0},{4,7},{5,6},{6,5},{7,4},{8,11},{9,10},{10,... | collective-permute-start | bytes 786440 | tf_op jit(solution)/shard_map/ppermute | solution.py:257

commit v6 on v5

--- a/solution.py
+++ b/solution.py
@@ -131,8 +131,8 @@
     acc_ref[...] = acc
 
 
-def last_kernel(q_ref, own_ref, m_in, acc_in, far_ref, beyond_ref, att_ref):
-    _, acc = run(q_ref, own_ref, m_in, acc_in, [far_ref, beyond_ref])
+def last_kernel(q_ref, own_ref, m_in, acc_in, far_ref, att_ref):
+    _, acc = run(q_ref, own_ref, m_in, acc_in, [far_ref])
     result = acc[0:128] / acc[128:129]
     for h in range(q_ref.shape[0] // att_ref.shape[0]):
         part = slice(h * HEAD_DIM, (h + 1) * HEAD_DIM)
@@ -225,16 +225,16 @@
     )
 
     far_b = send(jnp.stack([with_either(c == 0), *side_b]), swap_core(size))
-    state = attend("near_b", state, 6, side_b)
+    state = attend("near_b", state, 7, [*side_b, beyond])
     attention = pl.pallas_call(
         last_kernel,
         out_shape=jax.ShapeDtypeStruct(queries.shape, queries.dtype),
-        in_specs=[VMEM] * 6,
+        in_specs=[VMEM] * 5,
         out_specs=VMEM,
         compiler_params=params(16),
-        cost_estimate=cost(9, rows),
+        cost_estimate=cost(8, rows),
         name="last",
-    )(heads, own, *state, far_b, beyond)
+    )(heads, own, *state, far_b)
 
     width = out_weight.shape[1] // 4
 

time: 57.7 us -> 57.7 us (level)
  transfers between devices with their start and end apart: 15 -> 15, of which waited for: 8 -> 7; matrix products, arithmetic and copies ran while one was open for 0% -> 0% of each run, Pallas kernels for 12% -> 12%
where the time goes in v6:
time: 57.7 us; the launch traced here: 56.9 us
  starting transfers between devices  22 us (38%)
  waiting for transfers between devices  20.4 us (35%)
  Pallas kernels  10.8 us (19%)
  local copies, waits for them, and re-layouts  2.33 us (4%)
  other arithmetic  1.14 us (2%)
    ppermute x12, starting transfers between devices, send(): return lax.ppermute(value, 'ctx', pairs)  18 us
    ppermute x3, waiting for transfers between devices, pass_on(): return lax.ppermute(part, 'tp', [(i, i ^ k) for i in range(4)])  10.3 us
    ppermute x12, waiting for transfers between devices, send(): return lax.ppermute(value, 'ctx', pairs)  10.2 us
    pallas_call x3, Pallas kernels, attend(): pl.pallas_call(group_kernel, out_shape=state_shape, in_specs=[VMEM] * (4...  5.31 us
    ppermute x3, starting transfers between devices, pass_on(): return lax.ppermute(part, 'tp', [(i, i ^ k) for i in range(4)])  3.97 us
    unnamed x10, local copies, waits for them, and re-layouts  2.33 us
    pallas_call x1, Pallas kernels, on_device(): pl.pallas_call(last_kernel, out_shape=jax.ShapeDtypeStruct(queries.shape,...  1.85 us
    pallas_call x3, Pallas kernels, project(): pl.pallas_call(functools.partial(project_kernel, steps), out_shape=tuple(...  1.63 us
  transfers between devices with their start and end apart: 15, of which 7 were waited for; matrix products, arithmetic and copies ran while one was open for 0% of the time, Pallas kernels for 12%

profile of v6, /device:TPU:1, one launch (start us, length us, event | category | flops | bytes accessed | tf_op | source)
XLA Modules:
  0.0 56.9 jit_solution(8941555093551293405)
XLA Ops:
  0.0 1.5 %pack.1.own_ref = bf16[1,272,128]{2,1,0:T(8,128)(2,1)} custom-call(bf16[128,128]{1,0:T(8,128)(2,1)} %k_ref.1, bf16[128,128]{1,0:T(8,128)(2,1)} %v_ref.1, s32[1,128]{1,0:T(1,128)} %bitcast.20), custom_call_target="tpu_custom_call" | custom-call | tf_op jit(solution)/shard_map/pack/pallas_call | solution.py:161
  1.5 2.5 %collective-permute-start = (bf16[1,272,128]{2,1,0:T(8,128)(2,1)}, bf16[1,272,128]{2,1,0:T(8,128)(2,1)S(1)}, u32[]{:S(2)}, u32[]{:S(2)}) collective-permute-start(bf16[1,272,128]{2,1,0:T(8,128)(2,1)} %pack.1.own_ref), channel_id=1, source_target_pairs={{0,32},{4,36},{8,40},{12,44},{16,48},{20,52},{24,56},{28,60},{32,6... | collective-permute-start | bytes 208904 | tf_op jit(solution)/shard_map/ppermute | solution.py:159
  4.1 3.0 %collective-permute-start.1 = (bf16[1,272,128]{2,1,0:T(8,128)(2,1)}, bf16[1,272,128]{2,1,0:T(8,128)(2,1)S(1)}, u32[]{:S(2)}, u32[]{:S(2)}) collective-permute-start(bf16[1,272,128]{2,1,0:T(8,128)(2,1)} %pack.1.own_ref), channel_id=1, source_target_pairs={{0,64},{4,68},{8,72},{12,76},{16,80},{20,84},{24,88},{28,92},{32,9... | collective-permute-start | bytes 208904 | tf_op jit(solution)/shard_map/ppermute | solution.py:159
  7.1 0.9 %copy-done = bf16[1,272,128]{2,1,0:T(8,128)(2,1)S(1)} copy-done((bf16[1,272,128]{2,1,0:T(8,128)(2,1)S(1)}, bf16[1,272,128]{2,1,0:T(8,128)(2,1)}, u32[]{:S(2)}) %copy-start) | copy-done | bytes 69656
  8.0 0.9 %copy-done.2 = bf16[128,1024]{1,0:T(8,128)(2,1)S(1)} copy-done((bf16[128,1024]{1,0:T(8,128)(2,1)S(1)}, bf16[128,1024]{1,0:T(8,128)(2,1)}, u32[]{:S(2)}) %copy-start.2) | copy-done | bytes 262168
  8.9 0.5 own.1
  9.5 0.5 collective-permute-done
  9.9 3.0 %collective-permute-done.1 = bf16[1,272,128]{2,1,0:T(8,128)(2,1)S(1)} collective-permute-done((bf16[1,272,128]{2,1,0:T(8,128)(2,1)}, bf16[1,272,128]{2,1,0:T(8,128)(2,1)S(1)}, u32[]{:S(2)}, u32[]{:S(2)}) %collective-permute-start.1) | collective-permute-done | bytes 69664 | tf_op jit(solution)/shard_map/ppermute | solution.py:159
  13.1 1.3 %collective-permute-start.3 = (bf16[2,272,128]{2,1,0:T(8,128)(2,1)S(1)}, bf16[2,272,128]{2,1,0:T(8,128)(2,1)S(1)}, u32[]{:S(2)}, u32[]{:S(2)}) collective-permute-start(bf16[2,272,128]{2,1,0:T(8,128)(2,1)S(1)} %get-tuple-element.42.rest_0_), channel_id=1, source_target_pairs={{0,8},{4,12},{8,16},{12,20},{16,24},{20,28},{24,0},{28,4},{32,40},... | collective-permute-start | bytes 417800 | tf_op jit(solution)/shard_map/ppermute | solution.py:159
  14.4 1.5 %collective-permute-start.4 = (bf16[2,272,128]{2,1,0:T(8,128)(2,1)S(1)}, bf16[2,272,128]{2,1,0:T(8,128)(2,1)S(1)}, u32[]{:S(2)}, u32[]{:S(2)}) collective-permute-start(bf16[2,272,128]{2,1,0:T(8,128)(2,1)S(1)} %get-tuple-element.42.rest_0_), channel_id=1, source_target_pairs={{0,24},{4,28},{8,0},{12,4},{16,8},{20,12},{24,16},{28,20},{32,56},... | collective-permute-start | bytes 417800 | tf_op jit(solution)/shard_map/ppermute | solution.py:159
  15.9 1.5 %collective-permute-start.5 = (bf16[2,272,128]{2,1,0:T(8,128)(2,1)S(1)}, bf16[2,272,128]{2,1,0:T(8,128)(2,1)S(1)}, u32[]{:S(2)}, u32[]{:S(2)}) collective-permute-start(bf16[2,272,128]{2,1,0:T(8,128)(2,1)S(1)} %get-tuple-element.42.rest_0_), channel_id=1, source_target_pairs={{0,16},{4,20},{8,24},{12,28},{16,0},{20,4},{24,8},{28,12},{32,48},... | collective-permute-start | bytes 417800 | tf_op jit(solution)/shard_map/ppermute | solution.py:159
  17.4 2.8 %collective-permute-done.2.rest_1_ = bf16[2,272,128]{2,1,0:T(8,128)(2,1)S(1)} collective-permute-done((bf16[2,272,128]{2,1,0:T(8,128)(2,1)S(1)}, bf16[2,272,128]{2,1,0:T(8,128)(2,1)S(1)}, u32[]{:S(2)}, u32[]{:S(2)}) %collective-permute-start.2) | collective-permute-done | bytes 139296 | tf_op jit(solution)/shard_map/ppermute | solution.py:159
  20.2 2.4 %collective-permute-done.5.rest_1_ = bf16[2,272,128]{2,1,0:T(8,128)(2,1)S(1)} collective-permute-done((bf16[2,272,128]{2,1,0:T(8,128)(2,1)S(1)}, bf16[2,272,128]{2,1,0:T(8,128)(2,1)S(1)}, u32[]{:S(2)}, u32[]{:S(2)}) %collective-permute-start.5) | collective-permute-done | bytes 139296 | tf_op jit(solution)/shard_map/ppermute | solution.py:159
  22.7 2.5 %collective-permute-start.10 = (bf16[4,2,272,128]{3,2,1,0:T(8,128)(2,1)S(1)}, bf16[4,2,272,128]{3,2,1,0:T(8,128)(2,1)S(1)}, u32[]{:S(2)}, u32[]{:S(2)}) collective-permute-start(bf16[4,2,272,128]{3,2,1,0:T(8,128)(2,1)S(1)} %pad_maximum_fusion), channel_id=1, source_target_pairs={{0,4},{4,0},{8,12},{12,8},{16,20},{20,16},{24,28},{28,24},{32,36},... | collective-permute-start | bytes 1671176 | tf_op jit(solution)/shard_map/ppermute | solution.py:159
  25.3 0.6 %collective-permute-start.6 = (bf16[2,272,128]{2,1,0:T(8,128)(2,1)S(1)}, bf16[2,272,128]{2,1,0:T(8,128)(2,1)S(1)}, u32[]{:S(2)}, u32[]{:S(2)}) collective-permute-start(bf16[2,272,128]{2,1,0:T(8,128)(2,1)S(1)} %get-tuple-element.70), channel_id=1, source_target_pairs={{0,8},{4,12},{8,16},{12,20},{16,24},{20,28},{24,0},{28,4},{32,40},... | collective-permute-start | bytes 417800 | tf_op jit(solution)/shard_map/ppermute | solution.py:159
  25.9 2.2 %collective-permute-start.7 = (bf16[2,272,128]{2,1,0:T(8,128)(2,1)S(1)}, bf16[2,272,128]{2,1,0:T(8,128)(2,1)S(1)}, u32[]{:S(2)}, u32[]{:S(2)}) collective-permute-start(bf16[2,272,128]{2,1,0:T(8,128)(2,1)S(1)} %get-tuple-element.68), channel_id=1, source_target_pairs={{0,24},{4,28},{8,0},{12,4},{16,8},{20,12},{24,16},{28,20},{32,56},... | collective-permute-start | bytes 417800 | tf_op jit(solution)/shard_map/ppermute | solution.py:159
  28.0 0.8 %collective-permute-start.8 = (bf16[2,272,128]{2,1,0:T(8,128)(2,1)S(1)}, bf16[2,272,128]{2,1,0:T(8,128)(2,1)S(1)}, u32[]{:S(2)}, u32[]{:S(2)}) collective-permute-start(bf16[2,272,128]{2,1,0:T(8,128)(2,1)S(1)} %get-tuple-element.69), channel_id=1, source_target_pairs={{0,16},{4,20},{8,24},{12,28},{16,0},{20,4},{24,8},{28,12},{32,48},... | collective-permute-start | bytes 417800 | tf_op jit(solution)/shard_map/ppermute | solution.py:159
  28.9 0.7 %collective-permute-start.9 = (bf16[1,272,128]{2,1,0:T(8,128)(2,1)S(1)}, bf16[1,272,128]{2,1,0:T(8,128)(2,1)S(1)}, u32[]{:S(2)}, u32[]{:S(2)}) collective-permute-start(bf16[1,272,128]{2,1,0:T(8,128)(2,1)S(1)} %get-tuple-element.65), channel_id=1, source_target_pairs={{128,132},{132,136},{136,140},{140,144},{144,148},{148,152},{152,1... | collective-permute-start | bytes 208904 | tf_op jit(solution)/shard_map/ppermute | solution.py:159
  29.5 1.7 %near_a.1 = (f32[8,1024]{1,0:T(8,128)S(1)}, f32[144,1024]{1,0:T(8,128)S(1)}) custom-call(bf16[1024,128]{1,0:T(8,128)(2,1)S(1)} %get-tuple-element.36.q_ref, bf16[1,272,128]{2,1,0:T(8,128)(2,1)S(1)} %copy-done.1, f32[8,1024]{1,0:T(8,128)S(1)} %get-tuple-element.40.m_in, f32[144,1024]{1,0:T(8,128)S(1)} %get-tuple-element.41.acc_in, ...), custom_call_target="tpu_custom_call" | custom-call | flops 17179869184 | bytes 524288 | tf_op jit(solution)/shard_map/near_a/pallas_call | solution.py:181
  31.2 2.0 %far_a.1 = (f32[8,1024]{1,0:T(8,128)S(1)}, f32[144,1024]{1,0:T(8,128)S(1)}) custom-call(bf16[1024,128]{1,0:T(8,128)(2,1)S(1)} %get-tuple-element.36.q_ref, bf16[1,272,128]{2,1,0:T(8,128)(2,1)S(1)} %copy-done.1, f32[8,1024]{1,0:T(8,128)S(1)} %get-tuple-element.46.m_in, f32[144,1024]{1,0:T(8,128)S(1)} %get-tuple-element.47.acc_in, ...), custom_call_target="tpu_custom_call" | custom-call | flops 21474836480 | bytes 655360 | tf_op jit(solution)/shard_map/far_a/pallas_call | solution.py:181
  33.3 1.4 %collective-permute-done.8.rest_0_ = bf16[2,272,128]{2,1,0:T(8,128)(2,1)S(1)} collective-permute-done((bf16[2,272,128]{2,1,0:T(8,128)(2,1)S(1)}, bf16[2,272,128]{2,1,0:T(8,128)(2,1)S(1)}, u32[]{:S(2)}, u32[]{:S(2)}) %collective-permute-start.8) | collective-permute-done | bytes 139296 | tf_op jit(solution)/shard_map/ppermute | solution.py:159
  34.8 1.4 %collective-permute-start.11 = (bf16[4,2,272,128]{3,2,1,0:T(8,128)(2,1)S(1)}, bf16[4,2,272,128]{3,2,1,0:T(8,128)(2,1)S(1)}, u32[]{:S(2)}, u32[]{:S(2)}) collective-permute-start(bf16[4,2,272,128]{3,2,1,0:T(8,128)(2,1)S(1)} %pad_maximum_fusion.1), channel_id=1, source_target_pairs={{0,4},{4,0},{8,12},{12,8},{16,20},{20,16},{24,28},{28,24},{32,36},... | collective-permute-start | bytes 1671176 | tf_op jit(solution)/shard_map/ppermute | solution.py:159
  36.3 1.6 %near_b.1 = (f32[8,1024]{1,0:T(8,128)S(1)}, f32[144,1024]{1,0:T(8,128)S(1)}) custom-call(bf16[1024,128]{1,0:T(8,128)(2,1)S(1)} %get-tuple-element.36.q_ref, bf16[1,272,128]{2,1,0:T(8,128)(2,1)S(1)} %copy-done.1, f32[8,1024]{1,0:T(8,128)S(1)} %get-tuple-element.50.m_in, f32[144,1024]{1,0:T(8,128)S(1)} %get-tuple-element.51.acc_in, ...), custom_call_target="tpu_custom_call" | custom-call | flops 15032385536 | bytes 458752 | tf_op jit(solution)/shard_map/near_b/pallas_call | solution.py:181
  37.9 1.9 %last.1.att_ref = bf16[128,1024]{1,0:T(8,128)(2,1)S(1)} custom-call(bf16[1024,128]{1,0:T(8,128)(2,1)S(1)} %get-tuple-element.36.q_ref, bf16[1,272,128]{2,1,0:T(8,128)(2,1)S(1)} %copy-done.1, f32[8,1024]{1,0:T(8,128)S(1)} %get-tuple-element.56.m_in, f32[144,1024]{1,0:T(8,128)S(1)} %get-tuple-element.57.acc_in, ...), custom_call_target="tpu_custom_call" | custom-call | flops 17179869184 | bytes 524288 | tf_op jit(solution)/shard_map/last/pallas_call | solution.py:229
  39.7 0.5 slice-done.1
  40.6 3.0 %collective-permute-start.12 = (bf16[128,1024]{1,0:T(8,128)(2,1)S(1)}, bf16[128,1024]{1,0:T(8,128)(2,1)S(1)}, u32[]{:S(2)}, u32[]{:S(2)}) collective-permute-start(bf16[128,1024]{1,0:T(8,128)(2,1)S(1)} %project_2.1), channel_id=1, source_target_pairs={{0,2},{1,3},{2,0},{3,1},{4,6},{5,7},{6,4},{7,5},{8,10},{9,11},{10,... | collective-permute-start | bytes 786440 | tf_op jit(solution)/shard_map/ppermute | solution.py:257
  43.6 0.7 %project_1_3.1 = (bf16[128,1024]{1,0:T(8,128)(2,1)S(1)}, bf16[128,1024]{1,0:T(8,128)(2,1)S(1)}) custom-call(s32[1]{0:T(128)} %bitcast.lane_ref, bf16[128,1024]{1,0:T(8,128)(2,1)S(1)} %last.1.att_ref, bf16[1024,4096]{1,0:T(8,128)(2,1)S(1)} %bitcast.12), custom_call_target="tpu_custom_call" | custom-call | flops 34359738368 | bytes 4194304 | tf_op jit(solution)/shard_map/project_1_3/pallas_call | solution.py:242
  44.4 0.5 collective-permute-start.13
  44.9 0.5 collective-permute-start.14
  45.3 0.5 project_own.1
  45.8 10.0 %collective-permute-done.13 = bf16[128,1024]{1,0:T(8,128)(2,1)S(1)} collective-permute-done((bf16[128,1024]{1,0:T(8,128)(2,1)S(1)}, bf16[128,1024]{1,0:T(8,128)(2,1)S(1)}, u32[]{:S(2)}, u32[]{:S(2)}) %collective-permute-start.13) | collective-permute-done | bytes 262176 | tf_op jit(solution)/shard_map/ppermute | solution.py:257
  56.1 0.8 %add_convert_fusion = bf16[128,1024]{1,0:T(8,128)(2,1)} fusion(bf16[128,1024]{1,0:T(8,128)(2,1)S(1)} %collective-permute-done.14, bf16[128,1024]{1,0:T(8,128)(2,1)S(1)} %collective-permute-done.13, f32[128,1024]{1,0:T(8,128)S(1)} %project_own.1, bf16[128,1024]{1,0:T(8,128)(2,1)S(1)} %collective-permute-done.12), kind=kLoop, calls=%fused_computation.2 | loop fusion | flops 917504 | bytes 1572864 | tf_op jit(solution)/shard_map/convert_element_type | solution.py:266
  (26 shorter events, 1.1 us)
Async XLA Ops:
  1.5 8.4 %collective-permute-start = (bf16[1,272,128]{2,1,0:T(8,128)(2,1)}, bf16[1,272,128]{2,1,0:T(8,128)(2,1)S(1)}, u32[]{:S(2)}, u32[]{:S(2)}) collective-permute-start(bf16[1,272,128]{2,1,0:T(8,128)(2,1)} %pack.1.own_ref), channel_id=1, source_target_pairs={{0,32},{4,36},{8,40},{12,44},{16,48},{20,52},{24,56},{28,60},{32,6... | collective-permute-start | bytes 208904 | tf_op jit(solution)/shard_map/ppermute | solution.py:159
  4.1 8.9 %collective-permute-start.1 = (bf16[1,272,128]{2,1,0:T(8,128)(2,1)}, bf16[1,272,128]{2,1,0:T(8,128)(2,1)S(1)}, u32[]{:S(2)}, u32[]{:S(2)}) collective-permute-start(bf16[1,272,128]{2,1,0:T(8,128)(2,1)} %pack.1.own_ref), channel_id=1, source_target_pairs={{0,64},{4,68},{8,72},{12,76},{16,80},{20,84},{24,88},{28,92},{32,9... | collective-permute-start | bytes 208904 | tf_op jit(solution)/shard_map/ppermute | solution.py:159
  7.1 0.9 %copy-start = (bf16[1,272,128]{2,1,0:T(8,128)(2,1)S(1)}, bf16[1,272,128]{2,1,0:T(8,128)(2,1)}, u32[]{:S(2)}) copy-start(bf16[1,272,128]{2,1,0:T(8,128)(2,1)} %pack.1.own_ref) | copy-start | bytes 208900
  8.0 0.9 %copy-start.2 = (bf16[128,1024]{1,0:T(8,128)(2,1)S(1)}, bf16[128,1024]{1,0:T(8,128)(2,1)}, u32[]{:S(2)}) copy-start(bf16[128,1024]{1,0:T(8,128)(2,1)} %q_ref.1) | copy-start | bytes 786436
  8.9 16.3 %copy-start.1 = (bf16[1,272,128]{2,1,0:T(8,128)(2,1)S(1)}, bf16[1,272,128]{2,1,0:T(8,128)(2,1)}, u32[]{:S(2)}) copy-start(bf16[1,272,128]{2,1,0:T(8,128)(2,1)} %pack.1.own_ref) | copy-start | bytes 208900
  13.0 7.2 %collective-permute-start.2 = (bf16[2,272,128]{2,1,0:T(8,128)(2,1)S(1)}, bf16[2,272,128]{2,1,0:T(8,128)(2,1)S(1)}, u32[]{:S(2)}, u32[]{:S(2)}) collective-permute-start(bf16[2,272,128]{2,1,0:T(8,128)(2,1)S(1)} %pad_maximum_fusion.6), channel_id=1, source_target_pairs={{0,64},{4,68},{8,72},{12,76},{16,80},{20,84},{24,88},{28,92},{32,9... | collective-permute-start | bytes 417800 | tf_op jit(solution)/shard_map/ppermute | solution.py:159
  13.1 7.1 %collective-permute-start.3 = (bf16[2,272,128]{2,1,0:T(8,128)(2,1)S(1)}, bf16[2,272,128]{2,1,0:T(8,128)(2,1)S(1)}, u32[]{:S(2)}, u32[]{:S(2)}) collective-permute-start(bf16[2,272,128]{2,1,0:T(8,128)(2,1)S(1)} %get-tuple-element.42.rest_0_), channel_id=1, source_target_pairs={{0,8},{4,12},{8,16},{12,20},{16,24},{20,28},{24,0},{28,4},{32,40},... | collective-permute-start | bytes 417800 | tf_op jit(solution)/shard_map/ppermute | solution.py:159
  14.4 5.8 %collective-permute-start.4 = (bf16[2,272,128]{2,1,0:T(8,128)(2,1)S(1)}, bf16[2,272,128]{2,1,0:T(8,128)(2,1)S(1)}, u32[]{:S(2)}, u32[]{:S(2)}) collective-permute-start(bf16[2,272,128]{2,1,0:T(8,128)(2,1)S(1)} %get-tuple-element.42.rest_0_), channel_id=1, source_target_pairs={{0,24},{4,28},{8,0},{12,4},{16,8},{20,12},{24,16},{28,20},{32,56},... | collective-permute-start | bytes 417800 | tf_op jit(solution)/shard_map/ppermute | solution.py:159
  15.9 6.8 %collective-permute-start.5 = (bf16[2,272,128]{2,1,0:T(8,128)(2,1)S(1)}, bf16[2,272,128]{2,1,0:T(8,128)(2,1)S(1)}, u32[]{:S(2)}, u32[]{:S(2)}) collective-permute-start(bf16[2,272,128]{2,1,0:T(8,128)(2,1)S(1)} %get-tuple-element.42.rest_0_), channel_id=1, source_target_pairs={{0,16},{4,20},{8,24},{12,28},{16,0},{20,4},{24,8},{28,12},{32,48},... | collective-permute-start | bytes 417800 | tf_op jit(solution)/shard_map/ppermute | solution.py:159
  22.7 8.5 %collective-permute-start.10 = (bf16[4,2,272,128]{3,2,1,0:T(8,128)(2,1)S(1)}, bf16[4,2,272,128]{3,2,1,0:T(8,128)(2,1)S(1)}, u32[]{:S(2)}, u32[]{:S(2)}) collective-permute-start(bf16[4,2,272,128]{3,2,1,0:T(8,128)(2,1)S(1)} %pad_maximum_fusion), channel_id=1, source_target_pairs={{0,4},{4,0},{8,12},{12,8},{16,20},{20,16},{24,28},{28,24},{32,36},... | collective-permute-start | bytes 1671176 | tf_op jit(solution)/shard_map/ppermute | solution.py:159
  25.3 8.0 %collective-permute-start.6 = (bf16[2,272,128]{2,1,0:T(8,128)(2,1)S(1)}, bf16[2,272,128]{2,1,0:T(8,128)(2,1)S(1)}, u32[]{:S(2)}, u32[]{:S(2)}) collective-permute-start(bf16[2,272,128]{2,1,0:T(8,128)(2,1)S(1)} %get-tuple-element.70), channel_id=1, source_target_pairs={{0,8},{4,12},{8,16},{12,20},{16,24},{20,28},{24,0},{28,4},{32,40},... | collective-permute-start | bytes 417800 | tf_op jit(solution)/shard_map/ppermute | solution.py:159
  25.9 7.5 %collective-permute-start.7 = (bf16[2,272,128]{2,1,0:T(8,128)(2,1)S(1)}, bf16[2,272,128]{2,1,0:T(8,128)(2,1)S(1)}, u32[]{:S(2)}, u32[]{:S(2)}) collective-permute-start(bf16[2,272,128]{2,1,0:T(8,128)(2,1)S(1)} %get-tuple-element.68), channel_id=1, source_target_pairs={{0,24},{4,28},{8,0},{12,4},{16,8},{20,12},{24,16},{28,20},{32,56},... | collective-permute-start | bytes 417800 | tf_op jit(solution)/shard_map/ppermute | solution.py:159
  28.0 6.7 %collective-permute-start.8 = (bf16[2,272,128]{2,1,0:T(8,128)(2,1)S(1)}, bf16[2,272,128]{2,1,0:T(8,128)(2,1)S(1)}, u32[]{:S(2)}, u32[]{:S(2)}) collective-permute-start(bf16[2,272,128]{2,1,0:T(8,128)(2,1)S(1)} %get-tuple-element.69), channel_id=1, source_target_pairs={{0,16},{4,20},{8,24},{12,28},{16,0},{20,4},{24,8},{28,12},{32,48},... | collective-permute-start | bytes 417800 | tf_op jit(solution)/shard_map/ppermute | solution.py:159
  28.9 4.4 %collective-permute-start.9 = (bf16[1,272,128]{2,1,0:T(8,128)(2,1)S(1)}, bf16[1,272,128]{2,1,0:T(8,128)(2,1)S(1)}, u32[]{:S(2)}, u32[]{:S(2)}) collective-permute-start(bf16[1,272,128]{2,1,0:T(8,128)(2,1)S(1)} %get-tuple-element.65), channel_id=1, source_target_pairs={{128,132},{132,136},{136,140},{140,144},{144,148},{148,152},{152,1... | collective-permute-start | bytes 208904 | tf_op jit(solution)/shard_map/ppermute | solution.py:159
  34.8 3.0 %collective-permute-start.11 = (bf16[4,2,272,128]{3,2,1,0:T(8,128)(2,1)S(1)}, bf16[4,2,272,128]{3,2,1,0:T(8,128)(2,1)S(1)}, u32[]{:S(2)}, u32[]{:S(2)}) collective-permute-start(bf16[4,2,272,128]{3,2,1,0:T(8,128)(2,1)S(1)} %pad_maximum_fusion.1), channel_id=1, source_target_pairs={{0,4},{4,0},{8,12},{12,8},{16,20},{20,16},{24,28},{28,24},{32,36},... | collective-permute-start | bytes 1671176 | tf_op jit(solution)/shard_map/ppermute | solution.py:159
  36.3 3.5 %slice-start = ((s8[8388608]{0:T(1024)(128)(4,1)}), s8[4194304]{0:T(1024)(128)(4,1)S(1)}, s32[]{:S(2)}) async-start(s8[8388608]{0:T(1024)(128)(4,1)} %bitcast.11), calls=%async_computation | async-start | bytes 8388608
  37.8 2.3 %slice-start.1 = ((s8[8388608]{0:T(1024)(128)(4,1)}), s8[4194304]{0:T(1024)(128)(4,1)S(1)}, s32[]{:S(2)}) async-start(s8[8388608]{0:T(1024)(128)(4,1)} %bitcast.11), calls=%async_computation.1 | async-start | bytes 8388608
  40.6 15.4 %collective-permute-start.12 = (bf16[128,1024]{1,0:T(8,128)(2,1)S(1)}, bf16[128,1024]{1,0:T(8,128)(2,1)S(1)}, u32[]{:S(2)}, u32[]{:S(2)}) collective-permute-start(bf16[128,1024]{1,0:T(8,128)(2,1)S(1)} %project_2.1), channel_id=1, source_target_pairs={{0,2},{1,3},{2,0},{3,1},{4,6},{5,7},{6,4},{7,5},{8,10},{9,11},{10,... | collective-permute-start | bytes 786440 | tf_op jit(solution)/shard_map/ppermute | solution.py:257
  44.4 11.5 %collective-permute-start.13 = (bf16[128,1024]{1,0:T(8,128)(2,1)S(1)}, bf16[128,1024]{1,0:T(8,128)(2,1)S(1)}, u32[]{:S(2)}, u32[]{:S(2)}) collective-permute-start(bf16[128,1024]{1,0:T(8,128)(2,1)S(1)} %get-tuple-element.59), channel_id=1, source_target_pairs={{0,1},{1,0},{2,3},{3,2},{4,5},{5,4},{6,7},{7,6},{8,9},{9,8},{10,11... | collective-permute-start | bytes 786440 | tf_op jit(solution)/shard_map/ppermute | solution.py:257
  44.9 11.2 %collective-permute-start.14 = (bf16[128,1024]{1,0:T(8,128)(2,1)S(1)}, bf16[128,1024]{1,0:T(8,128)(2,1)S(1)}, u32[]{:S(2)}, u32[]{:S(2)}) collective-permute-start(bf16[128,1024]{1,0:T(8,128)(2,1)S(1)} %get-tuple-element.60), channel_id=1, source_target_pairs={{0,3},{1,2},{2,1},{3,0},{4,7},{5,6},{6,5},{7,4},{8,11},{9,10},{10,... | collective-permute-start | bytes 786440 | tf_op jit(solution)/shard_map/ppermute | solution.py:257

commit v7 on v5

--- a/solution.py
+++ b/solution.py
@@ -208,8 +208,8 @@
         [jnp.where(onward & (z >= 1), p1, 0), jnp.where(onward & (z >= 2), p2, 0)], 0
     )
     p34 = send(p12_on, shift_z(size, 2))
-    p34, near_a[2], near_a[3], near_a[1], near_a[0] = lax.optimization_barrier(
-        (p34, near_a[2], near_a[3], near_a[1], near_a[0])
+    near_a[2], near_a[3], near_a[1], p34, near_a[0] = lax.optimization_barrier(
+        (near_a[2], near_a[3], near_a[1], p34, near_a[0])
     )
 
     def with_either(first):

time: 57.7 us -> 57.7 us (level)
  no operation moved by 1% of the time
where the time goes in v7:
time: 57.7 us; the launch traced here: 56.9 us
  starting transfers between devices  22 us (38%)
  waiting for transfers between devices  20.6 us (36%)
  Pallas kernels  10.8 us (19%)
  local copies, waits for them, and re-layouts  2.22 us (4%)
  other arithmetic  1.14 us (2%)
    ppermute x12, starting transfers between devices, send(): return lax.ppermute(value, 'ctx', pairs)  18 us
    ppermute x12, waiting for transfers between devices, send(): return lax.ppermute(value, 'ctx', pairs)  10.3 us
    ppermute x3, waiting for transfers between devices, pass_on(): return lax.ppermute(part, 'tp', [(i, i ^ k) for i in range(4)])  10.3 us
    pallas_call x3, Pallas kernels, attend(): pl.pallas_call(group_kernel, out_shape=state_shape, in_specs=[VMEM] * (4...  5.13 us
    ppermute x3, starting transfers between devices, pass_on(): return lax.ppermute(part, 'tp', [(i, i ^ k) for i in range(4)])  3.96 us
    unnamed x10, local copies, waits for them, and re-layouts  2.22 us
    pallas_call x1, Pallas kernels, on_device(): pl.pallas_call(last_kernel, out_shape=jax.ShapeDtypeStruct(queries.shape,...  1.97 us
    pallas_call x3, Pallas kernels, project(): pl.pallas_call(functools.partial(project_kernel, steps), out_shape=tuple(...  1.64 us
  transfers between devices with their start and end apart: 15, of which 8 were waited for; matrix products, arithmetic and copies ran while one was open for 0% of the time, Pallas kernels for 12%

profile of v7, /device:TPU:1, one launch (start us, length us, event | category | flops | bytes accessed | tf_op | source)
XLA Modules:
  0.0 56.9 jit_solution(13802294797421780060)
XLA Ops:
  0.0 1.5 %pack.1.own_ref = bf16[1,272,128]{2,1,0:T(8,128)(2,1)} custom-call(bf16[128,128]{1,0:T(8,128)(2,1)} %k_ref.1, bf16[128,128]{1,0:T(8,128)(2,1)} %v_ref.1, s32[1,128]{1,0:T(1,128)} %bitcast.20), custom_call_target="tpu_custom_call" | custom-call | tf_op jit(solution)/shard_map/pack/pallas_call | solution.py:161
  1.5 2.5 %collective-permute-start = (bf16[1,272,128]{2,1,0:T(8,128)(2,1)}, bf16[1,272,128]{2,1,0:T(8,128)(2,1)S(1)}, u32[]{:S(2)}, u32[]{:S(2)}) collective-permute-start(bf16[1,272,128]{2,1,0:T(8,128)(2,1)} %pack.1.own_ref), channel_id=1, source_target_pairs={{0,32},{4,36},{8,40},{12,44},{16,48},{20,52},{24,56},{28,60},{32,6... | collective-permute-start | bytes 208904 | tf_op jit(solution)/shard_map/ppermute | solution.py:159
  4.1 3.0 %collective-permute-start.1 = (bf16[1,272,128]{2,1,0:T(8,128)(2,1)}, bf16[1,272,128]{2,1,0:T(8,128)(2,1)S(1)}, u32[]{:S(2)}, u32[]{:S(2)}) collective-permute-start(bf16[1,272,128]{2,1,0:T(8,128)(2,1)} %pack.1.own_ref), channel_id=1, source_target_pairs={{0,64},{4,68},{8,72},{12,76},{16,80},{20,84},{24,88},{28,92},{32,9... | collective-permute-start | bytes 208904 | tf_op jit(solution)/shard_map/ppermute | solution.py:159
  7.1 0.9 %copy-done = bf16[1,272,128]{2,1,0:T(8,128)(2,1)S(1)} copy-done((bf16[1,272,128]{2,1,0:T(8,128)(2,1)S(1)}, bf16[1,272,128]{2,1,0:T(8,128)(2,1)}, u32[]{:S(2)}) %copy-start) | copy-done | bytes 69656
  8.0 0.9 %copy-done.2 = bf16[128,1024]{1,0:T(8,128)(2,1)S(1)} copy-done((bf16[128,1024]{1,0:T(8,128)(2,1)S(1)}, bf16[128,1024]{1,0:T(8,128)(2,1)}, u32[]{:S(2)}) %copy-start.2) | copy-done | bytes 262168
  8.9 0.5 own.1
  9.5 0.5 collective-permute-done
  9.9 3.0 %collective-permute-done.1 = bf16[1,272,128]{2,1,0:T(8,128)(2,1)S(1)} collective-permute-done((bf16[1,272,128]{2,1,0:T(8,128)(2,1)}, bf16[1,272,128]{2,1,0:T(8,128)(2,1)S(1)}, u32[]{:S(2)}, u32[]{:S(2)}) %collective-permute-start.1) | collective-permute-done | bytes 69664 | tf_op jit(solution)/shard_map/ppermute | solution.py:159
  13.1 1.3 %collective-permute-start.2 = (bf16[2,272,128]{2,1,0:T(8,128)(2,1)S(1)}, bf16[2,272,128]{2,1,0:T(8,128)(2,1)S(1)}, u32[]{:S(2)}, u32[]{:S(2)}) collective-permute-start(bf16[2,272,128]{2,1,0:T(8,128)(2,1)S(1)} %get-tuple-element.42.rest_0_), channel_id=1, source_target_pairs={{0,8},{4,12},{8,16},{12,20},{16,24},{20,28},{24,0},{28,4},{32,40},... | collective-permute-start | bytes 417800 | tf_op jit(solution)/shard_map/ppermute | solution.py:159
  14.4 1.5 %collective-permute-start.3 = (bf16[2,272,128]{2,1,0:T(8,128)(2,1)S(1)}, bf16[2,272,128]{2,1,0:T(8,128)(2,1)S(1)}, u32[]{:S(2)}, u32[]{:S(2)}) collective-permute-start(bf16[2,272,128]{2,1,0:T(8,128)(2,1)S(1)} %get-tuple-element.42.rest_0_), channel_id=1, source_target_pairs={{0,24},{4,28},{8,0},{12,4},{16,8},{20,12},{24,16},{28,20},{32,56},... | collective-permute-start | bytes 417800 | tf_op jit(solution)/shard_map/ppermute | solution.py:159
  15.9 1.5 %collective-permute-start.4 = (bf16[2,272,128]{2,1,0:T(8,128)(2,1)S(1)}, bf16[2,272,128]{2,1,0:T(8,128)(2,1)S(1)}, u32[]{:S(2)}, u32[]{:S(2)}) collective-permute-start(bf16[2,272,128]{2,1,0:T(8,128)(2,1)S(1)} %get-tuple-element.42.rest_0_), channel_id=1, source_target_pairs={{0,16},{4,20},{8,24},{12,28},{16,0},{20,4},{24,8},{28,12},{32,48},... | collective-permute-start | bytes 417800 | tf_op jit(solution)/shard_map/ppermute | solution.py:159
  17.4 2.8 %collective-permute-done.5.rest_1_ = bf16[2,272,128]{2,1,0:T(8,128)(2,1)S(1)} collective-permute-done((bf16[2,272,128]{2,1,0:T(8,128)(2,1)S(1)}, bf16[2,272,128]{2,1,0:T(8,128)(2,1)S(1)}, u32[]{:S(2)}, u32[]{:S(2)}) %collective-permute-start.5) | collective-permute-done | bytes 139296 | tf_op jit(solution)/shard_map/ppermute | solution.py:159
  20.2 2.4 %collective-permute-done.4.rest_1_ = bf16[2,272,128]{2,1,0:T(8,128)(2,1)S(1)} collective-permute-done((bf16[2,272,128]{2,1,0:T(8,128)(2,1)S(1)}, bf16[2,272,128]{2,1,0:T(8,128)(2,1)S(1)}, u32[]{:S(2)}, u32[]{:S(2)}) %collective-permute-start.4) | collective-permute-done | bytes 139296 | tf_op jit(solution)/shard_map/ppermute | solution.py:159
  22.7 2.5 %collective-permute-start.10 = (bf16[4,2,272,128]{3,2,1,0:T(8,128)(2,1)S(1)}, bf16[4,2,272,128]{3,2,1,0:T(8,128)(2,1)S(1)}, u32[]{:S(2)}, u32[]{:S(2)}) collective-permute-start(bf16[4,2,272,128]{3,2,1,0:T(8,128)(2,1)S(1)} %pad_maximum_fusion), channel_id=1, source_target_pairs={{0,4},{4,0},{8,12},{12,8},{16,20},{20,16},{24,28},{28,24},{32,36},... | collective-permute-start | bytes 1671176 | tf_op jit(solution)/shard_map/ppermute | solution.py:159
  25.3 0.6 %collective-permute-start.6 = (bf16[2,272,128]{2,1,0:T(8,128)(2,1)S(1)}, bf16[2,272,128]{2,1,0:T(8,128)(2,1)S(1)}, u32[]{:S(2)}, u32[]{:S(2)}) collective-permute-start(bf16[2,272,128]{2,1,0:T(8,128)(2,1)S(1)} %get-tuple-element.70), channel_id=1, source_target_pairs={{0,8},{4,12},{8,16},{12,20},{16,24},{20,28},{24,0},{28,4},{32,40},... | collective-permute-start | bytes 417800 | tf_op jit(solution)/shard_map/ppermute | solution.py:159
  25.9 2.2 %collective-permute-start.7 = (bf16[2,272,128]{2,1,0:T(8,128)(2,1)S(1)}, bf16[2,272,128]{2,1,0:T(8,128)(2,1)S(1)}, u32[]{:S(2)}, u32[]{:S(2)}) collective-permute-start(bf16[2,272,128]{2,1,0:T(8,128)(2,1)S(1)} %get-tuple-element.68), channel_id=1, source_target_pairs={{0,24},{4,28},{8,0},{12,4},{16,8},{20,12},{24,16},{28,20},{32,56},... | collective-permute-start | bytes 417800 | tf_op jit(solution)/shard_map/ppermute | solution.py:159
  28.0 0.8 %collective-permute-start.8 = (bf16[2,272,128]{2,1,0:T(8,128)(2,1)S(1)}, bf16[2,272,128]{2,1,0:T(8,128)(2,1)S(1)}, u32[]{:S(2)}, u32[]{:S(2)}) collective-permute-start(bf16[2,272,128]{2,1,0:T(8,128)(2,1)S(1)} %get-tuple-element.69), channel_id=1, source_target_pairs={{0,16},{4,20},{8,24},{12,28},{16,0},{20,4},{24,8},{28,12},{32,48},... | collective-permute-start | bytes 417800 | tf_op jit(solution)/shard_map/ppermute | solution.py:159
  28.9 0.7 %collective-permute-start.9 = (bf16[1,272,128]{2,1,0:T(8,128)(2,1)S(1)}, bf16[1,272,128]{2,1,0:T(8,128)(2,1)S(1)}, u32[]{:S(2)}, u32[]{:S(2)}) collective-permute-start(bf16[1,272,128]{2,1,0:T(8,128)(2,1)S(1)} %get-tuple-element.65), channel_id=1, source_target_pairs={{128,132},{132,136},{136,140},{140,144},{144,148},{148,152},{152,1... | collective-permute-start | bytes 208904 | tf_op jit(solution)/shard_map/ppermute | solution.py:159
  29.5 1.7 %near_a.1 = (f32[8,1024]{1,0:T(8,128)S(1)}, f32[144,1024]{1,0:T(8,128)S(1)}) custom-call(bf16[1024,128]{1,0:T(8,128)(2,1)S(1)} %get-tuple-element.36.q_ref, bf16[1,272,128]{2,1,0:T(8,128)(2,1)S(1)} %copy-done.1, f32[8,1024]{1,0:T(8,128)S(1)} %get-tuple-element.40.m_in, f32[144,1024]{1,0:T(8,128)S(1)} %get-tuple-element.41.acc_in, ...), custom_call_target="tpu_custom_call" | custom-call | flops 17179869184 | bytes 524288 | tf_op jit(solution)/shard_map/near_a/pallas_call | solution.py:181
  31.2 2.1 %far_a.1 = (f32[8,1024]{1,0:T(8,128)S(1)}, f32[144,1024]{1,0:T(8,128)S(1)}) custom-call(bf16[1024,128]{1,0:T(8,128)(2,1)S(1)} %get-tuple-element.36.q_ref, bf16[1,272,128]{2,1,0:T(8,128)(2,1)S(1)} %copy-done.1, f32[8,1024]{1,0:T(8,128)S(1)} %get-tuple-element.46.m_in, f32[144,1024]{1,0:T(8,128)S(1)} %get-tuple-element.47.acc_in, ...), custom_call_target="tpu_custom_call" | custom-call | flops 21474836480 | bytes 655360 | tf_op jit(solution)/shard_map/far_a/pallas_call | solution.py:181
  33.3 1.4 %collective-permute-done.8.rest_0_ = bf16[2,272,128]{2,1,0:T(8,128)(2,1)S(1)} collective-permute-done((bf16[2,272,128]{2,1,0:T(8,128)(2,1)S(1)}, bf16[2,272,128]{2,1,0:T(8,128)(2,1)S(1)}, u32[]{:S(2)}, u32[]{:S(2)}) %collective-permute-start.8) | collective-permute-done | bytes 139296 | tf_op jit(solution)/shard_map/ppermute | solution.py:159
  34.8 1.4 %collective-permute-start.11 = (bf16[4,2,272,128]{3,2,1,0:T(8,128)(2,1)S(1)}, bf16[4,2,272,128]{3,2,1,0:T(8,128)(2,1)S(1)}, u32[]{:S(2)}, u32[]{:S(2)}) collective-permute-start(bf16[4,2,272,128]{3,2,1,0:T(8,128)(2,1)S(1)} %pad_maximum_fusion.1), channel_id=1, source_target_pairs={{0,4},{4,0},{8,12},{12,8},{16,20},{20,16},{24,28},{28,24},{32,36},... | collective-permute-start | bytes 1671176 | tf_op jit(solution)/shard_map/ppermute | solution.py:159
  36.3 1.4 %near_b.1 = (f32[8,1024]{1,0:T(8,128)S(1)}, f32[144,1024]{1,0:T(8,128)S(1)}) custom-call(bf16[1024,128]{1,0:T(8,128)(2,1)S(1)} %get-tuple-element.36.q_ref, bf16[1,272,128]{2,1,0:T(8,128)(2,1)S(1)} %copy-done.1, f32[8,1024]{1,0:T(8,128)S(1)} %get-tuple-element.50.m_in, f32[144,1024]{1,0:T(8,128)S(1)} %get-tuple-element.51.acc_in, ...), custom_call_target="tpu_custom_call" | custom-call | flops 12884901888 | bytes 393216 | tf_op jit(solution)/shard_map/near_b/pallas_call | solution.py:181
  37.8 2.0 %last.1.att_ref = bf16[128,1024]{1,0:T(8,128)(2,1)S(1)} custom-call(bf16[1024,128]{1,0:T(8,128)(2,1)S(1)} %get-tuple-element.36.q_ref, bf16[1,272,128]{2,1,0:T(8,128)(2,1)S(1)} %copy-done.1, f32[8,1024]{1,0:T(8,128)S(1)} %get-tuple-element.55.m_in, f32[144,1024]{1,0:T(8,128)S(1)} %get-tuple-element.56.acc_in, ...), custom_call_target="tpu_custom_call" | custom-call | flops 19327352832 | bytes 589824 | tf_op jit(solution)/shard_map/last/pallas_call | solution.py:229
  40.2 0.5 project_2.1
  40.6 3.0 %collective-permute-start.12 = (bf16[128,1024]{1,0:T(8,128)(2,1)S(1)}, bf16[128,1024]{1,0:T(8,128)(2,1)S(1)}, u32[]{:S(2)}, u32[]{:S(2)}) collective-permute-start(bf16[128,1024]{1,0:T(8,128)(2,1)S(1)} %project_2.1), channel_id=1, source_target_pairs={{0,2},{1,3},{2,0},{3,1},{4,6},{5,7},{6,4},{7,5},{8,10},{9,11},{10,... | collective-permute-start | bytes 786440 | tf_op jit(solution)/shard_map/ppermute | solution.py:257
  43.6 0.7 %project_1_3.1 = (bf16[128,1024]{1,0:T(8,128)(2,1)S(1)}, bf16[128,1024]{1,0:T(8,128)(2,1)S(1)}) custom-call(s32[1]{0:T(128)} %bitcast.lane_ref, bf16[128,1024]{1,0:T(8,128)(2,1)S(1)} %last.1.att_ref, bf16[1024,4096]{1,0:T(8,128)(2,1)S(1)} %bitcast.12), custom_call_target="tpu_custom_call" | custom-call | flops 34359738368 | bytes 4194304 | tf_op jit(solution)/shard_map/project_1_3/pallas_call | solution.py:242
  44.4 0.5 collective-permute-start.13
  44.9 0.5 collective-permute-start.14
  45.3 0.5 project_own.1
  45.8 10.0 %collective-permute-done.13 = bf16[128,1024]{1,0:T(8,128)(2,1)S(1)} collective-permute-done((bf16[128,1024]{1,0:T(8,128)(2,1)S(1)}, bf16[128,1024]{1,0:T(8,128)(2,1)S(1)}, u32[]{:S(2)}, u32[]{:S(2)}) %collective-permute-start.13) | collective-permute-done | bytes 262176 | tf_op jit(solution)/shard_map/ppermute | solution.py:257
  56.1 0.8 %add_convert_fusion = bf16[128,1024]{1,0:T(8,128)(2,1)} fusion(bf16[128,1024]{1,0:T(8,128)(2,1)S(1)} %collective-permute-done.14, bf16[128,1024]{1,0:T(8,128)(2,1)S(1)} %collective-permute-done.13, f32[128,1024]{1,0:T(8,128)S(1)} %project_own.1, bf16[128,1024]{1,0:T(8,128)(2,1)S(1)} %collective-permute-done.12), kind=kLoop, calls=%fused_computation.2 | loop fusion | flops 917504 | bytes 1572864 | tf_op jit(solution)/shard_map/convert_element_type | solution.py:266
  (26 shorter events, 1.2 us)
Async XLA Ops:
  1.5 8.4 %collective-permute-start = (bf16[1,272,128]{2,1,0:T(8,128)(2,1)}, bf16[1,272,128]{2,1,0:T(8,128)(2,1)S(1)}, u32[]{:S(2)}, u32[]{:S(2)}) collective-permute-start(bf16[1,272,128]{2,1,0:T(8,128)(2,1)} %pack.1.own_ref), channel_id=1, source_target_pairs={{0,32},{4,36},{8,40},{12,44},{16,48},{20,52},{24,56},{28,60},{32,6... | collective-permute-start | bytes 208904 | tf_op jit(solution)/shard_map/ppermute | solution.py:159
  4.1 8.9 %collective-permute-start.1 = (bf16[1,272,128]{2,1,0:T(8,128)(2,1)}, bf16[1,272,128]{2,1,0:T(8,128)(2,1)S(1)}, u32[]{:S(2)}, u32[]{:S(2)}) collective-permute-start(bf16[1,272,128]{2,1,0:T(8,128)(2,1)} %pack.1.own_ref), channel_id=1, source_target_pairs={{0,64},{4,68},{8,72},{12,76},{16,80},{20,84},{24,88},{28,92},{32,9... | collective-permute-start | bytes 208904 | tf_op jit(solution)/shard_map/ppermute | solution.py:159
  7.1 0.9 %copy-start = (bf16[1,272,128]{2,1,0:T(8,128)(2,1)S(1)}, bf16[1,272,128]{2,1,0:T(8,128)(2,1)}, u32[]{:S(2)}) copy-start(bf16[1,272,128]{2,1,0:T(8,128)(2,1)} %pack.1.own_ref) | copy-start | bytes 208900
  8.0 0.9 %copy-start.2 = (bf16[128,1024]{1,0:T(8,128)(2,1)S(1)}, bf16[128,1024]{1,0:T(8,128)(2,1)}, u32[]{:S(2)}) copy-start(bf16[128,1024]{1,0:T(8,128)(2,1)} %q_ref.1) | copy-start | bytes 786436
  8.9 16.3 %copy-start.1 = (bf16[1,272,128]{2,1,0:T(8,128)(2,1)S(1)}, bf16[1,272,128]{2,1,0:T(8,128)(2,1)}, u32[]{:S(2)}) copy-start(bf16[1,272,128]{2,1,0:T(8,128)(2,1)} %pack.1.own_ref) | copy-start | bytes 208900
  13.0 7.2 %collective-permute-start.5 = (bf16[2,272,128]{2,1,0:T(8,128)(2,1)S(1)}, bf16[2,272,128]{2,1,0:T(8,128)(2,1)S(1)}, u32[]{:S(2)}, u32[]{:S(2)}) collective-permute-start(bf16[2,272,128]{2,1,0:T(8,128)(2,1)S(1)} %pad_maximum_fusion.6), channel_id=1, source_target_pairs={{0,64},{4,68},{8,72},{12,76},{16,80},{20,84},{24,88},{28,92},{32,9... | collective-permute-start | bytes 417800 | tf_op jit(solution)/shard_map/ppermute | solution.py:159
  13.1 7.1 %collective-permute-start.2 = (bf16[2,272,128]{2,1,0:T(8,128)(2,1)S(1)}, bf16[2,272,128]{2,1,0:T(8,128)(2,1)S(1)}, u32[]{:S(2)}, u32[]{:S(2)}) collective-permute-start(bf16[2,272,128]{2,1,0:T(8,128)(2,1)S(1)} %get-tuple-element.42.rest_0_), channel_id=1, source_target_pairs={{0,8},{4,12},{8,16},{12,20},{16,24},{20,28},{24,0},{28,4},{32,40},... | collective-permute-start | bytes 417800 | tf_op jit(solution)/shard_map/ppermute | solution.py:159
  14.4 5.8 %collective-permute-start.3 = (bf16[2,272,128]{2,1,0:T(8,128)(2,1)S(1)}, bf16[2,272,128]{2,1,0:T(8,128)(2,1)S(1)}, u32[]{:S(2)}, u32[]{:S(2)}) collective-permute-start(bf16[2,272,128]{2,1,0:T(8,128)(2,1)S(1)} %get-tuple-element.42.rest_0_), channel_id=1, source_target_pairs={{0,24},{4,28},{8,0},{12,4},{16,8},{20,12},{24,16},{28,20},{32,56},... | collective-permute-start | bytes 417800 | tf_op jit(solution)/shard_map/ppermute | solution.py:159
  15.9 6.8 %collective-permute-start.4 = (bf16[2,272,128]{2,1,0:T(8,128)(2,1)S(1)}, bf16[2,272,128]{2,1,0:T(8,128)(2,1)S(1)}, u32[]{:S(2)}, u32[]{:S(2)}) collective-permute-start(bf16[2,272,128]{2,1,0:T(8,128)(2,1)S(1)} %get-tuple-element.42.rest_0_), channel_id=1, source_target_pairs={{0,16},{4,20},{8,24},{12,28},{16,0},{20,4},{24,8},{28,12},{32,48},... | collective-permute-start | bytes 417800 | tf_op jit(solution)/shard_map/ppermute | solution.py:159
  22.7 8.5 %collective-permute-start.10 = (bf16[4,2,272,128]{3,2,1,0:T(8,128)(2,1)S(1)}, bf16[4,2,272,128]{3,2,1,0:T(8,128)(2,1)S(1)}, u32[]{:S(2)}, u32[]{:S(2)}) collective-permute-start(bf16[4,2,272,128]{3,2,1,0:T(8,128)(2,1)S(1)} %pad_maximum_fusion), channel_id=1, source_target_pairs={{0,4},{4,0},{8,12},{12,8},{16,20},{20,16},{24,28},{28,24},{32,36},... | collective-permute-start | bytes 1671176 | tf_op jit(solution)/shard_map/ppermute | solution.py:159
  25.3 8.0 %collective-permute-start.6 = (bf16[2,272,128]{2,1,0:T(8,128)(2,1)S(1)}, bf16[2,272,128]{2,1,0:T(8,128)(2,1)S(1)}, u32[]{:S(2)}, u32[]{:S(2)}) collective-permute-start(bf16[2,272,128]{2,1,0:T(8,128)(2,1)S(1)} %get-tuple-element.70), channel_id=1, source_target_pairs={{0,8},{4,12},{8,16},{12,20},{16,24},{20,28},{24,0},{28,4},{32,40},... | collective-permute-start | bytes 417800 | tf_op jit(solution)/shard_map/ppermute | solution.py:159
  25.9 7.5 %collective-permute-start.7 = (bf16[2,272,128]{2,1,0:T(8,128)(2,1)S(1)}, bf16[2,272,128]{2,1,0:T(8,128)(2,1)S(1)}, u32[]{:S(2)}, u32[]{:S(2)}) collective-permute-start(bf16[2,272,128]{2,1,0:T(8,128)(2,1)S(1)} %get-tuple-element.68), channel_id=1, source_target_pairs={{0,24},{4,28},{8,0},{12,4},{16,8},{20,12},{24,16},{28,20},{32,56},... | collective-permute-start | bytes 417800 | tf_op jit(solution)/shard_map/ppermute | solution.py:159
  28.0 6.7 %collective-permute-start.8 = (bf16[2,272,128]{2,1,0:T(8,128)(2,1)S(1)}, bf16[2,272,128]{2,1,0:T(8,128)(2,1)S(1)}, u32[]{:S(2)}, u32[]{:S(2)}) collective-permute-start(bf16[2,272,128]{2,1,0:T(8,128)(2,1)S(1)} %get-tuple-element.69), channel_id=1, source_target_pairs={{0,16},{4,20},{8,24},{12,28},{16,0},{20,4},{24,8},{28,12},{32,48},... | collective-permute-start | bytes 417800 | tf_op jit(solution)/shard_map/ppermute | solution.py:159
  28.9 4.5 %collective-permute-start.9 = (bf16[1,272,128]{2,1,0:T(8,128)(2,1)S(1)}, bf16[1,272,128]{2,1,0:T(8,128)(2,1)S(1)}, u32[]{:S(2)}, u32[]{:S(2)}) collective-permute-start(bf16[1,272,128]{2,1,0:T(8,128)(2,1)S(1)} %get-tuple-element.65), channel_id=1, source_target_pairs={{128,132},{132,136},{136,140},{140,144},{144,148},{148,152},{152,1... | collective-permute-start | bytes 208904 | tf_op jit(solution)/shard_map/ppermute | solution.py:159
  34.8 3.0 %collective-permute-start.11 = (bf16[4,2,272,128]{3,2,1,0:T(8,128)(2,1)S(1)}, bf16[4,2,272,128]{3,2,1,0:T(8,128)(2,1)S(1)}, u32[]{:S(2)}, u32[]{:S(2)}) collective-permute-start(bf16[4,2,272,128]{3,2,1,0:T(8,128)(2,1)S(1)} %pad_maximum_fusion.1), channel_id=1, source_target_pairs={{0,4},{4,0},{8,12},{12,8},{16,20},{20,16},{24,28},{28,24},{32,36},... | collective-permute-start | bytes 1671176 | tf_op jit(solution)/shard_map/ppermute | solution.py:159
  36.3 3.6 %slice-start = ((s8[8388608]{0:T(1024)(128)(4,1)}), s8[4194304]{0:T(1024)(128)(4,1)S(1)}, s32[]{:S(2)}) async-start(s8[8388608]{0:T(1024)(128)(4,1)} %bitcast.11), calls=%async_computation | async-start | bytes 8388608
  37.8 2.3 %slice-start.1 = ((s8[8388608]{0:T(1024)(128)(4,1)}), s8[4194304]{0:T(1024)(128)(4,1)S(1)}, s32[]{:S(2)}) async-start(s8[8388608]{0:T(1024)(128)(4,1)} %bitcast.11), calls=%async_computation.1 | async-start | bytes 8388608
  40.6 15.4 %collective-permute-start.12 = (bf16[128,1024]{1,0:T(8,128)(2,1)S(1)}, bf16[128,1024]{1,0:T(8,128)(2,1)S(1)}, u32[]{:S(2)}, u32[]{:S(2)}) collective-permute-start(bf16[128,1024]{1,0:T(8,128)(2,1)S(1)} %project_2.1), channel_id=1, source_target_pairs={{0,2},{1,3},{2,0},{3,1},{4,6},{5,7},{6,4},{7,5},{8,10},{9,11},{10,... | collective-permute-start | bytes 786440 | tf_op jit(solution)/shard_map/ppermute | solution.py:257
  44.4 11.5 %collective-permute-start.13 = (bf16[128,1024]{1,0:T(8,128)(2,1)S(1)}, bf16[128,1024]{1,0:T(8,128)(2,1)S(1)}, u32[]{:S(2)}, u32[]{:S(2)}) collective-permute-start(bf16[128,1024]{1,0:T(8,128)(2,1)S(1)} %get-tuple-element.59), channel_id=1, source_target_pairs={{0,1},{1,0},{2,3},{3,2},{4,5},{5,4},{6,7},{7,6},{8,9},{9,8},{10,11... | collective-permute-start | bytes 786440 | tf_op jit(solution)/shard_map/ppermute | solution.py:257
  44.9 11.2 %collective-permute-start.14 = (bf16[128,1024]{1,0:T(8,128)(2,1)S(1)}, bf16[128,1024]{1,0:T(8,128)(2,1)S(1)}, u32[]{:S(2)}, u32[]{:S(2)}) collective-permute-start(bf16[128,1024]{1,0:T(8,128)(2,1)S(1)} %get-tuple-element.60), channel_id=1, source_target_pairs={{0,3},{1,2},{2,1},{3,0},{4,7},{5,6},{6,5},{7,4},{8,11},{9,10},{10,... | collective-permute-start | bytes 786440 | tf_op jit(solution)/shard_map/ppermute | solution.py:257
